TPU v7x, 256 devices: a whole 4x4x8 slice. The times are simulated.
256 devices in a mesh: row: 32 (over x, z_lo, core), col: 8 (over z_hi, y).
Axes of the slice: x: 4, y: 4, z: 8 (z_hi: 2, z_lo: 4; z = z_hi * 4 + z_lo), core: 2. Of those that a mesh axis runs over, the one named last changes fastest.
Arguments:
- features: bfloat16 [32768, 128], P(('col', 'row')), may hold values from -6 to 6
- block_values: bfloat16 [36864, 128, 128], P(('row', 'col')), may hold values from -0.25 to 0.25
- block_slots: int32 [36864], P(('row', 'col')), may hold values from 0 to 255, as said below
- block_counts: int32 [256], P(('row', 'col')), may hold values from 48 to 144, as said below
- w_in: bfloat16 [128, 256], replicated, may hold values from -0.5 to 0.5
- w_out: bfloat16 [256, 172], replicated, may hold values from -0.375 to 0.375
- logit_grad: bfloat16 [32768, 172], P(('col', 'row')), may hold values from -0.032958984 to 0.032958984
Outputs:
- logits: bfloat16 [32768, 172], P(('col', 'row'))
- w_in_grad: float32 [128, 256], replicated
- w_out_grad: float32 [256, 172], replicated
Inputs may be any that keep to these rules, and one draw needn't show every extreme that they name: `block_slots`: within each tile's 144 entries the slots are distinct; slot s is block row s // 8 and block column s % 8 of the tile. The first block_counts[t] blocks of tile t are live, the others are padding; some tile is full.
All inputs are finite; a program needn't handle non-finite values.
Results may differ from a plain program's by a relative error of at most 0.0071.
Values may be sent and summed in bfloat16 or wider, within the bound.
No kernel may reach another device: no remote copies, remote signals or barrier semaphores. Data moves between devices by JAX's collectives and lax.ppermute only.
A program may use at most 128 MiB of HBM per device.

v0:
```python
import jax
import jax.numpy as jnp
from jax import lax
from jax.sharding import PartitionSpec as P


def pick_blocks(rows_all, block_size, block_index):
    feature_width = rows_all.shape[1]
    return rows_all.reshape(-1, block_size, feature_width)[block_index]


def collect(products, block_index, segments):
    summed = jax.ops.segment_sum(products, block_index, num_segments=segments)
    return summed.reshape(segments * products.shape[1], products.shape[2])


def block_product(form, tile_blocks, picked):
    if picked.dtype == jnp.float32:
        return jnp.einsum(
            form,
            tile_blocks,
            picked,
            preferred_element_type=jnp.float32,
            precision=lax.Precision.HIGHEST,
        )
    return jnp.einsum(form, tile_blocks, picked, preferred_element_type=jnp.float32)


def forward_terms(tile_blocks, rows_all, dst_block, src_block, dst_count):
    picked = pick_blocks(rows_all, tile_blocks.shape[1], src_block)
    products = block_product("bij,bjf->bif", tile_blocks, picked)
    return collect(products, dst_block, dst_count)


def backward_terms(tile_blocks, rows_all, dst_block, src_block, src_count):
    picked = pick_blocks(rows_all, tile_blocks.shape[1], dst_block)
    products = block_product("bji,bjf->bif", tile_blocks, picked)
    return collect(products, src_block, src_count)


def on_device(features, block_values, block_slots, block_counts, w_in, w_out, logit_grad):
    local_rows = features.shape[0]
    block_size = block_values.shape[1]
    dst_count = lax.axis_size("row") * local_rows // block_size
    src_count = lax.axis_size("col") * local_rows // block_size
    alive_mask = (jnp.arange(block_values.shape[0]) < block_counts[0]).astype(jnp.bfloat16)
    tile_blocks = block_values * alive_mask[:, None, None]
    dst_block = block_slots // src_count
    src_block = block_slots % src_count
    input_all = lax.all_gather(features, "col", axis=0, tiled=True)
    input_terms = forward_terms(tile_blocks, input_all, dst_block, src_block, dst_count)
    aggregated = lax.psum_scatter(input_terms, "row", scatter_dimension=0, tiled=True).astype(
        jnp.bfloat16
    )
    pre_act = jnp.dot(aggregated, w_in, preferred_element_type=jnp.float32)
    hidden = jax.nn.silu(pre_act).astype(jnp.bfloat16)
    w_out_wide = w_out.astype(jnp.float32)
    tile_wide = tile_blocks.astype(jnp.float32)
    hidden_all = lax.all_gather(hidden, "col", axis=0, tiled=True)
    hidden_terms = forward_terms(tile_blocks, hidden_all, dst_block, src_block, dst_count)
    mixed_rows = lax.psum_scatter(hidden_terms, "row", scatter_dimension=0, tiled=True)
    logits = jnp.dot(mixed_rows, w_out_wide, precision=lax.Precision.HIGHEST).astype(jnp.bfloat16)
    output_grad = jnp.dot(
        mixed_rows.T, logit_grad.astype(jnp.float32), precision=lax.Precision.HIGHEST
    )
    back_rows = jnp.dot(logit_grad, w_out.T, preferred_element_type=jnp.float32)
    back_all = lax.all_gather(back_rows, "row", axis=0, tiled=True)
    back_terms = backward_terms(tile_wide, back_all, dst_block, src_block, src_count)
    spread = lax.psum_scatter(back_terms, "col", scatter_dimension=0, tiled=True)
    _, pullback = jax.vjp(jax.nn.silu, pre_act)
    pre_grad = pullback(spread)[0].astype(jnp.bfloat16)
    input_grad = jnp.dot(aggregated.T, pre_grad, preferred_element_type=jnp.float32)
    input_total, output_total = lax.psum((input_grad, output_grad), ("row", "col"))
    return (logits, input_total, output_total)


def solution(mesh):
    return jax.shard_map(
        on_device,
        mesh=mesh,
        in_specs=(
            P(("col", "row"), None),
            P(("row", "col"), None, None),
            P(("row", "col")),
            P(("row", "col")),
            P(),
            P(),
            P(("col", "row"), None),
        ),
        out_specs=(P(("col", "row"), None), P(), P()),
        check_vma=False,
    )
```

profile of v0, /device:TPU:32, one launch (start us, length us, event | category | flops | bytes accessed | tf_op | source)
XLA Modules:
  0.0 762.2 jit_solution(6608178093860096870)
XLA Ops:
  8.1 1.6 fusion.18
  11.1 46.1 %all_gather.9 = bf16[1024,128]{1,0:T(8,128)(2,1)S(1)} all-gather(bf16[128,128]{1,0:T(8,128)(2,1)} %param.7), channel_id=1, replica_groups=mesh['row'=32,'col'=8] {'col'}, dimensions={0}, use_global_device_ids=true | all-gather | bytes 294912 | tf_op jit(solution)/shard_map/all_gather | solution.py:50
  57.2 7.6 gather_fusion
  64.8 8.9 %fusion.4 = f32[144,128,128]{2,1,0:T(8,128)} fusion(bf16[144,128,128]{2,1,0:T(8,128)(2,1)} %gather_fusion, bf16[144,128,128]{2,1,0:T(8,128)(2,1)} %param.8, bf16[144]{0:T(256)(128)(2,1)S(1)} %compare_convert_fusion), kind=kOutput, calls=%fused_computation.10 | convolution fusion | flops 606339072 | bytes 18874656 | tf_op jit(solution)/shard_map/bij,bjf->bif/dot_general | solution.py:26
  74.0 19.1 %scatter_fusion = f32[32,128,128]{2,1,0:T(8,128)S(1)} fusion(f32[32,128,128]{2,1,0:T(8,128)S(1)} %broadcast_in_dim.26, s32[144]{0:T(256)S(1)} %get-tuple-element.10, f32[144,128,128]{2,1,0:T(8,128)} %fusion.4), kind=kCustom, calls=%fused_computation.3 | custom fusion | flops 2359296 | bytes 28312128 | tf_op jit(solution)/shard_map/scatter-add | solution.py:13
  93.1 1.3 copy-done.2
  94.7 12.8 %gather_fusion.2 = f32[144,128,256]{2,1,0:T(8,128)} fusion(f32[32,128,256]{2,1,0:T(8,128)} %bitcast.23, s32[1024]{0:T(1024)S(1)} %pad_clamp_fusion), kind=kCustom, calls=%fused_computation.2 | custom fusion | bytes 37749312 | tf_op jit(solution)/shard_map/gather | solution.py:9
  107.6 20.9 %fusion = f32[144,128,256]{2,1,0:T(8,128)} fusion(f32[144,128,256]{2,1,0:T(8,128)} %gather_fusion.2, bf16[144,128,128]{2,1,0:T(8,128)(2,1)} %param.8, bf16[144]{0:T(256)(128)(2,1)S(1)} %compare_convert_fusion), kind=kOutput, calls=%fused_computation.6 | convolution fusion | flops 7250116608 | bytes 42467616 | tf_op jit(solution)/shard_map/bji,bjf->bif/dot_general | solution.py:19
  128.5 27.2 %scatter_fusion.2 = f32[8,128,256]{2,1,0:T(8,128)S(1)} fusion(f32[8,128,256]{2,1,0:T(8,128)S(1)} %broadcast_in_dim.28, s32[144]{0:T(256)S(1)} %get-tuple-element.8, f32[144,128,256]{2,1,0:T(8,128)} %fusion), kind=kCustom, calls=%fused_computation.5 | custom fusion | flops 4718592 | bytes 56623680 | tf_op jit(solution)/shard_map/scatter-add | solution.py:13
  155.8 1.0 copy-done.1
  156.8 79.5 %reduce-scatter.4.cloned.1.call-done = f32[128,128]{1,0:T(8,128)} async-done(((f32[4096,128]{1,0:T(8,128)}), f32[128,128]{1,0:T(8,128)}) %reduce-scatter.4.cloned.1.call-update) | async-done | bytes 65552 | tf_op jit(solution)/shard_map/reduce_scatter | solution.py:52
  236.3 1.0 multiply_convert_fusion
  237.3 45.8 %all_gather.10 = bf16[1024,256]{1,0:T(8,128)(2,1)S(1)} all-gather(bf16[128,256]{1,0:T(8,128)(2,1)S(1)} %get-tuple-element.11), channel_id=1, replica_groups=mesh['row'=32,'col'=8] {'col'}, dimensions={0}, use_global_device_ids=true | all-gather | bytes 589824 | tf_op jit(solution)/shard_map/all_gather | solution.py:59
  283.1 7.2 gather_fusion.1
  290.4 14.3 %fusion.2 = f32[144,128,256]{2,1,0:T(8,128)} fusion(bf16[144,128,256]{2,1,0:T(8,128)(2,1)} %gather_fusion.1, bf16[144,128,128]{2,1,0:T(8,128)(2,1)} %param.8, bf16[144]{0:T(256)(128)(2,1)S(1)} %compare_convert_fusion), kind=kOutput, calls=%fused_computation.8 | convolution fusion | flops 1210318848 | bytes 33030432 | tf_op jit(solution)/shard_map/bij,bjf->bif/dot_general | solution.py:26
  304.7 2.5 broadcast_in_dim.24
  307.2 43.0 %scatter_fusion.1 = f32[32,128,256]{2,1,0:T(8,128)} fusion(f32[32,128,256]{2,1,0:T(8,128)} %broadcast_in_dim.24, s32[144]{0:T(256)S(1)} %get-tuple-element.10, f32[144,128,256]{2,1,0:T(8,128)} %fusion.2), kind=kCustom, calls=%fused_computation.4 | custom fusion | flops 4718592 | bytes 56623680 | tf_op jit(solution)/shard_map/scatter-add | solution.py:13
  350.3 1.8 fusion.12
  352.0 146.1 %reduce-scatter.6.cloned.1.call-done = f32[128,256]{1,0:T(8,128)} async-done(((f32[4096,256]{1,0:T(8,128)}), f32[128,256]{1,0:T(8,128)}) %reduce-scatter.6.cloned.1.call-update) | async-done | bytes 131088 | tf_op jit(solution)/shard_map/reduce_scatter | solution.py:61
  498.2 1.8 fusion.19
  500.0 1.8 convolution_convert_fusion
  501.8 250.7 %all-reduce.3.cloned.1.call-done = (f32[128,256]{1,0:T(8,128)}, f32[256,172]{0,1:T(8,128)}) async-done(((f32[128,256]{1,0:T(8,128)}, f32[256,172]{0,1:T(8,128)}), (f32[128,256]{1,0:T(8,128)}, f32[256,172]{0,1:T(8,128)})) %all-reduce.3.cloned.1.call-update) | async-done | bytes 307216 | tf_op jit(solution)/shard_map/psum | solution.py:73
  752.5 1.6 copy.18
  754.1 1.6 copy.19
  (28 shorter events, 2.4 us)
Async XLA Ops:
  7.2 0.9 copy-start
  7.2 87.5 %all-gather.2.cloned.1.call-start = ((), (), s32[]{:S(2)}) async-start(), calls=%async_computation.5 | async-start | bytes 4325376 | tf_op jit(solution)/shard_map/all_gather | solution.py:67
  9.7 226.6 %reduce-scatter.4.cloned.1.call-start = ((), (), s32[]{:S(2)}) async-start(), calls=%async_computation.3 | async-start | bytes 2162688 | tf_op jit(solution)/shard_map/reduce_scatter | solution.py:52
  93.1 1.3 copy-start.2
  94.4 255.8 %reduce-scatter.8.cloned.1.call-start = ((), (), s32[]{:S(2)}) async-start(), calls=%async_computation.6 | async-start | bytes 1179648 | tf_op jit(solution)/shard_map/reduce_scatter | solution.py:69
  128.5 107.8 %copy-start.4 = (bf16[128,256]{1,0:T(8,128)(2,1)S(1)}, bf16[128,256]{1,0:T(8,128)(2,1)}, u32[]{:S(2)}) copy-start(bf16[128,256]{1,0:T(8,128)(2,1)} %param.11) | copy-start | bytes 196612
  155.8 1.0 copy-start.1
  156.8 341.4 %reduce-scatter.6.cloned.1.call-start = ((), (), s32[]{:S(2)}) async-start(), calls=%async_computation.4 | async-start | bytes 4325376 | tf_op jit(solution)/shard_map/reduce_scatter | solution.py:61
  307.2 43.1 %copy-start.5 = (f32[128,128]{1,0:T(8,128)S(1)}, f32[128,128]{1,0:T(8,128)}, u32[]{:S(2)}) copy-start(f32[128,128]{1,0:T(8,128)} %reduce-scatter.4.cloned.1.call-done) | copy-start | bytes 196612
  350.2 148.0 %copy-start.3 = (bf16[128,172]{0,1:T(8,128)(2,1)S(1)}, bf16[128,172]{0,1:T(8,128)(2,1)}, u32[]{:S(2)}) copy-start(bf16[128,172]{0,1:T(8,128)(2,1)} %param.13) | copy-start | bytes 132100
  350.2 402.3 %all-reduce.3.cloned.1.call-start = ((), (), s32[]{:S(2)}) async-start(), calls=%async_computation.7 | async-start | bytes 622592 | tf_op jit(solution)/shard_map/psum | solution.py:73
Sparse Core Ops, SparseCore 0:
  10.4 65.6 all-gather.1
  94.6 141.6 reduce-scatter.3
  240.7 88.1 reduce-scatter.7
  350.3 147.7 reduce-scatter.5
  504.2 248.2 all-reduce.2
where the time goes:
time: 765 us; the launch traced here: 762 us
  waiting for transfers between devices  476 us (62%)
  blocking collectives  91.9 us (12%)
  other arithmetic  90 us (12%)
  matrix products  52.1 us (7%)
  local copies, waits for them, and re-layouts  36.8 us (5%)
  between operations  14.5 us (2%)
    psum x1, waiting for transfers between devices, on_device(): lax.psum((input_grad, output_grad), ('row', 'col'))  251 us
    reduce_scatter x1, waiting for transfers between devices, on_device(): lax.psum_scatter(hidden_terms, 'row', scatter_dimension=0, tiled=True)  146 us
    scatter-add x3, other arithmetic, collect(): summed = jax.ops.segment_sum(products, block_index, num_segments=segments)  89.3 us
    reduce_scatter x1, waiting for transfers between devices, on_device(): lax.psum_scatter(input_terms, 'row', scatter_dimension=0, tiled=True)  79.5 us
    all_gather x1, blocking collectives, on_device(): input_all = lax.all_gather(features, 'col', axis=0, tiled=True)  46.1 us
    all_gather x1, blocking collectives, on_device(): hidden_all = lax.all_gather(hidden, 'col', axis=0, tiled=True)  45.8 us
    gather x3, local copies, waits for them, and re-layouts, pick_blocks(): return rows_all.reshape(-1, block_size, feature_width)[block_index]  27.7 us
    dot_general x2, matrix products, block_product(): jnp.einsum(form, tile_blocks, picked, preferred_element_type=jnp.float32)  23.2 us
  transfers between devices with their start and end apart: 5, of which 3 were waited for; matrix products, arithmetic and copies ran while one was open for 22% of the time, Pallas kernels for 0%

commit v1 on v0

v1 whole, which is shorter than its diff:
```python
import functools

import jax
import jax.numpy as jnp
from jax import lax
from jax.experimental import pallas as pl
from jax.experimental.pallas import tpu as pltpu
from jax.sharding import PartitionSpec as P

F32 = jnp.float32
BF16 = jnp.bfloat16
BS = 128
CLSP = 176
UNIT = 16
UNITS = 10
SHARE = UNITS * UNIT
VMEM_LIMIT = 48 * 1024 * 1024
STEP = 512


def vmem():
    return pl.BlockSpec(memory_space=pltpu.VMEM)


def smem():
    return pl.BlockSpec(memory_space=pltpu.SMEM)


def dot(a, b, da, db):
    return lax.dot_general(a, b, (((da,), (db,)), ((), ())), preferred_element_type=F32)


def call(body, outs, args, specs=None, scratch=(), flops=0):
    return pl.pallas_call(
        body,
        out_shape=[o if len(o) == 1 else jax.ShapeDtypeStruct(*o) for o in outs],
        in_specs=specs or [vmem()] * len(args),
        out_specs=[vmem()] * len(outs),
        scratch_shapes=scratch,
        compiler_params=pltpu.CompilerParams(vmem_limit_bytes=VMEM_LIMIT),
        cost_estimate=pl.CostEstimate(flops=flops, bytes_accessed=2**20, transcendentals=0),
    )(*args)


def densify_body(me_ref, count_ref, slot_ref, block_ref, dense_ref):
    dense_ref[...] = jnp.zeros_like(dense_ref)
    me = me_ref[0]

    def place(b, carry):
        slot = slot_ref[b]
        rel = lax.bitwise_xor(slot // 8, me)
        at = (rel % 2) * 16 + rel // 2
        row = pl.multiple_of(at * BS, BS)
        col = pl.multiple_of((slot % 8) * BS, BS)
        dense_ref[pl.ds(row, BS), pl.ds(col, BS)] = block_ref[b]
        return carry

    lax.fori_loop(0, count_ref[0], place, 0)


def densify(me, counts, slots, blocks):
    return call(
        densify_body,
        [((4096, 1024), BF16)],
        (me, counts, slots, blocks),
        [smem(), smem(), smem(), vmem()],
    )[0]


def hbm():
    return pl.BlockSpec(memory_space=pl.ANY)


def stage(chunks):
    return [pltpu.VMEM((chunks, STEP, 1024), BF16), pltpu.SemaphoreType.DMA((chunks,))]


def copies(dense_ref, buffer_ref, sem_ref, first, chunks):
    return [
        pltpu.make_async_copy(
            dense_ref.at[pl.ds((first + i) * STEP, STEP)], buffer_ref.at[i], sem_ref.at[i]
        )
        for i in range(chunks)
    ]


def rows_product_body(half, dense_ref, right_ref, out_ref, buffer_ref, sem_ref):
    moves = copies(dense_ref, buffer_ref, sem_ref, 4 * half, 4)
    for move in moves:
        move.start()
    right = right_ref[...]
    for i, move in enumerate(moves):
        move.wait()
        out_ref[i * STEP : (i + 1) * STEP, :] = dot(buffer_ref[i], right, 1, 0).astype(out_ref.dtype)


def rows_product(dense, right, half, dtype):
    return call(
        functools.partial(rows_product_body, half),
        [((2048, BS), dtype)],
        (dense, right),
        [hbm(), vmem()],
        stage(4),
        flops=2 * 2048 * 1024 * 256,
    )[0]


def class_rows(wide, moves, buffer_ref, out_ref):
    for i, move in enumerate(moves):
        move.wait()
        part = dot(wide, buffer_ref[i], 1, 1).astype(out_ref.dtype)
        for j in range(4):
            at = (i * 4 + j) * CLSP
            out_ref[at : at + CLSP, :] = part[:, j * BS : (j + 1) * BS]


def silu_inputs(agg_ref, w_in_ref):
    pre = dot(agg_ref[...], w_in_ref[...], 1, 0)
    gate = 1.0 / (1.0 + jnp.exp(-pre))
    return pre, gate, (pre * gate).astype(BF16)


def add_grads(pre, gate, hid, agg, q, w_out, x, out_ref):
    high = q.astype(BF16)
    low = (q - high.astype(F32)).astype(BF16)
    spread = dot(high, w_out, 0, 0) + dot(low, w_out, 0, 0)
    pre_grad = (spread * (gate * (1.0 + pre * (1.0 - gate)))).astype(BF16)
    in_grad = dot(agg, pre_grad, 0, 0)
    out_grad = dot(high, hid, 1, 0) + dot(low, hid, 1, 0)
    pieces = []
    for array in (in_grad, out_grad):
        rows = array.shape[0]
        over = -rows % UNIT
        if over:
            array = jnp.concatenate([array, jnp.zeros((over, array.shape[1]), F32)])
        array = array.astype(BF16)
        for side in range(2):
            pieces.append(array[:, side * BS : (side + 1) * BS])
    used = sum(piece.shape[0] for piece in pieces)
    pieces.append(jnp.zeros((4 * SHARE - used, BS), BF16))
    flat = jnp.concatenate(pieces)
    for j in range(4):
        at = pl.multiple_of(16 * CLSP + lax.bitwise_xor(j, x) * SHARE, UNIT)
        out_ref[pl.ds(at, SHARE), :] = flat[j * SHARE : (j + 1) * SHARE, :]


def class_rows_far_body(
    agg_ref, w_in_ref, w_out_ref, q_ref, me_ref, dense_ref, wide_ref, out_ref, buffer_ref, sem_ref
):
    moves = copies(dense_ref, buffer_ref, sem_ref, 4, 4)
    for move in moves:
        move.start()
    pre, gate, hid = silu_inputs(agg_ref, w_in_ref)
    wide = dot(w_out_ref[...], hid, 1, 1)
    zeros = jnp.zeros((CLSP - wide.shape[0], wide.shape[1]), F32)
    wide_ref[...] = jnp.concatenate([wide, zeros]).astype(BF16)
    class_rows(wide_ref[...], moves, buffer_ref, out_ref)
    add_grads(pre, gate, hid, agg_ref[...], q_ref[...], w_out_ref[...], me_ref[0] // 8, out_ref)


def class_rows_far(agg, w_in, w_out_t, q, me, dense):
    return call(
        class_rows_far_body,
        [((CLSP, 1024), BF16), ((16 * CLSP + 4 * SHARE, BS), BF16)],
        (agg, w_in, w_out_t, q, me, dense),
        [vmem(), vmem(), vmem(), vmem(), smem(), hbm()],
        stage(4),
        flops=4 * 2048 * 1024 * 256,
    )


def class_rows_near_body(wide_ref, dense_ref, out_ref, buffer_ref, sem_ref):
    moves = copies(dense_ref, buffer_ref, sem_ref, 0, 4)
    for move in moves:
        move.start()
    class_rows(wide_ref[...], moves, buffer_ref, out_ref)


def class_rows_near(wide, dense):
    return call(
        class_rows_near_body,
        [((16 * CLSP, BS), F32)],
        (wide, dense),
        [vmem(), hbm()],
        stage(4),
        flops=2 * 2048 * 1024 * 256,
    )[0]


def class_columns_body(near_ref, far_ref, dense_ref, out_ref, buffer_ref, sem_ref):
    moves = copies(dense_ref, buffer_ref, sem_ref, 0, 8)
    for move in moves:
        move.start()
    for i, move in enumerate(moves):
        ref = near_ref if i < 4 else far_ref
        left = jnp.concatenate([ref[(i % 4) * 4 + j] for j in range(4)], axis=1)
        move.wait()
        part = dot(left, buffer_ref[i], 1, 0)
        if i == 0:
            out_ref[...] = part
        else:
            out_ref[...] += part


def class_columns(near, far, dense):
    return call(
        class_columns_body,
        [((near.shape[1], 1024), F32)],
        (near, far, dense),
        [vmem(), vmem(), hbm()],
        stage(8),
        flops=2 * 4096 * 1024 * 256,
    )[0]


def copies_body(features_ref, send_ref):
    for c in range(8):
        send_ref[c] = features_ref[...]


def eight_copies(features):
    return call(copies_body, [((8, BS, BS), BF16)], (features,))[0]


def core_sum_body(mine_ref, got_ref, s1_ref, s2_ref, s3_ref, keep_ref):
    n = keep_ref.shape[0]
    for d, ref in ((1, s1_ref), (2, s2_ref), (3, s3_ref), (0, keep_ref)):
        at = slice(d * n, (d + 1) * n)
        ref[...] = (mine_ref[at, :].astype(F32) + got_ref[at, :].astype(F32)).astype(ref.dtype)


def core_sum(mine, got):
    rows = mine.shape[0] // 4
    shape = (rows, BS)
    return call(core_sum_body, [(shape, BF16)] * 3 + [(shape, F32)], (mine, got))


def four(a, b, c, d):
    return (a.astype(F32) + b.astype(F32)) + (c.astype(F32) + d.astype(F32))


def x_sum_body(keep_ref, r1_ref, r2_ref, r3_ref, s1_ref, s2_ref, s3_ref, out_ref):
    n = out_ref.shape[0]
    for d, ref in ((1, s1_ref), (2, s2_ref), (3, s3_ref), (0, out_ref)):
        at = slice(d * n, (d + 1) * n)
        total = four(keep_ref[at, :], r1_ref[at, :], r2_ref[at, :], r3_ref[at, :])
        ref[...] = total.astype(ref.dtype)


def x_sum(keep, received):
    shape = (keep.shape[0] // 4, BS)
    return call(x_sum_body, [(shape, BF16)] * 3 + [(shape, F32)], (keep, *received))


def core_sum_grad_body(mine_ref, far_ref, got_ref, s1_ref, s2_ref, s3_ref, keep_ref):
    n = 4 * CLSP
    for d, ref in ((1, s1_ref), (2, s2_ref), (3, s3_ref), (0, keep_ref)):
        at = slice(d * n, (d + 1) * n)
        ref[:n, :] = (mine_ref[at, :].astype(F32) + got_ref[at, :].astype(F32)).astype(ref.dtype)
        at = slice(4 * n + d * SHARE, 4 * n + (d + 1) * SHARE)
        ref[n:, :] = (far_ref[at, :].astype(F32) + got_ref[at, :].astype(F32)).astype(ref.dtype)


def core_sum_grad(mine, far, got):
    shape = (4 * CLSP + SHARE, BS)
    return call(core_sum_grad_body, [(shape, BF16)] * 3 + [(shape, F32)], (mine, far, got))


def x_sum_grad_body(keep_ref, r1_ref, r2_ref, r3_ref, s1_ref, s2_ref, s3_ref, out_ref):
    n = CLSP
    tail = slice(4 * n, 4 * n + SHARE)
    share = four(keep_ref[tail, :], r1_ref[tail, :], r2_ref[tail, :], r3_ref[tail, :])
    for d, ref in ((1, s1_ref), (2, s2_ref), (3, s3_ref), (0, out_ref)):
        at = slice(d * n, (d + 1) * n)
        total = four(keep_ref[at, :], r1_ref[at, :], r2_ref[at, :], r3_ref[at, :])
        ref[:n, :] = total.astype(ref.dtype)
        ref[n:, :] = share.astype(BF16).astype(ref.dtype)


def x_sum_grad(keep, received):
    shape = (CLSP + SHARE, BS)
    return call(x_sum_grad_body, [(shape, BF16)] * 3 + [(shape, F32)], (keep, *received))


def z_sum_grad_body(keep_ref, r1_ref, r2_ref, r3_ref, logit_ref, share_ref):
    total = four(keep_ref[...], r1_ref[...], r2_ref[...], r3_ref[...])
    logit_ref[...] = total[: logit_ref.shape[0], :].astype(BF16)
    for c in range(8):
        share_ref[c] = total[CLSP:, :].astype(BF16)


def z_sum_grad(keep, received, classes):
    return call(
        z_sum_grad_body,
        [((classes, BS), BF16), ((8, SHARE, BS), BF16)],
        (keep, *received),
    )


def aggregate_body(keep_ref, r1_ref, r2_ref, r3_ref, send_ref):
    agg = four(keep_ref[...], r1_ref[...], r2_ref[...], r3_ref[...]).astype(BF16)
    for c in range(8):
        send_ref[c] = agg


def aggregate(keep, received):
    return call(aggregate_body, [((8, BS, BS), BF16)], (keep, *received))[0]


def share_sum_body(parts_ref, out_ref):
    total = parts_ref[0].astype(F32)
    for c in range(1, 8):
        total = total + parts_ref[c].astype(F32)
    out_ref[...] = total


def share_sum(parts):
    return call(share_sum_body, [((SHARE, BS), F32)], (parts,))[0]


def unpack_body(me_ref, own_ref, r1_ref, r2_ref, r3_ref, in_ref, out_ref, all_ref):
    x = me_ref[0] // 8
    for d, ref in enumerate((own_ref, r1_ref, r2_ref, r3_ref)):
        all_ref[lax.bitwise_xor(d, x)] = ref[...]
    unit = 0
    for ref in (in_ref, out_ref):
        for side in range(2):
            for u in range(-(-ref.shape[0] // UNIT)):
                place, at = divmod(unit, UNITS)
                rows = min(UNIT, ref.shape[0] - u * UNIT)
                ref[u * UNIT : u * UNIT + rows, side * BS : (side + 1) * BS] = all_ref[
                    place, at * UNIT : at * UNIT + rows, :
                ]
                unit += 1


def unpack(me, own, received, classes):
    return call(
        unpack_body,
        [((128, 256), F32), ((classes, 256), F32)],
        (me, own, *received),
        [smem()] + [vmem()] * 4,
        [pltpu.VMEM((4, SHARE, BS), F32)],
    )


def permute(x, flip):
    return lax.ppermute(x, "row", [(i, i ^ flip) for i in range(32)])


CORE = 1
Z_FLIPS = (2, 4, 6)
X_FLIPS = (8, 16, 24)


def on_device(features, block_values, block_slots, block_counts, w_in, w_out, logit_grad):
    classes = logit_grad.shape[1]
    me = lax.axis_index("row").astype(jnp.int32).reshape(1)
    w_out_t = w_out.T
    feature_parts = lax.all_to_all(eight_copies(features), "col", 0, 0).reshape(1024, BS)
    dense = densify(me, block_counts, block_slots, block_values)
    grad_t = logit_grad.T
    grad_z = jnp.stack([grad_t] + [permute(grad_t, f) for f in Z_FLIPS])
    grad_near = jnp.concatenate([grad_z] + [permute(grad_z, f) for f in X_FLIPS])
    grad_far = permute(grad_near, CORE)

    far = rows_product(dense, feature_parts, 1, F32)
    got = permute(far, CORE)
    mine = rows_product(dense, feature_parts, 0, F32)
    s1, s2, s3, keep = core_sum(mine, got)
    s1, s2, s3, keep = x_sum(keep, [permute(s, f) for s, f in zip((s1, s2, s3), X_FLIPS)])
    received = [permute(s, f) for s, f in zip((s1, s2, s3), Z_FLIPS)]
    q = class_columns(grad_near, grad_far, dense)
    agg = lax.all_to_all(aggregate(keep, received), "col", 0, 0).reshape(1024, BS)

    wide, far = class_rows_far(agg, w_in, w_out_t, q, me, dense)
    got = permute(far, CORE)
    mine = class_rows_near(wide, dense)
    s1, s2, s3, keep = core_sum_grad(mine, far, got)
    s1, s2, s3, keep = x_sum_grad(keep, [permute(s, f) for s, f in zip((s1, s2, s3), X_FLIPS)])
    received = [permute(s, f) for s, f in zip((s1, s2, s3), Z_FLIPS)]
    logits_t, shares = z_sum_grad(keep, received, classes)
    own = share_sum(lax.all_to_all(shares, "col", 0, 0))
    in_grad, out_grad_t = unpack(me, own, [permute(own, f) for f in X_FLIPS], classes)
    return (logits_t.T, in_grad, out_grad_t.T)


def solution(mesh):
    return jax.shard_map(
        on_device,
        mesh=mesh,
        in_specs=(
            P(("col", "row"), None),
            P(("row", "col"), None, None),
            P(("row", "col")),
            P(("row", "col")),
            P(),
            P(),
            P(("col", "row"), None),
        ),
        out_specs=(P(("col", "row"), None), P(), P()),
        check_vma=False,
    )
```

time: 765 us -> 149 us (0.19)
  waiting for transfers between devices: 476 us -> 45.2 us
  other arithmetic: 90 us -> 0.03 us
  blocking collectives: 91.9 us -> 16.2 us
  matrix products: 52.1 us -> 0 us
  starting transfers between devices: 0.39 us -> 50.4 us
  local copies, waits for them, and re-layouts: 36.8 us -> 5.05 us
  Pallas kernels: 0 us -> 30.1 us
  between operations: 14.5 us -> 1.54 us
    psum x1 -> x0, waiting for transfers between devices: 251 us -> none  [on_device(): lax.psum((input_grad, output_grad), ('row', 'col'))]
    reduce_scatter x3 -> x0, waiting for transfers between devices: 226 us -> none  [the longest x1 146 us: on_device(): lax.psum_scatter(hidden_terms, 'row', scatter_dimension=0, tiled=True)]
    all_gather x2 -> x0, blocking collectives: 91.9 us -> none  [the longest x1 46.1 us: on_device(): input_all = lax.all_gather(features, 'col', axis=0, tiled=True)]
    scatter-add x3 -> x0, other arithmetic: 89.3 us -> none  [collect(): summed = jax.ops.segment_sum(products, block_index, num_segments=segments)]
    dot_general x8 -> x0, matrix products: 52.1 us -> none  [the longest x2 23.2 us: block_product(): jnp.einsum(form, tile_blocks, picked, preferred_element_type=jnp.float32)]
    ppermute x0 -> x24, waiting for transfers between devices: none -> 37.2 us  [permute(): return lax.ppermute(x, 'row', [(i, i ^ flip) for i in range(32)])]
    ppermute x0 -> x24, starting transfers between devices: none -> 31.7 us  [permute(): return lax.ppermute(x, 'row', [(i, i ^ flip) for i in range(32)])]
    pallas_call x0 -> x15, Pallas kernels: none -> 30.1 us  [call(): pl.pallas_call(body, out_shape=[o if len(o) == 1 else jax.ShapeDtypeStruc...]
  transfers between devices with their start and end apart: 5 -> 26, of which waited for: 3 -> 17; matrix products, arithmetic and copies ran while one was open for 22% -> 1% of each run, Pallas kernels for 0% -> 16%
where the time goes in v1:
time: 149 us
  starting transfers between devices  50.4 us (34%)
  waiting for transfers between devices  45.2 us (30%)
  Pallas kernels  30.1 us (20%)
  blocking collectives  16.2 us (11%)
  local copies, waits for them, and re-layouts  5.05 us (3%)
  between operations  1.54 us (1%)
    ppermute x24, waiting for transfers between devices, permute(): return lax.ppermute(x, 'row', [(i, i ^ flip) for i in range(32)])  37.2 us
    ppermute x24, starting transfers between devices, permute(): return lax.ppermute(x, 'row', [(i, i ^ flip) for i in range(32)])  31.7 us
    pallas_call x15, Pallas kernels, call(): pl.pallas_call(body, out_shape=[o if len(o) == 1 else jax.ShapeDtypeStruc...  30.1 us
    all_to_all x1, blocking collectives, on_device(): own = share_sum(lax.all_to_all(shares, 'col', 0, 0))  16.2 us
    all_to_all x1, starting transfers between devices, on_device(): lax.all_to_all(eight_copies(features), 'col', 0, 0).reshape(1024, BS)  9.85 us
    all_to_all x1, starting transfers between devices, on_device(): lax.all_to_all(aggregate(keep, received), 'col', 0, 0).reshape(1024, BS)  8.84 us
    all_to_all x1, waiting for transfers between devices, on_device(): lax.all_to_all(aggregate(keep, received), 'col', 0, 0).reshape(1024, BS)  7.97 us
    unnamed x18, local copies, waits for them, and re-layouts  4.66 us
  transfers between devices with their start and end apart: 26, of which 17 were waited for; matrix products, arithmetic and copies ran while one was open for 1% of the time, Pallas kernels for 16%

profile of v1, /device:TPU:32, one launch (start us, length us, event | category | flops | bytes accessed | tf_op | source)
XLA Modules:
  0.0 148.6 jit_solution(7024835953949199541)
XLA Ops:
  6.1 9.8 %all-to-all-start = ((bf16[8,128,128]{2,1,0:T(8,128)(2,1)}), bf16[8,128,128]{2,1,0:T(8,128)(2,1)S(1)}, u32[]{:S(2)}, u32[]{:S(2)}) async-start(bf16[8,128,128]{2,1,0:T(8,128)(2,1)} %shard_map.95), calls=%async_computation | async-start | bytes 524288 | tf_op jit(solution)/shard_map/all_to_all | solution.py:360
  17.4 2.3 %copy-done = bf16[144,128,128]{2,1,0:T(8,128)(2,1)S(1)} copy-done((bf16[144,128,128]{2,1,0:T(8,128)(2,1)S(1)}, bf16[144,128,128]{2,1,0:T(8,128)(2,1)}, u32[]{:S(2)}) %copy-start) | copy-done | bytes 4718616
  20.4 6.8 %shard_map.94.dense_ref = bf16[4096,1024]{1,0:T(8,128)(2,1)} custom-call(s32[1]{0:T(128)} %bitcast.me_ref, s32[1]{0:T(128)S(6)} %copy.18.count_ref, s32[144]{0:T(256)S(1)} %copy-done.4, bf16[144,128,128]{2,1,0:T(8,128)(2,1)S(1)} %copy-done), custom_call_target="tpu_custom_call" | custom-call | bytes 1048576 | tf_op jit(solution)/shard_map/pallas_call | solution.py:34
  27.2 2.4 %collective-permute-start.10 = (bf16[4,172,128]{2,1,0:T(8,128)(2,1)S(1)}, bf16[4,172,128]{2,1,0:T(8,128)(2,1)S(1)}, u32[]{:S(2)}, u32[]{:S(2)}) collective-permute-start(bf16[4,172,128]{2,1,0:T(8,128)(2,1)S(1)} %pad_maximum_fusion), channel_id=1, source_target_pairs={{0,64},{8,72},{16,80},{24,88},{32,96},{40,104},{48,112},{56,120},{... | collective-permute-start | bytes 528392 | tf_op jit(solution)/shard_map/ppermute | solution.py:348
  32.4 4.0 %shard_map.97 = f32[2048,128]{1,0:T(8,128)S(1)} custom-call(bf16[4096,1024]{1,0:T(8,128)(2,1)} %shard_map.94.dense_ref, bf16[1024,128]{1,0:T(8,128)(2,1)S(1)} %bitcast.16), custom_call_target="tpu_custom_call" | custom-call | flops 1073741824 | bytes 1048576 | tf_op jit(solution)/shard_map/pallas_call | solution.py:34
  40.5 4.0 %shard_map.96.mine_ref = f32[2048,128]{1,0:T(8,128)S(1)} custom-call(bf16[4096,1024]{1,0:T(8,128)(2,1)} %shard_map.94.dense_ref, bf16[1024,128]{1,0:T(8,128)(2,1)S(1)} %bitcast.17), custom_call_target="tpu_custom_call" | custom-call | flops 1073741824 | bytes 1048576 | tf_op jit(solution)/shard_map/pallas_call | solution.py:34
  46.8 2.6 %collective-permute-start.3 = (bf16[512,128]{1,0:T(8,128)(2,1)S(1)}, bf16[512,128]{1,0:T(8,128)(2,1)S(1)}, u32[]{:S(2)}, u32[]{:S(2)}) collective-permute-start(bf16[512,128]{1,0:T(8,128)(2,1)S(1)} %get-tuple-element.28), channel_id=1, source_target_pairs={{0,192},{8,200},{16,208},{24,216},{32,224},{40,232},{48,240},{56,2... | collective-permute-start | bytes 393224 | tf_op jit(solution)/shard_map/ppermute | solution.py:348
  51.0 2.6 %collective-permute-done.2.r2_ref = bf16[512,128]{1,0:T(8,128)(2,1)S(1)} collective-permute-done((bf16[512,128]{1,0:T(8,128)(2,1)S(1)}, bf16[512,128]{1,0:T(8,128)(2,1)S(1)}, u32[]{:S(2)}, u32[]{:S(2)}) %collective-permute-start.2) | collective-permute-done | bytes 131104 | tf_op jit(solution)/shard_map/ppermute | solution.py:348
  53.6 2.4 %collective-permute-done.3.r3_ref = bf16[512,128]{1,0:T(8,128)(2,1)S(1)} collective-permute-done((bf16[512,128]{1,0:T(8,128)(2,1)S(1)}, bf16[512,128]{1,0:T(8,128)(2,1)S(1)}, u32[]{:S(2)}, u32[]{:S(2)}) %collective-permute-start.3) | collective-permute-done | bytes 131104 | tf_op jit(solution)/shard_map/ppermute | solution.py:348
  56.1 2.8 %collective-permute-start.4 = (bf16[128,128]{1,0:T(8,128)(2,1)S(1)}, bf16[128,128]{1,0:T(8,128)(2,1)S(1)}, u32[]{:S(2)}, u32[]{:S(2)}) collective-permute-start(bf16[128,128]{1,0:T(8,128)(2,1)S(1)} %get-tuple-element.30), channel_id=1, source_target_pairs={{0,16},{8,24},{16,0},{24,8},{32,48},{40,56},{48,32},{56,40},{64,80... | collective-permute-start | bytes 98312 | tf_op jit(solution)/shard_map/ppermute | solution.py:348
  60.7 2.9 %collective-permute-done.5.r2_ref = bf16[128,128]{1,0:T(8,128)(2,1)S(1)} collective-permute-done((bf16[128,128]{1,0:T(8,128)(2,1)S(1)}, bf16[128,128]{1,0:T(8,128)(2,1)S(1)}, u32[]{:S(2)}, u32[]{:S(2)}) %collective-permute-start.5) | collective-permute-done | bytes 32800 | tf_op jit(solution)/shard_map/ppermute | solution.py:348
  65.5 8.8 %all-to-all-start.1 = ((bf16[8,128,128]{2,1,0:T(8,128)(2,1)}), bf16[8,128,128]{2,1,0:T(8,128)(2,1)S(1)}, u32[]{:S(2)}, u32[]{:S(2)}) async-start(bf16[8,128,128]{2,1,0:T(8,128)(2,1)} %shard_map.100), calls=%async_computation.1 | async-start | bytes 524288 | tf_op jit(solution)/shard_map/all_to_all | solution.py:374
  74.6 4.3 %shard_map.101.q_ref = f32[172,1024]{1,0:T(8,128)S(1)} custom-call(bf16[16,172,128]{2,1,0:T(8,128)(2,1)S(1)} %constant_dynamic-update-slice_fusion.near_ref, bf16[16,172,128]{2,1,0:T(8,128)(2,1)S(1)} %copy.11.far_ref, bf16[4096,1024]{1,0:T(8,128)(2,1)} %shard_map.94.dense_ref), custom_call_target="tpu_custom_call" | custom-call | flops 2147483648 | bytes 1048576 | tf_op jit(solution)/shard_map/pallas_call | solution.py:34
  78.9 8.0 %all-to-all-done.1 = bf16[8,128,128]{2,1,0:T(8,128)(2,1)S(1)} async-done(((bf16[8,128,128]{2,1,0:T(8,128)(2,1)}), bf16[8,128,128]{2,1,0:T(8,128)(2,1)S(1)}, u32[]{:S(2)}, u32[]{:S(2)}) %all-to-all-start.1) | async-done | bytes 262176 | tf_op jit(solution)/shard_map/all_to_all | solution.py:374
  86.9 4.3 %shard_map.102 = (bf16[176,1024]{1,0:T(8,128)(2,1)S(1)}, bf16[3456,128]{1,0:T(8,128)(2,1)S(1)}) custom-call(bf16[1024,128]{1,0:T(8,128)(2,1)S(1)} %bitcast.18, bf16[128,256]{1,0:T(8,128)(2,1)S(1)} %copy-done.2, bf16[172,256]{1,0:T(8,128)(2,1)S(1)} %bitcast.19, f32[172,1024]{1,0:T(8,128)S(1)} %shard_map.101.q_ref, s32[1]{0:T(128)} %bitcast.me_ref, ...), custom_call_target="tpu_custom_call" | custom-call | flops 2147483648 | bytes 1048576 | tf_op jit(solution)/shard_map/pallas_call | solution.py:34
  91.3 3.3 %shard_map.103.mine_ref = f32[2816,128]{1,0:T(8,128)S(1)} custom-call(bf16[176,1024]{1,0:T(8,128)(2,1)S(1)} %get-tuple-element.33.wide_ref, bf16[4096,1024]{1,0:T(8,128)(2,1)} %shard_map.94.dense_ref), custom_call_target="tpu_custom_call" | custom-call | flops 1073741824 | bytes 1048576 | tf_op jit(solution)/shard_map/pallas_call | solution.py:34
  94.9 4.5 %collective-permute-start.16 = (bf16[864,128]{1,0:T(8,128)(2,1)S(1)}, bf16[864,128]{1,0:T(8,128)(2,1)S(1)}, u32[]{:S(2)}, u32[]{:S(2)}) collective-permute-start(bf16[864,128]{1,0:T(8,128)(2,1)S(1)} %get-tuple-element.37), channel_id=1, source_target_pairs={{0,128},{8,136},{16,144},{24,152},{32,160},{40,168},{48,176},{56,1... | collective-permute-start | bytes 663560 | tf_op jit(solution)/shard_map/ppermute | solution.py:348
  99.6 3.5 %collective-permute-done.15.r1_ref = bf16[864,128]{1,0:T(8,128)(2,1)S(1)} collective-permute-done((bf16[864,128]{1,0:T(8,128)(2,1)S(1)}, bf16[864,128]{1,0:T(8,128)(2,1)S(1)}, u32[]{:S(2)}, u32[]{:S(2)}) %collective-permute-start.15) | collective-permute-done | bytes 221216 | tf_op jit(solution)/shard_map/ppermute | solution.py:348
  103.1 6.9 %collective-permute-done.16.r2_ref = bf16[864,128]{1,0:T(8,128)(2,1)S(1)} collective-permute-done((bf16[864,128]{1,0:T(8,128)(2,1)S(1)}, bf16[864,128]{1,0:T(8,128)(2,1)S(1)}, u32[]{:S(2)}, u32[]{:S(2)}) %collective-permute-start.16) | collective-permute-done | bytes 221216 | tf_op jit(solution)/shard_map/ppermute | solution.py:348
  110.0 2.6 %collective-permute-done.17.r3_ref = bf16[864,128]{1,0:T(8,128)(2,1)S(1)} collective-permute-done((bf16[864,128]{1,0:T(8,128)(2,1)S(1)}, bf16[864,128]{1,0:T(8,128)(2,1)S(1)}, u32[]{:S(2)}, u32[]{:S(2)}) %collective-permute-start.17) | collective-permute-done | bytes 221216 | tf_op jit(solution)/shard_map/ppermute | solution.py:348
  113.2 2.1 %collective-permute-start.19 = (bf16[336,128]{1,0:T(8,128)(2,1)S(1)}, bf16[336,128]{1,0:T(8,128)(2,1)S(1)}, u32[]{:S(2)}, u32[]{:S(2)}) collective-permute-start(bf16[336,128]{1,0:T(8,128)(2,1)S(1)} %get-tuple-element.41), channel_id=1, source_target_pairs={{0,32},{8,40},{16,48},{24,56},{32,0},{40,8},{48,16},{56,24},{64,96... | collective-permute-start | bytes 258056 | tf_op jit(solution)/shard_map/ppermute | solution.py:348
  118.0 3.0 %collective-permute-done.19.r2_ref = bf16[336,128]{1,0:T(8,128)(2,1)S(1)} collective-permute-done((bf16[336,128]{1,0:T(8,128)(2,1)S(1)}, bf16[336,128]{1,0:T(8,128)(2,1)S(1)}, u32[]{:S(2)}, u32[]{:S(2)}) %collective-permute-start.19) | collective-permute-done | bytes 86048 | tf_op jit(solution)/shard_map/ppermute | solution.py:348
  123.7 16.2 %all_to_all.15.parts_ref = bf16[8,160,128]{2,1,0:T(8,128)(2,1)S(1)} all-to-all(bf16[8,160,128]{2,1,0:T(8,128)(2,1)S(1)} %get-tuple-element.44), channel_id=1, replica_groups=mesh['row'=32,'col'=8] {'col'}, dimensions={0} | all-to-all | bytes 655360 | tf_op jit(solution)/shard_map/all_to_all | solution.py:383
  142.1 2.6 %collective-permute-start.23 = (f32[160,128]{1,0:T(8,128)S(1)}, f32[160,128]{1,0:T(8,128)S(1)}, u32[]{:S(2)}, u32[]{:S(2)}) collective-permute-start(f32[160,128]{1,0:T(8,128)S(1)} %shard_map.107.own_ref), channel_id=1, source_target_pairs={{0,192},{8,200},{16,208},{24,216},{32,224},{40,232},{48,240},{56,2... | collective-permute-start | bytes 245768 | tf_op jit(solution)/shard_map/ppermute | solution.py:348
  (66 shorter events, 34.2 us)
Async XLA Ops:
  0.6 26.5 %collective-permute-start.7 = (bf16[172,128]{1,0:T(8,128)(2,1)}, bf16[172,128]{1,0:T(8,128)(2,1)S(1)}, u32[]{:S(2)}, u32[]{:S(2)}) collective-permute-start(bf16[172,128]{1,0:T(8,128)(2,1)} %bitcast.20), channel_id=1, source_target_pairs={{0,16},{8,24},{16,0},{24,8},{32,48},{40,56},{48,32},{56,40},{64,80... | collective-permute-start | bytes 132104 | tf_op jit(solution)/shard_map/ppermute | solution.py:348
  2.6 24.6 %collective-permute-start.8 = (bf16[172,128]{1,0:T(8,128)(2,1)}, bf16[172,128]{1,0:T(8,128)(2,1)S(1)}, u32[]{:S(2)}, u32[]{:S(2)}) collective-permute-start(bf16[172,128]{1,0:T(8,128)(2,1)} %bitcast.21), channel_id=1, source_target_pairs={{0,32},{8,40},{16,48},{24,56},{32,0},{40,8},{48,16},{56,24},{64,96... | collective-permute-start | bytes 132104 | tf_op jit(solution)/shard_map/ppermute | solution.py:348
  4.1 23.1 %collective-permute-start.9 = (bf16[172,128]{1,0:T(8,128)(2,1)}, bf16[172,128]{1,0:T(8,128)(2,1)S(1)}, u32[]{:S(2)}, u32[]{:S(2)}) collective-permute-start(bf16[172,128]{1,0:T(8,128)(2,1)} %bitcast.22), channel_id=1, source_target_pairs={{0,48},{8,56},{16,32},{24,40},{32,16},{40,24},{48,0},{56,8},{64,11... | collective-permute-start | bytes 132104 | tf_op jit(solution)/shard_map/ppermute | solution.py:348
  6.1 26.3 %all-to-all-start = ((bf16[8,128,128]{2,1,0:T(8,128)(2,1)}), bf16[8,128,128]{2,1,0:T(8,128)(2,1)S(1)}, u32[]{:S(2)}, u32[]{:S(2)}) async-start(bf16[8,128,128]{2,1,0:T(8,128)(2,1)} %shard_map.95), calls=%async_computation | async-start | bytes 524288 | tf_op jit(solution)/shard_map/all_to_all | solution.py:360
  27.2 9.4 %collective-permute-start.10 = (bf16[4,172,128]{2,1,0:T(8,128)(2,1)S(1)}, bf16[4,172,128]{2,1,0:T(8,128)(2,1)S(1)}, u32[]{:S(2)}, u32[]{:S(2)}) collective-permute-start(bf16[4,172,128]{2,1,0:T(8,128)(2,1)S(1)} %pad_maximum_fusion), channel_id=1, source_target_pairs={{0,64},{8,72},{16,80},{24,88},{32,96},{40,104},{48,112},{56,120},{... | collective-permute-start | bytes 528392 | tf_op jit(solution)/shard_map/ppermute | solution.py:348
  29.6 8.5 %collective-permute-start.11 = (bf16[4,172,128]{2,1,0:T(8,128)(2,1)S(1)}, bf16[4,172,128]{2,1,0:T(8,128)(2,1)S(1)}, u32[]{:S(2)}, u32[]{:S(2)}) collective-permute-start(bf16[4,172,128]{2,1,0:T(8,128)(2,1)S(1)} %pad_maximum_fusion), channel_id=1, source_target_pairs={{0,128},{8,136},{16,144},{24,152},{32,160},{40,168},{48,176},{56,1... | collective-permute-start | bytes 528392 | tf_op jit(solution)/shard_map/ppermute | solution.py:348
  30.8 9.4 %collective-permute-start.12 = (bf16[4,172,128]{2,1,0:T(8,128)(2,1)S(1)}, bf16[4,172,128]{2,1,0:T(8,128)(2,1)S(1)}, u32[]{:S(2)}, u32[]{:S(2)}) collective-permute-start(bf16[4,172,128]{2,1,0:T(8,128)(2,1)S(1)} %pad_maximum_fusion), channel_id=1, source_target_pairs={{0,192},{8,200},{16,208},{24,216},{32,224},{40,232},{48,240},{56,2... | collective-permute-start | bytes 528392 | tf_op jit(solution)/shard_map/ppermute | solution.py:348
  36.4 8.1 %collective-permute-start = (f32[2048,128]{1,0:T(8,128)S(1)}, f32[2048,128]{1,0:T(8,128)S(1)}, u32[]{:S(2)}, u32[]{:S(2)}) collective-permute-start(f32[2048,128]{1,0:T(8,128)S(1)} %shard_map.97), channel_id=1, source_target_pairs={{0,8},{8,0},{16,24},{24,16},{32,40},{40,32},{48,56},{56,48},{64,72... | collective-permute-start | bytes 3145736 | tf_op jit(solution)/shard_map/ppermute | solution.py:348
  40.4 34.0 %collective-permute-start.13 = (bf16[16,172,128]{2,0,1:T(8,128)(2,1)S(1)}, bf16[16,172,128]{2,0,1:T(8,128)(2,1)S(1)}, u32[]{:S(2)}, u32[]{:S(2)}) collective-permute-start(bf16[16,172,128]{2,0,1:T(8,128)(2,1)S(1)} %copy.10), channel_id=1, source_target_pairs={{0,8},{8,0},{16,24},{24,16},{32,40},{40,32},{48,56},{56,48},{64,72... | collective-permute-start | bytes 2113544 | tf_op jit(solution)/shard_map/ppermute | solution.py:348
  44.6 6.4 %collective-permute-start.1 = (bf16[512,128]{1,0:T(8,128)(2,1)S(1)}, bf16[512,128]{1,0:T(8,128)(2,1)S(1)}, u32[]{:S(2)}, u32[]{:S(2)}) collective-permute-start(bf16[512,128]{1,0:T(8,128)(2,1)S(1)} %get-tuple-element.26), channel_id=1, source_target_pairs={{0,64},{8,72},{16,80},{24,88},{32,96},{40,104},{48,112},{56,120},{... | collective-permute-start | bytes 393224 | tf_op jit(solution)/shard_map/ppermute | solution.py:348
  44.7 8.9 %collective-permute-start.2 = (bf16[512,128]{1,0:T(8,128)(2,1)S(1)}, bf16[512,128]{1,0:T(8,128)(2,1)S(1)}, u32[]{:S(2)}, u32[]{:S(2)}) collective-permute-start(bf16[512,128]{1,0:T(8,128)(2,1)S(1)} %get-tuple-element.27), channel_id=1, source_target_pairs={{0,128},{8,136},{16,144},{24,152},{32,160},{40,168},{48,176},{56,1... | collective-permute-start | bytes 393224 | tf_op jit(solution)/shard_map/ppermute | solution.py:348
  46.8 9.2 %collective-permute-start.3 = (bf16[512,128]{1,0:T(8,128)(2,1)S(1)}, bf16[512,128]{1,0:T(8,128)(2,1)S(1)}, u32[]{:S(2)}, u32[]{:S(2)}) collective-permute-start(bf16[512,128]{1,0:T(8,128)(2,1)S(1)} %get-tuple-element.28), channel_id=1, source_target_pairs={{0,192},{8,200},{16,208},{24,216},{32,224},{40,232},{48,240},{56,2... | collective-permute-start | bytes 393224 | tf_op jit(solution)/shard_map/ppermute | solution.py:348
  56.1 4.7 %collective-permute-start.4 = (bf16[128,128]{1,0:T(8,128)(2,1)S(1)}, bf16[128,128]{1,0:T(8,128)(2,1)S(1)}, u32[]{:S(2)}, u32[]{:S(2)}) collective-permute-start(bf16[128,128]{1,0:T(8,128)(2,1)S(1)} %get-tuple-element.30), channel_id=1, source_target_pairs={{0,16},{8,24},{16,0},{24,8},{32,48},{40,56},{48,32},{56,40},{64,80... | collective-permute-start | bytes 98312 | tf_op jit(solution)/shard_map/ppermute | solution.py:348
  58.9 4.8 %collective-permute-start.5 = (bf16[128,128]{1,0:T(8,128)(2,1)S(1)}, bf16[128,128]{1,0:T(8,128)(2,1)S(1)}, u32[]{:S(2)}, u32[]{:S(2)}) collective-permute-start(bf16[128,128]{1,0:T(8,128)(2,1)S(1)} %get-tuple-element.31), channel_id=1, source_target_pairs={{0,32},{8,40},{16,48},{24,56},{32,0},{40,8},{48,16},{56,24},{64,96... | collective-permute-start | bytes 98312 | tf_op jit(solution)/shard_map/ppermute | solution.py:348
  65.5 21.4 %all-to-all-start.1 = ((bf16[8,128,128]{2,1,0:T(8,128)(2,1)}), bf16[8,128,128]{2,1,0:T(8,128)(2,1)S(1)}, u32[]{:S(2)}, u32[]{:S(2)}) async-start(bf16[8,128,128]{2,1,0:T(8,128)(2,1)} %shard_map.100), calls=%async_computation.1 | async-start | bytes 524288 | tf_op jit(solution)/shard_map/all_to_all | solution.py:374
  94.8 8.3 %collective-permute-start.15 = (bf16[864,128]{1,0:T(8,128)(2,1)S(1)}, bf16[864,128]{1,0:T(8,128)(2,1)S(1)}, u32[]{:S(2)}, u32[]{:S(2)}) collective-permute-start(bf16[864,128]{1,0:T(8,128)(2,1)S(1)} %get-tuple-element.36), channel_id=1, source_target_pairs={{0,64},{8,72},{16,80},{24,88},{32,96},{40,104},{48,112},{56,120},{... | collective-permute-start | bytes 663560 | tf_op jit(solution)/shard_map/ppermute | solution.py:348
  94.9 15.1 %collective-permute-start.16 = (bf16[864,128]{1,0:T(8,128)(2,1)S(1)}, bf16[864,128]{1,0:T(8,128)(2,1)S(1)}, u32[]{:S(2)}, u32[]{:S(2)}) collective-permute-start(bf16[864,128]{1,0:T(8,128)(2,1)S(1)} %get-tuple-element.37), channel_id=1, source_target_pairs={{0,128},{8,136},{16,144},{24,152},{32,160},{40,168},{48,176},{56,1... | collective-permute-start | bytes 663560 | tf_op jit(solution)/shard_map/ppermute | solution.py:348
  99.4 13.2 %collective-permute-start.17 = (bf16[864,128]{1,0:T(8,128)(2,1)S(1)}, bf16[864,128]{1,0:T(8,128)(2,1)S(1)}, u32[]{:S(2)}, u32[]{:S(2)}) collective-permute-start(bf16[864,128]{1,0:T(8,128)(2,1)S(1)} %get-tuple-element.38), channel_id=1, source_target_pairs={{0,192},{8,200},{16,208},{24,216},{32,224},{40,232},{48,240},{56,2... | collective-permute-start | bytes 663560 | tf_op jit(solution)/shard_map/ppermute | solution.py:348
  112.7 5.3 %collective-permute-start.18 = (bf16[336,128]{1,0:T(8,128)(2,1)S(1)}, bf16[336,128]{1,0:T(8,128)(2,1)S(1)}, u32[]{:S(2)}, u32[]{:S(2)}) collective-permute-start(bf16[336,128]{1,0:T(8,128)(2,1)S(1)} %get-tuple-element.40), channel_id=1, source_target_pairs={{0,16},{8,24},{16,0},{24,8},{32,48},{40,56},{48,32},{56,40},{64,80... | collective-permute-start | bytes 258056 | tf_op jit(solution)/shard_map/ppermute | solution.py:348
  113.2 7.7 %collective-permute-start.19 = (bf16[336,128]{1,0:T(8,128)(2,1)S(1)}, bf16[336,128]{1,0:T(8,128)(2,1)S(1)}, u32[]{:S(2)}, u32[]{:S(2)}) collective-permute-start(bf16[336,128]{1,0:T(8,128)(2,1)S(1)} %get-tuple-element.41), channel_id=1, source_target_pairs={{0,32},{8,40},{16,48},{24,56},{32,0},{40,8},{48,16},{56,24},{64,96... | collective-permute-start | bytes 258056 | tf_op jit(solution)/shard_map/ppermute | solution.py:348
  115.3 7.7 %collective-permute-start.20 = (bf16[336,128]{1,0:T(8,128)(2,1)S(1)}, bf16[336,128]{1,0:T(8,128)(2,1)S(1)}, u32[]{:S(2)}, u32[]{:S(2)}) collective-permute-start(bf16[336,128]{1,0:T(8,128)(2,1)S(1)} %get-tuple-element.42), channel_id=1, source_target_pairs={{0,48},{8,56},{16,32},{24,40},{32,16},{40,24},{48,0},{56,8},{64,11... | collective-permute-start | bytes 258056 | tf_op jit(solution)/shard_map/ppermute | solution.py:348
  140.0 4.8 %collective-permute-start.21 = (f32[160,128]{1,0:T(8,128)S(1)}, f32[160,128]{1,0:T(8,128)S(1)}, u32[]{:S(2)}, u32[]{:S(2)}) collective-permute-start(f32[160,128]{1,0:T(8,128)S(1)} %shard_map.107.own_ref), channel_id=1, source_target_pairs={{0,64},{8,72},{16,80},{24,88},{32,96},{40,104},{48,112},{56,120},{... | collective-permute-start | bytes 245768 | tf_op jit(solution)/shard_map/ppermute | solution.py:348
  140.1 6.0 %collective-permute-start.22 = (f32[160,128]{1,0:T(8,128)S(1)}, f32[160,128]{1,0:T(8,128)S(1)}, u32[]{:S(2)}, u32[]{:S(2)}) collective-permute-start(f32[160,128]{1,0:T(8,128)S(1)} %shard_map.107.own_ref), channel_id=1, source_target_pairs={{0,128},{8,136},{16,144},{24,152},{32,160},{40,168},{48,176},{56,1... | collective-permute-start | bytes 245768 | tf_op jit(solution)/shard_map/ppermute | solution.py:348
  142.1 5.7 %collective-permute-start.23 = (f32[160,128]{1,0:T(8,128)S(1)}, f32[160,128]{1,0:T(8,128)S(1)}, u32[]{:S(2)}, u32[]{:S(2)}) collective-permute-start(f32[160,128]{1,0:T(8,128)S(1)} %shard_map.107.own_ref), channel_id=1, source_target_pairs={{0,192},{8,200},{16,208},{24,216},{32,224},{40,232},{48,240},{56,2... | collective-permute-start | bytes 245768 | tf_op jit(solution)/shard_map/ppermute | solution.py:348
  (8 other events, 42.9 us)

commit v2 on v1

--- a/solution.py
+++ b/solution.py
@@ -14,8 +14,10 @@
 UNIT = 16
 UNITS = 10
 SHARE = UNITS * UNIT
-VMEM_LIMIT = 48 * 1024 * 1024
+VMEM_LIMIT = 32 * 1024 * 1024
 STEP = 512
+LOADS = 3
+LOAD = 48
 
 
 def vmem():
@@ -42,80 +44,94 @@
     )(*args)
 
 
-def densify_body(me_ref, count_ref, slot_ref, block_ref, dense_ref):
+def hbm():
+    return pl.BlockSpec(memory_space=pl.ANY)
+
+
+def rows_of(dense_ref, first, i):
+    at = (first + i) * STEP
+    return dense_ref[at : at + STEP, :]
+
+
+def densify_body(
+    me_ref, side_ref, count_ref, slot_ref, block_ref, g0_ref, g1_ref, g2_ref, g3_ref,
+    dense_ref, near_ref, held_ref, sem_ref,
+):
+    moves = [
+        pltpu.make_async_copy(
+            block_ref.at[pl.ds(i * LOAD, LOAD)], held_ref.at[pl.ds(i * LOAD, LOAD)], sem_ref.at[i]
+        )
+        for i in range(LOADS)
+    ]
+    for move in moves:
+        move.start()
     dense_ref[...] = jnp.zeros_like(dense_ref)
+    for d, ref in enumerate((g0_ref, g1_ref, g2_ref, g3_ref)):
+        near_ref[d] = ref[...]
     me = me_ref[0]
+    side = side_ref[0]
+    count = count_ref[0]
 
     def place(b, carry):
         slot = slot_ref[b]
         rel = lax.bitwise_xor(slot // 8, me)
         at = (rel % 2) * 16 + rel // 2
+        across = lax.bitwise_xor(slot % 8, side)
         row = pl.multiple_of(at * BS, BS)
-        col = pl.multiple_of((slot % 8) * BS, BS)
-        dense_ref[pl.ds(row, BS), pl.ds(col, BS)] = block_ref[b]
+        col = pl.multiple_of(((across % 4) * 2 + across // 4) * BS, BS)
+        dense_ref[pl.ds(row, BS), pl.ds(col, BS)] = held_ref[b]
         return carry
 
-    lax.fori_loop(0, count_ref[0], place, 0)
-
-
-def densify(me, counts, slots, blocks):
-    return call(
-        densify_body,
-        [((4096, 1024), BF16)],
-        (me, counts, slots, blocks),
-        [smem(), smem(), smem(), vmem()],
-    )[0]
-
-
-def hbm():
-    return pl.BlockSpec(memory_space=pl.ANY)
-
-
-def stage(chunks):
-    return [pltpu.VMEM((chunks, STEP, 1024), BF16), pltpu.SemaphoreType.DMA((chunks,))]
-
-
-def copies(dense_ref, buffer_ref, sem_ref, first, chunks):
-    return [
-        pltpu.make_async_copy(
-            dense_ref.at[pl.ds((first + i) * STEP, STEP)], buffer_ref.at[i], sem_ref.at[i]
-        )
-        for i in range(chunks)
-    ]
-
-
-def rows_product_body(half, dense_ref, right_ref, out_ref, buffer_ref, sem_ref):
-    moves = copies(dense_ref, buffer_ref, sem_ref, 4 * half, 4)
-    for move in moves:
-        move.start()
-    right = right_ref[...]
     for i, move in enumerate(moves):
         move.wait()
-        out_ref[i * STEP : (i + 1) * STEP, :] = dot(buffer_ref[i], right, 1, 0).astype(out_ref.dtype)
-
-
-def rows_product(dense, right, half, dtype):
+        lax.fori_loop(i * LOAD, jnp.clip(count, i * LOAD, (i + 1) * LOAD), place, 0)
+
+
+def densify(me, side, counts, slots, blocks, cotangents):
+    return pl.pallas_call(
+        densify_body,
+        out_shape=[
+            pltpu.VMEM((4096, 1024), BF16),
+            jax.ShapeDtypeStruct((4,) + cotangents[0].shape, BF16),
+        ],
+        in_specs=[smem(), smem(), smem(), smem(), hbm()] + [vmem()] * 4,
+        out_specs=[vmem(), vmem()],
+        scratch_shapes=[pltpu.VMEM(blocks.shape, BF16), pltpu.SemaphoreType.DMA((LOADS,))],
+        compiler_params=pltpu.CompilerParams(vmem_limit_bytes=52 * 1024 * 1024),
+    )(me, side, counts, slots, blocks, *cotangents)
+
+
+def joined(refs):
+    return jnp.concatenate([ref[h] for ref in refs for h in range(2)])
+
+
+def rows_product_body(half, dense_ref, r0_ref, r1_ref, r2_ref, r3_ref, out_ref):
+    right = joined((r0_ref, r1_ref, r2_ref, r3_ref))
+    for i in range(4):
+        part = dot(rows_of(dense_ref, 4 * half, i), right, 1, 0)
+        out_ref[i * STEP : (i + 1) * STEP, :] = part.astype(out_ref.dtype)
+
+
+def rows_product(dense, parts, half, dtype):
     return call(
         functools.partial(rows_product_body, half),
         [((2048, BS), dtype)],
-        (dense, right),
-        [hbm(), vmem()],
-        stage(4),
+        (dense, *parts),
+        [vmem()] * 5,
         flops=2 * 2048 * 1024 * 256,
     )[0]
 
 
-def class_rows(wide, moves, buffer_ref, out_ref):
-    for i, move in enumerate(moves):
-        move.wait()
-        part = dot(wide, buffer_ref[i], 1, 1).astype(out_ref.dtype)
+def class_rows(wide, dense_ref, first, out_ref):
+    for i in range(4):
+        part = dot(wide, rows_of(dense_ref, first, i), 1, 1).astype(out_ref.dtype)
         for j in range(4):
             at = (i * 4 + j) * CLSP
             out_ref[at : at + CLSP, :] = part[:, j * BS : (j + 1) * BS]
 
 
-def silu_inputs(agg_ref, w_in_ref):
-    pre = dot(agg_ref[...], w_in_ref[...], 1, 0)
+def silu_inputs(agg, w_in_ref):
+    pre = dot(agg, w_in_ref[...], 1, 0)
     gate = 1.0 / (1.0 + jnp.exp(-pre))
     return pre, gate, (pre * gate).astype(BF16)
 
@@ -145,35 +161,30 @@
 
 
 def class_rows_far_body(
-    agg_ref, w_in_ref, w_out_ref, q_ref, me_ref, dense_ref, wide_ref, out_ref, buffer_ref, sem_ref
+    a0_ref, a1_ref, a2_ref, a3_ref, w_in_ref, w_out_ref, q_ref, me_ref, dense_ref,
+    wide_ref, out_ref,
 ):
-    moves = copies(dense_ref, buffer_ref, sem_ref, 4, 4)
-    for move in moves:
-        move.start()
-    pre, gate, hid = silu_inputs(agg_ref, w_in_ref)
+    agg = joined((a0_ref, a1_ref, a2_ref, a3_ref))
+    pre, gate, hid = silu_inputs(agg, w_in_ref)
     wide = dot(w_out_ref[...], hid, 1, 1)
     zeros = jnp.zeros((CLSP - wide.shape[0], wide.shape[1]), F32)
     wide_ref[...] = jnp.concatenate([wide, zeros]).astype(BF16)
-    class_rows(wide_ref[...], moves, buffer_ref, out_ref)
-    add_grads(pre, gate, hid, agg_ref[...], q_ref[...], w_out_ref[...], me_ref[0] // 8, out_ref)
+    class_rows(wide_ref[...], dense_ref, 4, out_ref)
+    add_grads(pre, gate, hid, agg, q_ref[...], w_out_ref[...], me_ref[0] // 8, out_ref)
 
 
 def class_rows_far(agg, w_in, w_out_t, q, me, dense):
     return call(
         class_rows_far_body,
         [((CLSP, 1024), BF16), ((16 * CLSP + 4 * SHARE, BS), BF16)],
-        (agg, w_in, w_out_t, q, me, dense),
-        [vmem(), vmem(), vmem(), vmem(), smem(), hbm()],
-        stage(4),
+        (*agg, w_in, w_out_t, q, me, dense),
+        [vmem()] * 7 + [smem(), vmem()],
         flops=4 * 2048 * 1024 * 256,
     )
 
 
-def class_rows_near_body(wide_ref, dense_ref, out_ref, buffer_ref, sem_ref):
-    moves = copies(dense_ref, buffer_ref, sem_ref, 0, 4)
-    for move in moves:
-        move.start()
-    class_rows(wide_ref[...], moves, buffer_ref, out_ref)
+def class_rows_near_body(wide_ref, dense_ref, out_ref):
+    class_rows(wide_ref[...], dense_ref, 0, out_ref)
 
 
 def class_rows_near(wide, dense):
@@ -181,21 +192,15 @@
         class_rows_near_body,
         [((16 * CLSP, BS), F32)],
         (wide, dense),
-        [vmem(), hbm()],
-        stage(4),
         flops=2 * 2048 * 1024 * 256,
     )[0]
 
 
-def class_columns_body(near_ref, far_ref, dense_ref, out_ref, buffer_ref, sem_ref):
-    moves = copies(dense_ref, buffer_ref, sem_ref, 0, 8)
-    for move in moves:
-        move.start()
-    for i, move in enumerate(moves):
+def class_columns_body(near_ref, far_ref, dense_ref, out_ref):
+    for i in range(8):
         ref = near_ref if i < 4 else far_ref
         left = jnp.concatenate([ref[(i % 4) * 4 + j] for j in range(4)], axis=1)
-        move.wait()
-        part = dot(left, buffer_ref[i], 1, 0)
+        part = dot(left, rows_of(dense_ref, 0, i), 1, 0)
         if i == 0:
             out_ref[...] = part
         else:
@@ -207,32 +212,30 @@
         class_columns_body,
         [((near.shape[1], 1024), F32)],
         (near, far, dense),
-        [vmem(), vmem(), hbm()],
-        stage(8),
         flops=2 * 4096 * 1024 * 256,
     )[0]
 
 
-def copies_body(features_ref, send_ref):
-    for c in range(8):
-        send_ref[c] = features_ref[...]
-
-
-def eight_copies(features):
-    return call(copies_body, [((8, BS, BS), BF16)], (features,))[0]
-
-
-def core_sum_body(mine_ref, got_ref, s1_ref, s2_ref, s3_ref, keep_ref):
+def core_sum_body(
+    mine_ref, got_ref, g0_ref, g1_ref, g2_ref, g3_ref, s1_ref, s2_ref, s3_ref, keep_ref, near_ref
+):
     n = keep_ref.shape[0]
     for d, ref in ((1, s1_ref), (2, s2_ref), (3, s3_ref), (0, keep_ref)):
         at = slice(d * n, (d + 1) * n)
         ref[...] = (mine_ref[at, :].astype(F32) + got_ref[at, :].astype(F32)).astype(ref.dtype)
-
-
-def core_sum(mine, got):
+    for d, ref in enumerate((g0_ref, g1_ref, g2_ref, g3_ref)):
+        near_ref[4 * d : 4 * d + 4] = ref[...]
+
+
+def core_sum(mine, got, cotangents):
     rows = mine.shape[0] // 4
     shape = (rows, BS)
-    return call(core_sum_body, [(shape, BF16)] * 3 + [(shape, F32)], (mine, got))
+    near = (16,) + cotangents[0].shape[1:]
+    return call(
+        core_sum_body,
+        [(shape, BF16)] * 3 + [(shape, F32), (near, BF16)],
+        (mine, got, *cotangents),
+    )
 
 
 def four(a, b, c, d):
@@ -297,14 +300,12 @@
     )
 
 
-def aggregate_body(keep_ref, r1_ref, r2_ref, r3_ref, send_ref):
-    agg = four(keep_ref[...], r1_ref[...], r2_ref[...], r3_ref[...]).astype(BF16)
-    for c in range(8):
-        send_ref[c] = agg
+def aggregate_body(keep_ref, r1_ref, r2_ref, r3_ref, out_ref):
+    out_ref[...] = four(keep_ref[...], r1_ref[...], r2_ref[...], r3_ref[...]).astype(BF16)
 
 
 def aggregate(keep, received):
-    return call(aggregate_body, [((8, BS, BS), BF16)], (keep, *received))[0]
+    return call(aggregate_body, [((BS, BS), BF16)], (keep, *received))[0]
 
 
 def share_sum_body(parts_ref, out_ref):
@@ -348,6 +349,12 @@
     return lax.ppermute(x, "row", [(i, i ^ flip) for i in range(32)])
 
 
+def gather_col(x):
+    far = lax.ppermute(x, "col", [(i, i ^ 4) for i in range(8)])
+    pair = jnp.stack([x, far])
+    return [pair] + [lax.ppermute(pair, "col", [(i, i ^ d) for i in range(8)]) for d in (1, 2, 3)]
+
+
 CORE = 1
 Z_FLIPS = (2, 4, 6)
 X_FLIPS = (8, 16, 24)
@@ -356,22 +363,23 @@
 def on_device(features, block_values, block_slots, block_counts, w_in, w_out, logit_grad):
     classes = logit_grad.shape[1]
     me = lax.axis_index("row").astype(jnp.int32).reshape(1)
+    side = lax.axis_index("col").astype(jnp.int32).reshape(1)
     w_out_t = w_out.T
-    feature_parts = lax.all_to_all(eight_copies(features), "col", 0, 0).reshape(1024, BS)
-    dense = densify(me, block_counts, block_slots, block_values)
+    parts = gather_col(features)
     grad_t = logit_grad.T
-    grad_z = jnp.stack([grad_t] + [permute(grad_t, f) for f in Z_FLIPS])
-    grad_near = jnp.concatenate([grad_z] + [permute(grad_z, f) for f in X_FLIPS])
+    cotangents = [grad_t] + [permute(grad_t, f) for f in Z_FLIPS]
+    dense, grad_z = densify(me, side, block_counts, block_slots, block_values, cotangents)
+    grad_x = [grad_z] + [permute(grad_z, f) for f in X_FLIPS]
+
+    far = rows_product(dense, parts, 1, F32)
+    got = permute(far, CORE)
+    mine = rows_product(dense, parts, 0, F32)
+    s1, s2, s3, keep, grad_near = core_sum(mine, got, grad_x)
     grad_far = permute(grad_near, CORE)
-
-    far = rows_product(dense, feature_parts, 1, F32)
-    got = permute(far, CORE)
-    mine = rows_product(dense, feature_parts, 0, F32)
-    s1, s2, s3, keep = core_sum(mine, got)
     s1, s2, s3, keep = x_sum(keep, [permute(s, f) for s, f in zip((s1, s2, s3), X_FLIPS)])
     received = [permute(s, f) for s, f in zip((s1, s2, s3), Z_FLIPS)]
     q = class_columns(grad_near, grad_far, dense)
-    agg = lax.all_to_all(aggregate(keep, received), "col", 0, 0).reshape(1024, BS)
+    agg = gather_col(aggregate(keep, received))
 
     wide, far = class_rows_far(agg, w_in, w_out_t, q, me, dense)
     got = permute(far, CORE)

time: 149 us -> 142 us (0.953)
  Pallas kernels: 30.1 us -> 14.6 us
  waiting for transfers between devices: 45.2 us -> 52.1 us
  blocking collectives: 16.2 us -> 20.6 us
  local copies, waits for them, and re-layouts: 5.05 us -> 1.01 us
    pallas_call x15 -> x13, Pallas kernels: 30.1 us -> 10.3 us  [call(): pl.pallas_call(body, out_shape=[o if len(o) == 1 else jax.ShapeDtypeStruc...]
    all_to_all x2 -> x0, starting transfers between devices: 18.7 us -> none  [the longest x1 9.85 us: on_device(): lax.all_to_all(eight_copies(features), 'col', 0, 0).reshape(1024, BS)]
    ppermute x0 -> x8, starting transfers between devices: none -> 18.7 us  [the longest x2 10.4 us: gather_col(): far = lax.ppermute(x, 'col', [(i, i ^ 4) for i in range(8)])]
    all_to_all x2 -> x0, waiting for transfers between devices: 7.97 us -> none  [the longest x1 7.97 us: on_device(): lax.all_to_all(aggregate(keep, received), 'col', 0, 0).reshape(1024, BS)]
    ppermute x0 -> x8, waiting for transfers between devices: none -> 7.94 us  [the longest x2 5.01 us: gather_col(): far = lax.ppermute(x, 'col', [(i, i ^ 4) for i in range(8)])]
    ppermute x24, waiting for transfers between devices: 37.2 us -> 44.2 us  [permute(): return lax.ppermute(x, 'row', [(i, i ^ flip) for i in range(32)])]
    all_to_all x1, blocking collectives: 16.2 us -> 20.6 us  [on_device(): own = share_sum(lax.all_to_all(shares, 'col', 0, 0))]
    pallas_call x0 -> x1, Pallas kernels: none -> 4.33 us  [densify(): pl.pallas_call(densify_body, out_shape=[pltpu.VMEM((4096, 1024), BF16), j...]
  transfers between devices with their start and end apart: 26 -> 32, of which waited for: 17 -> 23; matrix products, arithmetic and copies ran while one was open for 1% -> 1% of each run, Pallas kernels for 16% -> 6%
where the time goes in v2:
time: 142 us
  waiting for transfers between devices  52.1 us (37%)
  starting transfers between devices  51.4 us (36%)
  blocking collectives  20.6 us (15%)
  Pallas kernels  14.6 us (10%)
  between operations  1.48 us (1%)
    ppermute x24, waiting for transfers between devices, permute(): return lax.ppermute(x, 'row', [(i, i ^ flip) for i in range(32)])  44.2 us
    ppermute x24, starting transfers between devices, permute(): return lax.ppermute(x, 'row', [(i, i ^ flip) for i in range(32)])  32.8 us
    all_to_all x1, blocking collectives, on_device(): own = share_sum(lax.all_to_all(shares, 'col', 0, 0))  20.6 us
    ppermute x2, starting transfers between devices, gather_col(): far = lax.ppermute(x, 'col', [(i, i ^ 4) for i in range(8)])  10.4 us
    pallas_call x13, Pallas kernels, call(): pl.pallas_call(body, out_shape=[o if len(o) == 1 else jax.ShapeDtypeStruc...  10.3 us
    ppermute x6, starting transfers between devices, gather_col(): lax.ppermute(pair, 'col', [(i, i ^ d) for i in range(8)])  8.29 us
    ppermute x2, waiting for transfers between devices, gather_col(): far = lax.ppermute(x, 'col', [(i, i ^ 4) for i in range(8)])  5.01 us
    pallas_call x1, Pallas kernels, densify(): pl.pallas_call(densify_body, out_shape=[pltpu.VMEM((4096, 1024), BF16), j...  4.33 us
  transfers between devices with their start and end apart: 32, of which 23 were waited for; matrix products, arithmetic and copies ran while one was open for 1% of the time, Pallas kernels for 6%

profile of v2, /device:TPU:32, one launch (start us, length us, event | category | flops | bytes accessed | tf_op | source)
XLA Modules:
  0.0 142.1 jit_solution(3672298858430261704)
XLA Ops:
  0.6 6.4 %collective-permute-start.3 = (bf16[128,128]{1,0:T(8,128)(2,1)}, bf16[128,128]{1,0:T(8,128)(2,1)S(1)}, u32[]{:S(2)}, u32[]{:S(2)}) collective-permute-start(bf16[128,128]{1,0:T(8,128)(2,1)} %param.7), channel_id=1, source_target_pairs={{0,4},{1,5},{2,6},{3,7},{4,0},{5,1},{6,2},{7,3},{8,12},{9,13},{10,... | collective-permute-start | bytes 98312 | tf_op jit(solution)/shard_map/ppermute | solution.py:353
  9.9 3.0 %collective-permute-start.6 = (bf16[2,128,128]{2,1,0:T(8,128)(2,1)S(1)}, bf16[2,128,128]{2,1,0:T(8,128)(2,1)S(1)}, u32[]{:S(2)}, u32[]{:S(2)}) collective-permute-start(bf16[2,128,128]{2,1,0:T(8,128)(2,1)S(1)} %pad_maximum_fusion.r0_ref), channel_id=1, source_target_pairs={{0,3},{1,2},{2,1},{3,0},{4,7},{5,6},{6,5},{7,4},{8,11},{9,10},{10,... | collective-permute-start | bytes 196616 | tf_op jit(solution)/shard_map/ppermute | solution.py:355
  14.0 3.0 %collective-permute-start.1 = (bf16[172,128]{1,0:T(8,128)(2,1)}, bf16[172,128]{1,0:T(8,128)(2,1)S(1)}, u32[]{:S(2)}, u32[]{:S(2)}) collective-permute-start(bf16[172,128]{1,0:T(8,128)(2,1)} %bitcast.13), channel_id=1, source_target_pairs={{0,32},{8,40},{16,48},{24,56},{32,0},{40,8},{48,16},{56,24},{64,96... | collective-permute-start | bytes 132104 | tf_op jit(solution)/shard_map/ppermute | solution.py:349
  21.8 4.3 %shard_map.94 = (bf16[4096,1024]{1,0:T(8,128)(2,1)S(1)}, bf16[4,172,128]{2,1,0:T(8,128)(2,1)}) custom-call(s32[1]{0:T(128)} %bitcast.me_ref, s32[1]{0:T(128)} %bitcast.1.side_ref, s32[1]{0:T(128)S(6)} %copy.12.count_ref, s32[144]{0:T(256)} %slot_ref.1, bf16[144,128,128]{2,1,0:T(8,128)(2,1)} %block_ref.1, bf16[172,128]{1,0:T(8,128)(2,1)} %bitcast.15, ...), custom_call_target="tpu_custom_call" | custom-call | tf_op jit(solution)/shard_map/pallas_call | solution.py:91
  27.5 4.3 %collective-permute-start.10 = (bf16[4,172,128]{2,1,0:T(8,128)(2,1)S(1)}, bf16[4,172,128]{2,1,0:T(8,128)(2,1)S(1)}, u32[]{:S(2)}, u32[]{:S(2)}) collective-permute-start(bf16[4,172,128]{2,1,0:T(8,128)(2,1)S(1)} %copy-done), channel_id=1, source_target_pairs={{0,192},{8,200},{16,208},{24,216},{32,224},{40,232},{48,240},{56,2... | collective-permute-start | bytes 528392 | tf_op jit(solution)/shard_map/ppermute | solution.py:349
  35.0 5.8 %collective-permute-done.10.g3_ref = bf16[4,172,128]{2,1,0:T(8,128)(2,1)S(1)} collective-permute-done((bf16[4,172,128]{2,1,0:T(8,128)(2,1)S(1)}, bf16[4,172,128]{2,1,0:T(8,128)(2,1)S(1)}, u32[]{:S(2)}, u32[]{:S(2)}) %collective-permute-start.10) | collective-permute-done | bytes 176160 | tf_op jit(solution)/shard_map/ppermute | solution.py:349
  42.3 2.6 %collective-permute-start.11 = (bf16[512,128]{1,0:T(8,128)(2,1)S(1)}, bf16[512,128]{1,0:T(8,128)(2,1)S(1)}, u32[]{:S(2)}, u32[]{:S(2)}) collective-permute-start(bf16[512,128]{1,0:T(8,128)(2,1)S(1)} %get-tuple-element.31), channel_id=1, source_target_pairs={{0,64},{8,72},{16,80},{24,88},{32,96},{40,104},{48,112},{56,120},{... | collective-permute-start | bytes 393224 | tf_op jit(solution)/shard_map/ppermute | solution.py:349
  49.2 4.0 %collective-permute-done.12.r2_ref = bf16[512,128]{1,0:T(8,128)(2,1)S(1)} collective-permute-done((bf16[512,128]{1,0:T(8,128)(2,1)S(1)}, bf16[512,128]{1,0:T(8,128)(2,1)S(1)}, u32[]{:S(2)}, u32[]{:S(2)}) %collective-permute-start.12) | collective-permute-done | bytes 131104 | tf_op jit(solution)/shard_map/ppermute | solution.py:349
  62.7 4.0 %collective-permute-start.17 = (bf16[128,128]{1,0:T(8,128)(2,1)S(1)}, bf16[128,128]{1,0:T(8,128)(2,1)S(1)}, u32[]{:S(2)}, u32[]{:S(2)}) collective-permute-start(bf16[128,128]{1,0:T(8,128)(2,1)S(1)} %shard_map.99), channel_id=1, source_target_pairs={{0,4},{1,5},{2,6},{3,7},{4,0},{5,1},{6,2},{7,3},{8,12},{9,13},{10,... | collective-permute-start | bytes 98312 | tf_op jit(solution)/shard_map/ppermute | solution.py:353
  66.7 3.9 %collective-permute-done.17 = bf16[128,128]{1,0:T(8,128)(2,1)S(1)} collective-permute-done((bf16[128,128]{1,0:T(8,128)(2,1)S(1)}, bf16[128,128]{1,0:T(8,128)(2,1)S(1)}, u32[]{:S(2)}, u32[]{:S(2)}) %collective-permute-start.17) | collective-permute-done | bytes 32800 | tf_op jit(solution)/shard_map/ppermute | solution.py:353
  70.6 3.2 %collective-permute-start.20 = (bf16[2,128,128]{2,1,0:T(8,128)(2,1)S(1)}, bf16[2,128,128]{2,1,0:T(8,128)(2,1)S(1)}, u32[]{:S(2)}, u32[]{:S(2)}) collective-permute-start(bf16[2,128,128]{2,1,0:T(8,128)(2,1)S(1)} %pad_maximum_fusion.1.a0_ref), channel_id=1, source_target_pairs={{0,3},{1,2},{2,1},{3,0},{4,7},{5,6},{6,5},{7,4},{8,11},{9,10},{10,... | collective-permute-start | bytes 196616 | tf_op jit(solution)/shard_map/ppermute | solution.py:355
  76.9 2.7 %collective-permute-done.19.a2_ref = bf16[2,128,128]{2,1,0:T(8,128)(2,1)S(1)} collective-permute-done((bf16[2,128,128]{2,1,0:T(8,128)(2,1)S(1)}, bf16[2,128,128]{2,1,0:T(8,128)(2,1)S(1)}, u32[]{:S(2)}, u32[]{:S(2)}) %collective-permute-start.19) | collective-permute-done | bytes 65568 | tf_op jit(solution)/shard_map/ppermute | solution.py:355
  79.6 2.7 %shard_map.101 = (bf16[176,1024]{1,0:T(8,128)(2,1)S(1)}, bf16[3456,128]{1,0:T(8,128)(2,1)S(1)}) custom-call(bf16[2,128,128]{2,1,0:T(8,128)(2,1)S(1)} %pad_maximum_fusion.1.a0_ref, bf16[2,128,128]{2,1,0:T(8,128)(2,1)S(1)} %collective-permute-done.18.a1_ref, bf16[2,128,128]{2,1,0:T(8,128)(2,1)S(1)} %collective-permute-done.19.a2_ref, ...), custom_call_target="tpu_custom_call" | custom-call | flops 2147483648 | bytes 1048576 | tf_op jit(solution)/shard_map/pallas_call | solution.py:36
  87.1 2.7 %collective-permute-start.25 = (bf16[864,128]{1,0:T(8,128)(2,1)S(1)}, bf16[864,128]{1,0:T(8,128)(2,1)S(1)}, u32[]{:S(2)}, u32[]{:S(2)}) collective-permute-start(bf16[864,128]{1,0:T(8,128)(2,1)S(1)} %get-tuple-element.44), channel_id=1, source_target_pairs={{0,192},{8,200},{16,208},{24,216},{32,224},{40,232},{48,240},{56,2... | collective-permute-start | bytes 663560 | tf_op jit(solution)/shard_map/ppermute | solution.py:349
  89.8 3.6 %collective-permute-done.23.r1_ref = bf16[864,128]{1,0:T(8,128)(2,1)S(1)} collective-permute-done((bf16[864,128]{1,0:T(8,128)(2,1)S(1)}, bf16[864,128]{1,0:T(8,128)(2,1)S(1)}, u32[]{:S(2)}, u32[]{:S(2)}) %collective-permute-start.23) | collective-permute-done | bytes 221216 | tf_op jit(solution)/shard_map/ppermute | solution.py:349
  93.4 4.0 %collective-permute-done.24.r2_ref = bf16[864,128]{1,0:T(8,128)(2,1)S(1)} collective-permute-done((bf16[864,128]{1,0:T(8,128)(2,1)S(1)}, bf16[864,128]{1,0:T(8,128)(2,1)S(1)}, u32[]{:S(2)}, u32[]{:S(2)}) %collective-permute-start.24) | collective-permute-done | bytes 221216 | tf_op jit(solution)/shard_map/ppermute | solution.py:349
  97.4 2.6 %collective-permute-done.25.r3_ref = bf16[864,128]{1,0:T(8,128)(2,1)S(1)} collective-permute-done((bf16[864,128]{1,0:T(8,128)(2,1)S(1)}, bf16[864,128]{1,0:T(8,128)(2,1)S(1)}, u32[]{:S(2)}, u32[]{:S(2)}) %collective-permute-start.25) | collective-permute-done | bytes 221216 | tf_op jit(solution)/shard_map/ppermute | solution.py:349
  100.1 2.6 %collective-permute-start.26 = (bf16[336,128]{1,0:T(8,128)(2,1)S(1)}, bf16[336,128]{1,0:T(8,128)(2,1)S(1)}, u32[]{:S(2)}, u32[]{:S(2)}) collective-permute-start(bf16[336,128]{1,0:T(8,128)(2,1)S(1)} %get-tuple-element.46), channel_id=1, source_target_pairs={{0,16},{8,24},{16,0},{24,8},{32,48},{40,56},{48,32},{56,40},{64,80... | collective-permute-start | bytes 258056 | tf_op jit(solution)/shard_map/ppermute | solution.py:349
  105.7 2.4 %collective-permute-done.27.r2_ref = bf16[336,128]{1,0:T(8,128)(2,1)S(1)} collective-permute-done((bf16[336,128]{1,0:T(8,128)(2,1)S(1)}, bf16[336,128]{1,0:T(8,128)(2,1)S(1)}, u32[]{:S(2)}, u32[]{:S(2)}) %collective-permute-start.27) | collective-permute-done | bytes 86048 | tf_op jit(solution)/shard_map/ppermute | solution.py:349
  108.1 2.9 %collective-permute-done.28.r3_ref = bf16[336,128]{1,0:T(8,128)(2,1)S(1)} collective-permute-done((bf16[336,128]{1,0:T(8,128)(2,1)S(1)}, bf16[336,128]{1,0:T(8,128)(2,1)S(1)}, u32[]{:S(2)}, u32[]{:S(2)}) %collective-permute-start.28) | collective-permute-done | bytes 86048 | tf_op jit(solution)/shard_map/ppermute | solution.py:349
  111.6 20.6 %all_to_all.5.parts_ref = bf16[8,160,128]{2,1,0:T(8,128)(2,1)S(1)} all-to-all(bf16[8,160,128]{2,1,0:T(8,128)(2,1)S(1)} %get-tuple-element.50), channel_id=1, replica_groups=mesh['row'=32,'col'=8] {'col'}, dimensions={0} | all-to-all | bytes 655360 | tf_op jit(solution)/shard_map/all_to_all | solution.py:391
  132.3 3.1 %collective-permute-start.31 = (f32[160,128]{1,0:T(8,128)S(1)}, f32[160,128]{1,0:T(8,128)S(1)}, u32[]{:S(2)}, u32[]{:S(2)}) collective-permute-start(f32[160,128]{1,0:T(8,128)S(1)} %shard_map.106.own_ref), channel_id=1, source_target_pairs={{0,192},{8,200},{16,208},{24,216},{32,224},{40,232},{48,240},{56,2... | collective-permute-start | bytes 245768 | tf_op jit(solution)/shard_map/ppermute | solution.py:349
  136.5 2.4 %collective-permute-done.31.r3_ref = f32[160,128]{1,0:T(8,128)S(1)} collective-permute-done((f32[160,128]{1,0:T(8,128)S(1)}, f32[160,128]{1,0:T(8,128)S(1)}, u32[]{:S(2)}, u32[]{:S(2)}) %collective-permute-start.31) | collective-permute-done | bytes 81952 | tf_op jit(solution)/shard_map/ppermute | solution.py:349
  138.9 2.4 %collective-permute-done.30.r2_ref = f32[160,128]{1,0:T(8,128)S(1)} collective-permute-done((f32[160,128]{1,0:T(8,128)S(1)}, f32[160,128]{1,0:T(8,128)S(1)}, u32[]{:S(2)}, u32[]{:S(2)}) %collective-permute-start.30) | collective-permute-done | bytes 81952 | tf_op jit(solution)/shard_map/ppermute | solution.py:349
  (71 shorter events, 41.3 us)
Async XLA Ops:
  0.6 8.5 %collective-permute-start.3 = (bf16[128,128]{1,0:T(8,128)(2,1)}, bf16[128,128]{1,0:T(8,128)(2,1)S(1)}, u32[]{:S(2)}, u32[]{:S(2)}) collective-permute-start(bf16[128,128]{1,0:T(8,128)(2,1)} %param.7), channel_id=1, source_target_pairs={{0,4},{1,5},{2,6},{3,7},{4,0},{5,1},{6,2},{7,3},{8,12},{9,13},{10,... | collective-permute-start | bytes 98312 | tf_op jit(solution)/shard_map/ppermute | solution.py:353
  7.0 9.9 %collective-permute-start.2 = (bf16[172,128]{1,0:T(8,128)(2,1)}, bf16[172,128]{1,0:T(8,128)(2,1)S(1)}, u32[]{:S(2)}, u32[]{:S(2)}) collective-permute-start(bf16[172,128]{1,0:T(8,128)(2,1)} %bitcast.12), channel_id=1, source_target_pairs={{0,48},{8,56},{16,32},{24,40},{32,16},{40,24},{48,0},{56,8},{64,11... | collective-permute-start | bytes 132104 | tf_op jit(solution)/shard_map/ppermute | solution.py:349
  9.9 16.3 %collective-permute-start.6 = (bf16[2,128,128]{2,1,0:T(8,128)(2,1)S(1)}, bf16[2,128,128]{2,1,0:T(8,128)(2,1)S(1)}, u32[]{:S(2)}, u32[]{:S(2)}) collective-permute-start(bf16[2,128,128]{2,1,0:T(8,128)(2,1)S(1)} %pad_maximum_fusion.r0_ref), channel_id=1, source_target_pairs={{0,3},{1,2},{2,1},{3,0},{4,7},{5,6},{6,5},{7,4},{8,11},{9,10},{10,... | collective-permute-start | bytes 196616 | tf_op jit(solution)/shard_map/ppermute | solution.py:355
  12.9 13.3 %collective-permute-start.5 = (bf16[2,128,128]{2,1,0:T(8,128)(2,1)S(1)}, bf16[2,128,128]{2,1,0:T(8,128)(2,1)S(1)}, u32[]{:S(2)}, u32[]{:S(2)}) collective-permute-start(bf16[2,128,128]{2,1,0:T(8,128)(2,1)S(1)} %pad_maximum_fusion.r0_ref), channel_id=1, source_target_pairs={{0,2},{1,3},{2,0},{3,1},{4,6},{5,7},{6,4},{7,5},{8,10},{9,11},{10,... | collective-permute-start | bytes 196616 | tf_op jit(solution)/shard_map/ppermute | solution.py:355
  13.5 12.7 %collective-permute-start.4 = (bf16[2,128,128]{2,1,0:T(8,128)(2,1)S(1)}, bf16[2,128,128]{2,1,0:T(8,128)(2,1)S(1)}, u32[]{:S(2)}, u32[]{:S(2)}) collective-permute-start(bf16[2,128,128]{2,1,0:T(8,128)(2,1)S(1)} %pad_maximum_fusion.r0_ref), channel_id=1, source_target_pairs={{0,1},{1,0},{2,3},{3,2},{4,5},{5,4},{6,7},{7,6},{8,9},{9,8},{10,11... | collective-permute-start | bytes 196616 | tf_op jit(solution)/shard_map/ppermute | solution.py:355
  27.4 14.4 %collective-permute-start.7 = (f32[2048,128]{1,0:T(8,128)S(1)}, f32[2048,128]{1,0:T(8,128)S(1)}, u32[]{:S(2)}, u32[]{:S(2)}) collective-permute-start(f32[2048,128]{1,0:T(8,128)S(1)} %shard_map.96), channel_id=1, source_target_pairs={{0,8},{8,0},{16,24},{24,16},{32,40},{40,32},{48,56},{56,48},{64,72... | collective-permute-start | bytes 3145736 | tf_op jit(solution)/shard_map/ppermute | solution.py:349
  27.5 13.3 %collective-permute-start.10 = (bf16[4,172,128]{2,1,0:T(8,128)(2,1)S(1)}, bf16[4,172,128]{2,1,0:T(8,128)(2,1)S(1)}, u32[]{:S(2)}, u32[]{:S(2)}) collective-permute-start(bf16[4,172,128]{2,1,0:T(8,128)(2,1)S(1)} %copy-done), channel_id=1, source_target_pairs={{0,192},{8,200},{16,208},{24,216},{32,224},{40,232},{48,240},{56,2... | collective-permute-start | bytes 528392 | tf_op jit(solution)/shard_map/ppermute | solution.py:349
  31.9 9.0 %collective-permute-start.9 = (bf16[4,172,128]{2,1,0:T(8,128)(2,1)S(1)}, bf16[4,172,128]{2,1,0:T(8,128)(2,1)S(1)}, u32[]{:S(2)}, u32[]{:S(2)}) collective-permute-start(bf16[4,172,128]{2,1,0:T(8,128)(2,1)S(1)} %copy-done), channel_id=1, source_target_pairs={{0,128},{8,136},{16,144},{24,152},{32,160},{40,168},{48,176},{56,1... | collective-permute-start | bytes 528392 | tf_op jit(solution)/shard_map/ppermute | solution.py:349
  33.8 8.0 %collective-permute-start.8 = (bf16[4,172,128]{2,1,0:T(8,128)(2,1)S(1)}, bf16[4,172,128]{2,1,0:T(8,128)(2,1)S(1)}, u32[]{:S(2)}, u32[]{:S(2)}) collective-permute-start(bf16[4,172,128]{2,1,0:T(8,128)(2,1)S(1)} %copy-done), channel_id=1, source_target_pairs={{0,64},{8,72},{16,80},{24,88},{32,96},{40,104},{48,112},{56,120},{... | collective-permute-start | bytes 528392 | tf_op jit(solution)/shard_map/ppermute | solution.py:349
  42.2 32.6 %collective-permute-start.21 = (bf16[16,172,128]{2,0,1:T(8,128)(2,1)S(1)}, bf16[16,172,128]{2,0,1:T(8,128)(2,1)S(1)}, u32[]{:S(2)}, u32[]{:S(2)}) collective-permute-start(bf16[16,172,128]{2,0,1:T(8,128)(2,1)S(1)} %copy.10), channel_id=1, source_target_pairs={{0,8},{8,0},{16,24},{24,16},{32,40},{40,32},{48,56},{56,48},{64,72... | collective-permute-start | bytes 2113544 | tf_op jit(solution)/shard_map/ppermute | solution.py:349
  42.3 6.9 %collective-permute-start.11 = (bf16[512,128]{1,0:T(8,128)(2,1)S(1)}, bf16[512,128]{1,0:T(8,128)(2,1)S(1)}, u32[]{:S(2)}, u32[]{:S(2)}) collective-permute-start(bf16[512,128]{1,0:T(8,128)(2,1)S(1)} %get-tuple-element.31), channel_id=1, source_target_pairs={{0,64},{8,72},{16,80},{24,88},{32,96},{40,104},{48,112},{56,120},{... | collective-permute-start | bytes 393224 | tf_op jit(solution)/shard_map/ppermute | solution.py:349
  44.8 8.3 %collective-permute-start.12 = (bf16[512,128]{1,0:T(8,128)(2,1)S(1)}, bf16[512,128]{1,0:T(8,128)(2,1)S(1)}, u32[]{:S(2)}, u32[]{:S(2)}) collective-permute-start(bf16[512,128]{1,0:T(8,128)(2,1)S(1)} %get-tuple-element.32), channel_id=1, source_target_pairs={{0,128},{8,136},{16,144},{24,152},{32,160},{40,168},{48,176},{56,1... | collective-permute-start | bytes 393224 | tf_op jit(solution)/shard_map/ppermute | solution.py:349
  46.4 9.1 %collective-permute-start.13 = (bf16[512,128]{1,0:T(8,128)(2,1)S(1)}, bf16[512,128]{1,0:T(8,128)(2,1)S(1)}, u32[]{:S(2)}, u32[]{:S(2)}) collective-permute-start(bf16[512,128]{1,0:T(8,128)(2,1)S(1)} %get-tuple-element.33), channel_id=1, source_target_pairs={{0,192},{8,200},{16,208},{24,216},{32,224},{40,232},{48,240},{56,2... | collective-permute-start | bytes 393224 | tf_op jit(solution)/shard_map/ppermute | solution.py:349
  62.7 7.9 %collective-permute-start.17 = (bf16[128,128]{1,0:T(8,128)(2,1)S(1)}, bf16[128,128]{1,0:T(8,128)(2,1)S(1)}, u32[]{:S(2)}, u32[]{:S(2)}) collective-permute-start(bf16[128,128]{1,0:T(8,128)(2,1)S(1)} %shard_map.99), channel_id=1, source_target_pairs={{0,4},{1,5},{2,6},{3,7},{4,0},{5,1},{6,2},{7,3},{8,12},{9,13},{10,... | collective-permute-start | bytes 98312 | tf_op jit(solution)/shard_map/ppermute | solution.py:353
  70.6 6.3 %collective-permute-start.20 = (bf16[2,128,128]{2,1,0:T(8,128)(2,1)S(1)}, bf16[2,128,128]{2,1,0:T(8,128)(2,1)S(1)}, u32[]{:S(2)}, u32[]{:S(2)}) collective-permute-start(bf16[2,128,128]{2,1,0:T(8,128)(2,1)S(1)} %pad_maximum_fusion.1.a0_ref), channel_id=1, source_target_pairs={{0,3},{1,2},{2,1},{3,0},{4,7},{5,6},{6,5},{7,4},{8,11},{9,10},{10,... | collective-permute-start | bytes 196616 | tf_op jit(solution)/shard_map/ppermute | solution.py:355
  73.8 5.8 %collective-permute-start.19 = (bf16[2,128,128]{2,1,0:T(8,128)(2,1)S(1)}, bf16[2,128,128]{2,1,0:T(8,128)(2,1)S(1)}, u32[]{:S(2)}, u32[]{:S(2)}) collective-permute-start(bf16[2,128,128]{2,1,0:T(8,128)(2,1)S(1)} %pad_maximum_fusion.1.a0_ref), channel_id=1, source_target_pairs={{0,2},{1,3},{2,0},{3,1},{4,6},{5,7},{6,4},{7,5},{8,10},{9,11},{10,... | collective-permute-start | bytes 196616 | tf_op jit(solution)/shard_map/ppermute | solution.py:355
  85.0 8.4 %collective-permute-start.23 = (bf16[864,128]{1,0:T(8,128)(2,1)S(1)}, bf16[864,128]{1,0:T(8,128)(2,1)S(1)}, u32[]{:S(2)}, u32[]{:S(2)}) collective-permute-start(bf16[864,128]{1,0:T(8,128)(2,1)S(1)} %get-tuple-element.42), channel_id=1, source_target_pairs={{0,64},{8,72},{16,80},{24,88},{32,96},{40,104},{48,112},{56,120},{... | collective-permute-start | bytes 663560 | tf_op jit(solution)/shard_map/ppermute | solution.py:349
  85.1 12.3 %collective-permute-start.24 = (bf16[864,128]{1,0:T(8,128)(2,1)S(1)}, bf16[864,128]{1,0:T(8,128)(2,1)S(1)}, u32[]{:S(2)}, u32[]{:S(2)}) collective-permute-start(bf16[864,128]{1,0:T(8,128)(2,1)S(1)} %get-tuple-element.43), channel_id=1, source_target_pairs={{0,128},{8,136},{16,144},{24,152},{32,160},{40,168},{48,176},{56,1... | collective-permute-start | bytes 663560 | tf_op jit(solution)/shard_map/ppermute | solution.py:349
  87.1 12.9 %collective-permute-start.25 = (bf16[864,128]{1,0:T(8,128)(2,1)S(1)}, bf16[864,128]{1,0:T(8,128)(2,1)S(1)}, u32[]{:S(2)}, u32[]{:S(2)}) collective-permute-start(bf16[864,128]{1,0:T(8,128)(2,1)S(1)} %get-tuple-element.44), channel_id=1, source_target_pairs={{0,192},{8,200},{16,208},{24,216},{32,224},{40,232},{48,240},{56,2... | collective-permute-start | bytes 663560 | tf_op jit(solution)/shard_map/ppermute | solution.py:349
  100.1 5.6 %collective-permute-start.26 = (bf16[336,128]{1,0:T(8,128)(2,1)S(1)}, bf16[336,128]{1,0:T(8,128)(2,1)S(1)}, u32[]{:S(2)}, u32[]{:S(2)}) collective-permute-start(bf16[336,128]{1,0:T(8,128)(2,1)S(1)} %get-tuple-element.46), channel_id=1, source_target_pairs={{0,16},{8,24},{16,0},{24,8},{32,48},{40,56},{48,32},{56,40},{64,80... | collective-permute-start | bytes 258056 | tf_op jit(solution)/shard_map/ppermute | solution.py:349
  102.9 8.1 %collective-permute-start.28 = (bf16[336,128]{1,0:T(8,128)(2,1)S(1)}, bf16[336,128]{1,0:T(8,128)(2,1)S(1)}, u32[]{:S(2)}, u32[]{:S(2)}) collective-permute-start(bf16[336,128]{1,0:T(8,128)(2,1)S(1)} %get-tuple-element.48), channel_id=1, source_target_pairs={{0,48},{8,56},{16,32},{24,40},{32,16},{40,24},{48,0},{56,8},{64,11... | collective-permute-start | bytes 258056 | tf_op jit(solution)/shard_map/ppermute | solution.py:349
  132.3 6.6 %collective-permute-start.31 = (f32[160,128]{1,0:T(8,128)S(1)}, f32[160,128]{1,0:T(8,128)S(1)}, u32[]{:S(2)}, u32[]{:S(2)}) collective-permute-start(f32[160,128]{1,0:T(8,128)S(1)} %shard_map.106.own_ref), channel_id=1, source_target_pairs={{0,192},{8,200},{16,208},{24,216},{32,224},{40,232},{48,240},{56,2... | collective-permute-start | bytes 245768 | tf_op jit(solution)/shard_map/ppermute | solution.py:349
  135.4 5.9 %collective-permute-start.30 = (f32[160,128]{1,0:T(8,128)S(1)}, f32[160,128]{1,0:T(8,128)S(1)}, u32[]{:S(2)}, u32[]{:S(2)}) collective-permute-start(f32[160,128]{1,0:T(8,128)S(1)} %shard_map.106.own_ref), channel_id=1, source_target_pairs={{0,128},{8,136},{16,144},{24,152},{32,160},{40,168},{48,176},{56,1... | collective-permute-start | bytes 245768 | tf_op jit(solution)/shard_map/ppermute | solution.py:349
  135.4 5.9 %collective-permute-start.29 = (f32[160,128]{1,0:T(8,128)S(1)}, f32[160,128]{1,0:T(8,128)S(1)}, u32[]{:S(2)}, u32[]{:S(2)}) collective-permute-start(f32[160,128]{1,0:T(8,128)S(1)} %shard_map.106.own_ref), channel_id=1, source_target_pairs={{0,64},{8,72},{16,80},{24,88},{32,96},{40,104},{48,112},{56,120},{... | collective-permute-start | bytes 245768 | tf_op jit(solution)/shard_map/ppermute | solution.py:349
  (14 other events, 53.6 us)

commit v3 on v2

--- a/solution.py
+++ b/solution.py
@@ -216,43 +216,43 @@
     )[0]
 
 
-def core_sum_body(
-    mine_ref, got_ref, g0_ref, g1_ref, g2_ref, g3_ref, s1_ref, s2_ref, s3_ref, keep_ref, near_ref
-):
+def core_sum_body(mine_ref, got_ref, s1_ref, s2_ref, s3_ref, keep_ref):
     n = keep_ref.shape[0]
     for d, ref in ((1, s1_ref), (2, s2_ref), (3, s3_ref), (0, keep_ref)):
         at = slice(d * n, (d + 1) * n)
-        ref[...] = (mine_ref[at, :].astype(F32) + got_ref[at, :].astype(F32)).astype(ref.dtype)
-    for d, ref in enumerate((g0_ref, g1_ref, g2_ref, g3_ref)):
-        near_ref[4 * d : 4 * d + 4] = ref[...]
-
-
-def core_sum(mine, got, cotangents):
-    rows = mine.shape[0] // 4
-    shape = (rows, BS)
-    near = (16,) + cotangents[0].shape[1:]
-    return call(
-        core_sum_body,
-        [(shape, BF16)] * 3 + [(shape, F32), (near, BF16)],
-        (mine, got, *cotangents),
-    )
+        ref[...] = (mine_ref[at, :] + got_ref[at, :]).astype(ref.dtype)
+
+
+def core_sum(mine, got):
+    shape = (mine.shape[0] // 4, BS)
+    return call(core_sum_body, [(shape, BF16)] * 3 + [(shape, F32)], (mine, got))
 
 
 def four(a, b, c, d):
     return (a.astype(F32) + b.astype(F32)) + (c.astype(F32) + d.astype(F32))
 
 
-def x_sum_body(keep_ref, r1_ref, r2_ref, r3_ref, s1_ref, s2_ref, s3_ref, out_ref):
+def x_sum_body(
+    keep_ref, r1_ref, r2_ref, r3_ref, g0_ref, g1_ref, g2_ref, g3_ref,
+    s1_ref, s2_ref, s3_ref, out_ref, grad_ref,
+):
     n = out_ref.shape[0]
     for d, ref in ((1, s1_ref), (2, s2_ref), (3, s3_ref), (0, out_ref)):
         at = slice(d * n, (d + 1) * n)
         total = four(keep_ref[at, :], r1_ref[at, :], r2_ref[at, :], r3_ref[at, :])
         ref[...] = total.astype(ref.dtype)
-
-
-def x_sum(keep, received):
+    for d, ref in enumerate((g0_ref, g1_ref, g2_ref, g3_ref)):
+        grad_ref[4 * d : 4 * d + 4] = ref[...]
+
+
+def x_sum(keep, received, cotangents):
     shape = (keep.shape[0] // 4, BS)
-    return call(x_sum_body, [(shape, BF16)] * 3 + [(shape, F32)], (keep, *received))
+    gathered = (16,) + cotangents[0].shape[1:]
+    return call(
+        x_sum_body,
+        [(shape, BF16)] * 3 + [(shape, F32), (gathered, BF16)],
+        (keep, *received, *cotangents),
+    )
 
 
 def core_sum_grad_body(mine_ref, far_ref, got_ref, s1_ref, s2_ref, s3_ref, keep_ref):
@@ -369,14 +369,14 @@
     grad_t = logit_grad.T
     cotangents = [grad_t] + [permute(grad_t, f) for f in Z_FLIPS]
     dense, grad_z = densify(me, side, block_counts, block_slots, block_values, cotangents)
-    grad_x = [grad_z] + [permute(grad_z, f) for f in X_FLIPS]
-
     far = rows_product(dense, parts, 1, F32)
     got = permute(far, CORE)
     mine = rows_product(dense, parts, 0, F32)
-    s1, s2, s3, keep, grad_near = core_sum(mine, got, grad_x)
+    s1, s2, s3, keep = core_sum(mine, got)
+    received = [permute(s, f) for s, f in zip((s1, s2, s3), X_FLIPS)]
+    grad_x = [grad_z] + [permute(grad_z, f) for f in X_FLIPS]
+    s1, s2, s3, keep, grad_near = x_sum(keep, received, grad_x)
     grad_far = permute(grad_near, CORE)
-    s1, s2, s3, keep = x_sum(keep, [permute(s, f) for s, f in zip((s1, s2, s3), X_FLIPS)])
     received = [permute(s, f) for s, f in zip((s1, s2, s3), Z_FLIPS)]
     q = class_columns(grad_near, grad_far, dense)
     agg = gather_col(aggregate(keep, received))

time: 142 us -> 141 us (level)
  waiting for transfers between devices: 52.1 us -> 46.4 us
  starting transfers between devices: 51.4 us -> 54.8 us
    ppermute x24, waiting for transfers between devices: 44.2 us -> 39.5 us  [permute(): return lax.ppermute(x, 'row', [(i, i ^ flip) for i in range(32)])]
    ppermute x2, starting transfers between devices: 10.4 us -> 12.7 us  [gather_col(): far = lax.ppermute(x, 'col', [(i, i ^ 4) for i in range(8)])]
    ppermute x2, waiting for transfers between devices: 5.01 us -> 3.34 us  [gather_col(): far = lax.ppermute(x, 'col', [(i, i ^ 4) for i in range(8)])]
    ppermute x6, starting transfers between devices: 8.29 us -> 9.79 us  [gather_col(): lax.ppermute(pair, 'col', [(i, i ^ d) for i in range(8)])]
  transfers between devices with their start and end apart: 32 -> 32, of which waited for: 23 -> 21; matrix products, arithmetic and copies ran while one was open for 1% -> 1% of each run, Pallas kernels for 6% -> 7%
where the time goes in v3:
time: 141 us
  starting transfers between devices  54.8 us (39%)
  waiting for transfers between devices  46.4 us (33%)
  blocking collectives  20.5 us (15%)
  Pallas kernels  15.7 us (11%)
  between operations  1.51 us (1%)
    ppermute x24, waiting for transfers between devices, permute(): return lax.ppermute(x, 'row', [(i, i ^ flip) for i in range(32)])  39.5 us
    ppermute x24, starting transfers between devices, permute(): return lax.ppermute(x, 'row', [(i, i ^ flip) for i in range(32)])  32.3 us
    all_to_all x1, blocking collectives, on_device(): own = share_sum(lax.all_to_all(shares, 'col', 0, 0))  20.5 us
    ppermute x2, starting transfers between devices, gather_col(): far = lax.ppermute(x, 'col', [(i, i ^ 4) for i in range(8)])  12.7 us
    pallas_call x13, Pallas kernels, call(): pl.pallas_call(body, out_shape=[o if len(o) == 1 else jax.ShapeDtypeStruc...  10.3 us
    ppermute x6, starting transfers between devices, gather_col(): lax.ppermute(pair, 'col', [(i, i ^ d) for i in range(8)])  9.79 us
    pallas_call x1, Pallas kernels, densify(): pl.pallas_call(densify_body, out_shape=[pltpu.VMEM((4096, 1024), BF16), j...  5.37 us
    ppermute x6, waiting for transfers between devices, gather_col(): lax.ppermute(pair, 'col', [(i, i ^ d) for i in range(8)])  3.58 us
  transfers between devices with their start and end apart: 32, of which 21 were waited for; matrix products, arithmetic and copies ran while one was open for 1% of the time, Pallas kernels for 7%

profile of v3, /device:TPU:32, one launch (start us, length us, event | category | flops | bytes accessed | tf_op | source)
XLA Modules:
  0.0 140.6 jit_solution(3079939748780793169)
XLA Ops:
  0.6 6.4 %collective-permute-start.3 = (bf16[128,128]{1,0:T(8,128)(2,1)}, bf16[128,128]{1,0:T(8,128)(2,1)S(1)}, u32[]{:S(2)}, u32[]{:S(2)}) collective-permute-start(bf16[128,128]{1,0:T(8,128)(2,1)} %param.7), channel_id=1, source_target_pairs={{0,4},{1,5},{2,6},{3,7},{4,0},{5,1},{6,2},{7,3},{8,12},{9,13},{10,... | collective-permute-start | bytes 98312 | tf_op jit(solution)/shard_map/ppermute | solution.py:353
  11.8 2.9 %collective-permute-start.5 = (bf16[2,128,128]{2,1,0:T(8,128)(2,1)S(1)}, bf16[2,128,128]{2,1,0:T(8,128)(2,1)S(1)}, u32[]{:S(2)}, u32[]{:S(2)}) collective-permute-start(bf16[2,128,128]{2,1,0:T(8,128)(2,1)S(1)} %pad_maximum_fusion.r0_ref), channel_id=1, source_target_pairs={{0,2},{1,3},{2,0},{3,1},{4,6},{5,7},{6,4},{7,5},{8,10},{9,11},{10,... | collective-permute-start | bytes 196616 | tf_op jit(solution)/shard_map/ppermute | solution.py:355
  14.9 2.6 %collective-permute-start.1 = (bf16[172,128]{1,0:T(8,128)(2,1)}, bf16[172,128]{1,0:T(8,128)(2,1)S(1)}, u32[]{:S(2)}, u32[]{:S(2)}) collective-permute-start(bf16[172,128]{1,0:T(8,128)(2,1)} %bitcast.13), channel_id=1, source_target_pairs={{0,32},{8,40},{16,48},{24,56},{32,0},{40,8},{48,16},{56,24},{64,96... | collective-permute-start | bytes 132104 | tf_op jit(solution)/shard_map/ppermute | solution.py:349
  22.4 5.4 %shard_map.94 = (bf16[4096,1024]{1,0:T(8,128)(2,1)S(1)}, bf16[4,172,128]{2,1,0:T(8,128)(2,1)}) custom-call(s32[1]{0:T(128)} %bitcast.me_ref, s32[1]{0:T(128)} %bitcast.1.side_ref, s32[1]{0:T(128)S(6)} %copy.12.count_ref, s32[144]{0:T(256)} %slot_ref.1, bf16[144,128,128]{2,1,0:T(8,128)(2,1)} %block_ref.1, bf16[172,128]{1,0:T(8,128)(2,1)} %bitcast.15, ...), custom_call_target="tpu_custom_call" | custom-call | tf_op jit(solution)/shard_map/pallas_call | solution.py:91
  30.9 4.2 %collective-permute-start.12 = (bf16[4,172,128]{2,1,0:T(8,128)(2,1)S(1)}, bf16[4,172,128]{2,1,0:T(8,128)(2,1)S(1)}, u32[]{:S(2)}, u32[]{:S(2)}) collective-permute-start(bf16[4,172,128]{2,1,0:T(8,128)(2,1)S(1)} %copy-done), channel_id=1, source_target_pairs={{0,128},{8,136},{16,144},{24,152},{32,160},{40,168},{48,176},{56,1... | collective-permute-start | bytes 528392 | tf_op jit(solution)/shard_map/ppermute | solution.py:349
  36.4 3.3 %collective-permute-start.10 = (bf16[512,128]{1,0:T(8,128)(2,1)S(1)}, bf16[512,128]{1,0:T(8,128)(2,1)S(1)}, u32[]{:S(2)}, u32[]{:S(2)}) collective-permute-start(bf16[512,128]{1,0:T(8,128)(2,1)S(1)} %get-tuple-element.32), channel_id=1, source_target_pairs={{0,192},{8,200},{16,208},{24,216},{32,224},{40,232},{48,240},{56,2... | collective-permute-start | bytes 393224 | tf_op jit(solution)/shard_map/ppermute | solution.py:349
  41.3 3.0 %collective-permute-done.12.g2_ref = bf16[4,172,128]{2,1,0:T(8,128)(2,1)S(1)} collective-permute-done((bf16[4,172,128]{2,1,0:T(8,128)(2,1)S(1)}, bf16[4,172,128]{2,1,0:T(8,128)(2,1)S(1)}, u32[]{:S(2)}, u32[]{:S(2)}) %collective-permute-start.12) | collective-permute-done | bytes 176160 | tf_op jit(solution)/shard_map/ppermute | solution.py:349
  44.3 5.9 %collective-permute-done.13.g3_ref = bf16[4,172,128]{2,1,0:T(8,128)(2,1)S(1)} collective-permute-done((bf16[4,172,128]{2,1,0:T(8,128)(2,1)S(1)}, bf16[4,172,128]{2,1,0:T(8,128)(2,1)S(1)}, u32[]{:S(2)}, u32[]{:S(2)}) %collective-permute-start.13) | collective-permute-done | bytes 176160 | tf_op jit(solution)/shard_map/ppermute | solution.py:349
  50.2 1.9 %collective-permute-done.10.r3_ref = bf16[512,128]{1,0:T(8,128)(2,1)S(1)} collective-permute-done((bf16[512,128]{1,0:T(8,128)(2,1)S(1)}, bf16[512,128]{1,0:T(8,128)(2,1)S(1)}, u32[]{:S(2)}, u32[]{:S(2)}) %collective-permute-start.10) | collective-permute-done | bytes 131104 | tf_op jit(solution)/shard_map/ppermute | solution.py:349
  53.3 2.8 %collective-permute-start.16 = (bf16[128,128]{1,0:T(8,128)(2,1)S(1)}, bf16[128,128]{1,0:T(8,128)(2,1)S(1)}, u32[]{:S(2)}, u32[]{:S(2)}) collective-permute-start(bf16[128,128]{1,0:T(8,128)(2,1)S(1)} %get-tuple-element.37), channel_id=1, source_target_pairs={{0,48},{8,56},{16,32},{24,40},{32,16},{40,24},{48,0},{56,8},{64,11... | collective-permute-start | bytes 98312 | tf_op jit(solution)/shard_map/ppermute | solution.py:349
  58.9 6.3 %collective-permute-start.17 = (bf16[128,128]{1,0:T(8,128)(2,1)S(1)}, bf16[128,128]{1,0:T(8,128)(2,1)S(1)}, u32[]{:S(2)}, u32[]{:S(2)}) collective-permute-start(bf16[128,128]{1,0:T(8,128)(2,1)S(1)} %shard_map.99), channel_id=1, source_target_pairs={{0,4},{1,5},{2,6},{3,7},{4,0},{5,1},{6,2},{7,3},{8,12},{9,13},{10,... | collective-permute-start | bytes 98312 | tf_op jit(solution)/shard_map/ppermute | solution.py:353
  67.6 4.7 %collective-permute-start.19 = (bf16[2,128,128]{2,1,0:T(8,128)(2,1)S(1)}, bf16[2,128,128]{2,1,0:T(8,128)(2,1)S(1)}, u32[]{:S(2)}, u32[]{:S(2)}) collective-permute-start(bf16[2,128,128]{2,1,0:T(8,128)(2,1)S(1)} %pad_maximum_fusion.1.a0_ref), channel_id=1, source_target_pairs={{0,2},{1,3},{2,0},{3,1},{4,6},{5,7},{6,4},{7,5},{8,10},{9,11},{10,... | collective-permute-start | bytes 196616 | tf_op jit(solution)/shard_map/ppermute | solution.py:355
  75.2 2.5 %collective-permute-done.20.a3_ref = bf16[2,128,128]{2,1,0:T(8,128)(2,1)S(1)} collective-permute-done((bf16[2,128,128]{2,1,0:T(8,128)(2,1)S(1)}, bf16[2,128,128]{2,1,0:T(8,128)(2,1)S(1)}, u32[]{:S(2)}, u32[]{:S(2)}) %collective-permute-start.20) | collective-permute-done | bytes 65568 | tf_op jit(solution)/shard_map/ppermute | solution.py:355
  77.8 2.7 %shard_map.101 = (bf16[176,1024]{1,0:T(8,128)(2,1)S(1)}, bf16[3456,128]{1,0:T(8,128)(2,1)S(1)}) custom-call(bf16[2,128,128]{2,1,0:T(8,128)(2,1)S(1)} %pad_maximum_fusion.1.a0_ref, bf16[2,128,128]{2,1,0:T(8,128)(2,1)S(1)} %collective-permute-done.18.a1_ref, bf16[2,128,128]{2,1,0:T(8,128)(2,1)S(1)} %collective-permute-done.19.a2_ref, ...), custom_call_target="tpu_custom_call" | custom-call | flops 2147483648 | bytes 1048576 | tf_op jit(solution)/shard_map/pallas_call | solution.py:36
  84.8 3.2 %collective-permute-start.25 = (bf16[864,128]{1,0:T(8,128)(2,1)S(1)}, bf16[864,128]{1,0:T(8,128)(2,1)S(1)}, u32[]{:S(2)}, u32[]{:S(2)}) collective-permute-start(bf16[864,128]{1,0:T(8,128)(2,1)S(1)} %get-tuple-element.44), channel_id=1, source_target_pairs={{0,192},{8,200},{16,208},{24,216},{32,224},{40,232},{48,240},{56,2... | collective-permute-start | bytes 663560 | tf_op jit(solution)/shard_map/ppermute | solution.py:349
  88.0 3.6 %collective-permute-done.23.r1_ref = bf16[864,128]{1,0:T(8,128)(2,1)S(1)} collective-permute-done((bf16[864,128]{1,0:T(8,128)(2,1)S(1)}, bf16[864,128]{1,0:T(8,128)(2,1)S(1)}, u32[]{:S(2)}, u32[]{:S(2)}) %collective-permute-start.23) | collective-permute-done | bytes 221216 | tf_op jit(solution)/shard_map/ppermute | solution.py:349
  91.5 3.6 %collective-permute-done.24.r2_ref = bf16[864,128]{1,0:T(8,128)(2,1)S(1)} collective-permute-done((bf16[864,128]{1,0:T(8,128)(2,1)S(1)}, bf16[864,128]{1,0:T(8,128)(2,1)S(1)}, u32[]{:S(2)}, u32[]{:S(2)}) %collective-permute-start.24) | collective-permute-done | bytes 221216 | tf_op jit(solution)/shard_map/ppermute | solution.py:349
  95.1 2.8 %collective-permute-done.25.r3_ref = bf16[864,128]{1,0:T(8,128)(2,1)S(1)} collective-permute-done((bf16[864,128]{1,0:T(8,128)(2,1)S(1)}, bf16[864,128]{1,0:T(8,128)(2,1)S(1)}, u32[]{:S(2)}, u32[]{:S(2)}) %collective-permute-start.25) | collective-permute-done | bytes 221216 | tf_op jit(solution)/shard_map/ppermute | solution.py:349
  98.0 2.4 %collective-permute-start.26 = (bf16[336,128]{1,0:T(8,128)(2,1)S(1)}, bf16[336,128]{1,0:T(8,128)(2,1)S(1)}, u32[]{:S(2)}, u32[]{:S(2)}) collective-permute-start(bf16[336,128]{1,0:T(8,128)(2,1)S(1)} %get-tuple-element.46), channel_id=1, source_target_pairs={{0,16},{8,24},{16,0},{24,8},{32,48},{40,56},{48,32},{56,40},{64,80... | collective-permute-start | bytes 258056 | tf_op jit(solution)/shard_map/ppermute | solution.py:349
  102.8 4.3 %collective-permute-done.27.r2_ref = bf16[336,128]{1,0:T(8,128)(2,1)S(1)} collective-permute-done((bf16[336,128]{1,0:T(8,128)(2,1)S(1)}, bf16[336,128]{1,0:T(8,128)(2,1)S(1)}, u32[]{:S(2)}, u32[]{:S(2)}) %collective-permute-start.27) | collective-permute-done | bytes 86048 | tf_op jit(solution)/shard_map/ppermute | solution.py:349
  109.7 20.5 %all_to_all.5.parts_ref = bf16[8,160,128]{2,1,0:T(8,128)(2,1)S(1)} all-to-all(bf16[8,160,128]{2,1,0:T(8,128)(2,1)S(1)} %get-tuple-element.50), channel_id=1, replica_groups=mesh['row'=32,'col'=8] {'col'}, dimensions={0} | all-to-all | bytes 655360 | tf_op jit(solution)/shard_map/all_to_all | solution.py:391
  130.3 3.9 %collective-permute-start.30 = (f32[160,128]{1,0:T(8,128)S(1)}, f32[160,128]{1,0:T(8,128)S(1)}, u32[]{:S(2)}, u32[]{:S(2)}) collective-permute-start(f32[160,128]{1,0:T(8,128)S(1)} %shard_map.106.own_ref), channel_id=1, source_target_pairs={{0,128},{8,136},{16,144},{24,152},{32,160},{40,168},{48,176},{56,1... | collective-permute-start | bytes 245768 | tf_op jit(solution)/shard_map/ppermute | solution.py:349
  135.0 2.5 %collective-permute-done.30.r2_ref = f32[160,128]{1,0:T(8,128)S(1)} collective-permute-done((f32[160,128]{1,0:T(8,128)S(1)}, f32[160,128]{1,0:T(8,128)S(1)}, u32[]{:S(2)}, u32[]{:S(2)}) %collective-permute-start.30) | collective-permute-done | bytes 81952 | tf_op jit(solution)/shard_map/ppermute | solution.py:349
  137.5 2.4 %collective-permute-done.31.r3_ref = f32[160,128]{1,0:T(8,128)S(1)} collective-permute-done((f32[160,128]{1,0:T(8,128)S(1)}, f32[160,128]{1,0:T(8,128)S(1)}, u32[]{:S(2)}, u32[]{:S(2)}) %collective-permute-start.31) | collective-permute-done | bytes 81952 | tf_op jit(solution)/shard_map/ppermute | solution.py:349
  (71 shorter events, 35.5 us)
Async XLA Ops:
  0.6 8.8 %collective-permute-start.3 = (bf16[128,128]{1,0:T(8,128)(2,1)}, bf16[128,128]{1,0:T(8,128)(2,1)S(1)}, u32[]{:S(2)}, u32[]{:S(2)}) collective-permute-start(bf16[128,128]{1,0:T(8,128)(2,1)} %param.7), channel_id=1, source_target_pairs={{0,4},{1,5},{2,6},{3,7},{4,0},{5,1},{6,2},{7,3},{8,12},{9,13},{10,... | collective-permute-start | bytes 98312 | tf_op jit(solution)/shard_map/ppermute | solution.py:353
  7.0 10.5 %collective-permute-start = (bf16[172,128]{1,0:T(8,128)(2,1)}, bf16[172,128]{1,0:T(8,128)(2,1)S(1)}, u32[]{:S(2)}, u32[]{:S(2)}) collective-permute-start(bf16[172,128]{1,0:T(8,128)(2,1)} %bitcast.12), channel_id=1, source_target_pairs={{0,16},{8,24},{16,0},{24,8},{32,48},{40,56},{48,32},{56,40},{64,80... | collective-permute-start | bytes 132104 | tf_op jit(solution)/shard_map/ppermute | solution.py:349
  10.2 17.5 %collective-permute-start.4 = (bf16[2,128,128]{2,1,0:T(8,128)(2,1)S(1)}, bf16[2,128,128]{2,1,0:T(8,128)(2,1)S(1)}, u32[]{:S(2)}, u32[]{:S(2)}) collective-permute-start(bf16[2,128,128]{2,1,0:T(8,128)(2,1)S(1)} %pad_maximum_fusion.r0_ref), channel_id=1, source_target_pairs={{0,1},{1,0},{2,3},{3,2},{4,5},{5,4},{6,7},{7,6},{8,9},{9,8},{10,11... | collective-permute-start | bytes 196616 | tf_op jit(solution)/shard_map/ppermute | solution.py:355
  11.8 15.9 %collective-permute-start.5 = (bf16[2,128,128]{2,1,0:T(8,128)(2,1)S(1)}, bf16[2,128,128]{2,1,0:T(8,128)(2,1)S(1)}, u32[]{:S(2)}, u32[]{:S(2)}) collective-permute-start(bf16[2,128,128]{2,1,0:T(8,128)(2,1)S(1)} %pad_maximum_fusion.r0_ref), channel_id=1, source_target_pairs={{0,2},{1,3},{2,0},{3,1},{4,6},{5,7},{6,4},{7,5},{8,10},{9,11},{10,... | collective-permute-start | bytes 196616 | tf_op jit(solution)/shard_map/ppermute | solution.py:355
  14.7 13.1 %collective-permute-start.6 = (bf16[2,128,128]{2,1,0:T(8,128)(2,1)S(1)}, bf16[2,128,128]{2,1,0:T(8,128)(2,1)S(1)}, u32[]{:S(2)}, u32[]{:S(2)}) collective-permute-start(bf16[2,128,128]{2,1,0:T(8,128)(2,1)S(1)} %pad_maximum_fusion.r0_ref), channel_id=1, source_target_pairs={{0,3},{1,2},{2,1},{3,0},{4,7},{5,6},{6,5},{7,4},{8,11},{9,10},{10,... | collective-permute-start | bytes 196616 | tf_op jit(solution)/shard_map/ppermute | solution.py:355
  29.0 7.3 %collective-permute-start.7 = (f32[2048,128]{1,0:T(8,128)S(1)}, f32[2048,128]{1,0:T(8,128)S(1)}, u32[]{:S(2)}, u32[]{:S(2)}) collective-permute-start(f32[2048,128]{1,0:T(8,128)S(1)} %shard_map.96), channel_id=1, source_target_pairs={{0,8},{8,0},{16,24},{24,16},{32,40},{40,32},{48,56},{56,48},{64,72... | collective-permute-start | bytes 3145736 | tf_op jit(solution)/shard_map/ppermute | solution.py:349
  29.1 10.6 %collective-permute-start.11 = (bf16[4,172,128]{2,1,0:T(8,128)(2,1)S(1)}, bf16[4,172,128]{2,1,0:T(8,128)(2,1)S(1)}, u32[]{:S(2)}, u32[]{:S(2)}) collective-permute-start(bf16[4,172,128]{2,1,0:T(8,128)(2,1)S(1)} %copy-done), channel_id=1, source_target_pairs={{0,64},{8,72},{16,80},{24,88},{32,96},{40,104},{48,112},{56,120},{... | collective-permute-start | bytes 528392 | tf_op jit(solution)/shard_map/ppermute | solution.py:349
  30.9 13.4 %collective-permute-start.12 = (bf16[4,172,128]{2,1,0:T(8,128)(2,1)S(1)}, bf16[4,172,128]{2,1,0:T(8,128)(2,1)S(1)}, u32[]{:S(2)}, u32[]{:S(2)}) collective-permute-start(bf16[4,172,128]{2,1,0:T(8,128)(2,1)S(1)} %copy-done), channel_id=1, source_target_pairs={{0,128},{8,136},{16,144},{24,152},{32,160},{40,168},{48,176},{56,1... | collective-permute-start | bytes 528392 | tf_op jit(solution)/shard_map/ppermute | solution.py:349
  35.1 15.1 %collective-permute-start.13 = (bf16[4,172,128]{2,1,0:T(8,128)(2,1)S(1)}, bf16[4,172,128]{2,1,0:T(8,128)(2,1)S(1)}, u32[]{:S(2)}, u32[]{:S(2)}) collective-permute-start(bf16[4,172,128]{2,1,0:T(8,128)(2,1)S(1)} %copy-done), channel_id=1, source_target_pairs={{0,192},{8,200},{16,208},{24,216},{32,224},{40,232},{48,240},{56,2... | collective-permute-start | bytes 528392 | tf_op jit(solution)/shard_map/ppermute | solution.py:349
  36.4 15.7 %collective-permute-start.10 = (bf16[512,128]{1,0:T(8,128)(2,1)S(1)}, bf16[512,128]{1,0:T(8,128)(2,1)S(1)}, u32[]{:S(2)}, u32[]{:S(2)}) collective-permute-start(bf16[512,128]{1,0:T(8,128)(2,1)S(1)} %get-tuple-element.32), channel_id=1, source_target_pairs={{0,192},{8,200},{16,208},{24,216},{32,224},{40,232},{48,240},{56,2... | collective-permute-start | bytes 393224 | tf_op jit(solution)/shard_map/ppermute | solution.py:349
  39.8 12.3 %collective-permute-start.8 = (bf16[512,128]{1,0:T(8,128)(2,1)S(1)}, bf16[512,128]{1,0:T(8,128)(2,1)S(1)}, u32[]{:S(2)}, u32[]{:S(2)}) collective-permute-start(bf16[512,128]{1,0:T(8,128)(2,1)S(1)} %get-tuple-element.30), channel_id=1, source_target_pairs={{0,64},{8,72},{16,80},{24,88},{32,96},{40,104},{48,112},{56,120},{... | collective-permute-start | bytes 393224 | tf_op jit(solution)/shard_map/ppermute | solution.py:349
  39.8 12.3 %collective-permute-start.9 = (bf16[512,128]{1,0:T(8,128)(2,1)S(1)}, bf16[512,128]{1,0:T(8,128)(2,1)S(1)}, u32[]{:S(2)}, u32[]{:S(2)}) collective-permute-start(bf16[512,128]{1,0:T(8,128)(2,1)S(1)} %get-tuple-element.31), channel_id=1, source_target_pairs={{0,128},{8,136},{16,144},{24,152},{32,160},{40,168},{48,176},{56,1... | collective-permute-start | bytes 393224 | tf_op jit(solution)/shard_map/ppermute | solution.py:349
  52.4 19.9 %collective-permute-start.21 = (bf16[16,172,128]{2,0,1:T(8,128)(2,1)S(1)}, bf16[16,172,128]{2,0,1:T(8,128)(2,1)S(1)}, u32[]{:S(2)}, u32[]{:S(2)}) collective-permute-start(bf16[16,172,128]{2,0,1:T(8,128)(2,1)S(1)} %copy.10), channel_id=1, source_target_pairs={{0,8},{8,0},{16,24},{24,16},{32,40},{40,32},{48,56},{56,48},{64,72... | collective-permute-start | bytes 2113544 | tf_op jit(solution)/shard_map/ppermute | solution.py:349
  53.3 5.6 %collective-permute-start.16 = (bf16[128,128]{1,0:T(8,128)(2,1)S(1)}, bf16[128,128]{1,0:T(8,128)(2,1)S(1)}, u32[]{:S(2)}, u32[]{:S(2)}) collective-permute-start(bf16[128,128]{1,0:T(8,128)(2,1)S(1)} %get-tuple-element.37), channel_id=1, source_target_pairs={{0,48},{8,56},{16,32},{24,40},{32,16},{40,24},{48,0},{56,8},{64,11... | collective-permute-start | bytes 98312 | tf_op jit(solution)/shard_map/ppermute | solution.py:349
  58.9 8.2 %collective-permute-start.17 = (bf16[128,128]{1,0:T(8,128)(2,1)S(1)}, bf16[128,128]{1,0:T(8,128)(2,1)S(1)}, u32[]{:S(2)}, u32[]{:S(2)}) collective-permute-start(bf16[128,128]{1,0:T(8,128)(2,1)S(1)} %shard_map.99), channel_id=1, source_target_pairs={{0,4},{1,5},{2,6},{3,7},{4,0},{5,1},{6,2},{7,3},{8,12},{9,13},{10,... | collective-permute-start | bytes 98312 | tf_op jit(solution)/shard_map/ppermute | solution.py:353
  67.2 7.0 %collective-permute-start.18 = (bf16[2,128,128]{2,1,0:T(8,128)(2,1)S(1)}, bf16[2,128,128]{2,1,0:T(8,128)(2,1)S(1)}, u32[]{:S(2)}, u32[]{:S(2)}) collective-permute-start(bf16[2,128,128]{2,1,0:T(8,128)(2,1)S(1)} %pad_maximum_fusion.1.a0_ref), channel_id=1, source_target_pairs={{0,1},{1,0},{2,3},{3,2},{4,5},{5,4},{6,7},{7,6},{8,9},{9,8},{10,11... | collective-permute-start | bytes 196616 | tf_op jit(solution)/shard_map/ppermute | solution.py:355
  67.6 7.6 %collective-permute-start.19 = (bf16[2,128,128]{2,1,0:T(8,128)(2,1)S(1)}, bf16[2,128,128]{2,1,0:T(8,128)(2,1)S(1)}, u32[]{:S(2)}, u32[]{:S(2)}) collective-permute-start(bf16[2,128,128]{2,1,0:T(8,128)(2,1)S(1)} %pad_maximum_fusion.1.a0_ref), channel_id=1, source_target_pairs={{0,2},{1,3},{2,0},{3,1},{4,6},{5,7},{6,4},{7,5},{8,10},{9,11},{10,... | collective-permute-start | bytes 196616 | tf_op jit(solution)/shard_map/ppermute | solution.py:355
  83.2 8.4 %collective-permute-start.23 = (bf16[864,128]{1,0:T(8,128)(2,1)S(1)}, bf16[864,128]{1,0:T(8,128)(2,1)S(1)}, u32[]{:S(2)}, u32[]{:S(2)}) collective-permute-start(bf16[864,128]{1,0:T(8,128)(2,1)S(1)} %get-tuple-element.42), channel_id=1, source_target_pairs={{0,64},{8,72},{16,80},{24,88},{32,96},{40,104},{48,112},{56,120},{... | collective-permute-start | bytes 663560 | tf_op jit(solution)/shard_map/ppermute | solution.py:349
  83.3 11.8 %collective-permute-start.24 = (bf16[864,128]{1,0:T(8,128)(2,1)S(1)}, bf16[864,128]{1,0:T(8,128)(2,1)S(1)}, u32[]{:S(2)}, u32[]{:S(2)}) collective-permute-start(bf16[864,128]{1,0:T(8,128)(2,1)S(1)} %get-tuple-element.43), channel_id=1, source_target_pairs={{0,128},{8,136},{16,144},{24,152},{32,160},{40,168},{48,176},{56,1... | collective-permute-start | bytes 663560 | tf_op jit(solution)/shard_map/ppermute | solution.py:349
  84.8 13.1 %collective-permute-start.25 = (bf16[864,128]{1,0:T(8,128)(2,1)S(1)}, bf16[864,128]{1,0:T(8,128)(2,1)S(1)}, u32[]{:S(2)}, u32[]{:S(2)}) collective-permute-start(bf16[864,128]{1,0:T(8,128)(2,1)S(1)} %get-tuple-element.44), channel_id=1, source_target_pairs={{0,192},{8,200},{16,208},{24,216},{32,224},{40,232},{48,240},{56,2... | collective-permute-start | bytes 663560 | tf_op jit(solution)/shard_map/ppermute | solution.py:349
  100.4 6.8 %collective-permute-start.27 = (bf16[336,128]{1,0:T(8,128)(2,1)S(1)}, bf16[336,128]{1,0:T(8,128)(2,1)S(1)}, u32[]{:S(2)}, u32[]{:S(2)}) collective-permute-start(bf16[336,128]{1,0:T(8,128)(2,1)S(1)} %get-tuple-element.47), channel_id=1, source_target_pairs={{0,32},{8,40},{16,48},{24,56},{32,0},{40,8},{48,16},{56,24},{64,96... | collective-permute-start | bytes 258056 | tf_op jit(solution)/shard_map/ppermute | solution.py:349
  101.9 7.1 %collective-permute-start.28 = (bf16[336,128]{1,0:T(8,128)(2,1)S(1)}, bf16[336,128]{1,0:T(8,128)(2,1)S(1)}, u32[]{:S(2)}, u32[]{:S(2)}) collective-permute-start(bf16[336,128]{1,0:T(8,128)(2,1)S(1)} %get-tuple-element.48), channel_id=1, source_target_pairs={{0,48},{8,56},{16,32},{24,40},{32,16},{40,24},{48,0},{56,8},{64,11... | collective-permute-start | bytes 258056 | tf_op jit(solution)/shard_map/ppermute | solution.py:349
  130.3 7.2 %collective-permute-start.30 = (f32[160,128]{1,0:T(8,128)S(1)}, f32[160,128]{1,0:T(8,128)S(1)}, u32[]{:S(2)}, u32[]{:S(2)}) collective-permute-start(f32[160,128]{1,0:T(8,128)S(1)} %shard_map.106.own_ref), channel_id=1, source_target_pairs={{0,128},{8,136},{16,144},{24,152},{32,160},{40,168},{48,176},{56,1... | collective-permute-start | bytes 245768 | tf_op jit(solution)/shard_map/ppermute | solution.py:349
  134.2 5.7 %collective-permute-start.31 = (f32[160,128]{1,0:T(8,128)S(1)}, f32[160,128]{1,0:T(8,128)S(1)}, u32[]{:S(2)}, u32[]{:S(2)}) collective-permute-start(f32[160,128]{1,0:T(8,128)S(1)} %shard_map.106.own_ref), channel_id=1, source_target_pairs={{0,192},{8,200},{16,208},{24,216},{32,224},{40,232},{48,240},{56,2... | collective-permute-start | bytes 245768 | tf_op jit(solution)/shard_map/ppermute | solution.py:349
  (14 other events, 54.9 us)

commit v4 on v3

--- a/solution.py
+++ b/solution.py
@@ -1,5 +1,3 @@
-import functools
-
 import jax
 import jax.numpy as jnp
 from jax import lax
@@ -54,8 +52,7 @@
 
 
 def densify_body(
-    me_ref, side_ref, count_ref, slot_ref, block_ref, g0_ref, g1_ref, g2_ref, g3_ref,
-    dense_ref, near_ref, held_ref, sem_ref,
+    me_ref, side_ref, count_ref, slot_ref, block_ref, dense_ref, held_ref, sem_ref
 ):
     moves = [
         pltpu.make_async_copy(
@@ -66,8 +63,6 @@
     for move in moves:
         move.start()
     dense_ref[...] = jnp.zeros_like(dense_ref)
-    for d, ref in enumerate((g0_ref, g1_ref, g2_ref, g3_ref)):
-        near_ref[d] = ref[...]
     me = me_ref[0]
     side = side_ref[0]
     count = count_ref[0]
@@ -87,37 +82,53 @@
         lax.fori_loop(i * LOAD, jnp.clip(count, i * LOAD, (i + 1) * LOAD), place, 0)
 
 
-def densify(me, side, counts, slots, blocks, cotangents):
+def densify(me, side, counts, slots, blocks):
     return pl.pallas_call(
         densify_body,
-        out_shape=[
-            pltpu.VMEM((4096, 1024), BF16),
-            jax.ShapeDtypeStruct((4,) + cotangents[0].shape, BF16),
-        ],
-        in_specs=[smem(), smem(), smem(), smem(), hbm()] + [vmem()] * 4,
-        out_specs=[vmem(), vmem()],
+        out_shape=pltpu.VMEM((4096, 1024), BF16),
+        in_specs=[smem(), smem(), smem(), smem(), hbm()],
+        out_specs=vmem(),
         scratch_shapes=[pltpu.VMEM(blocks.shape, BF16), pltpu.SemaphoreType.DMA((LOADS,))],
         compiler_params=pltpu.CompilerParams(vmem_limit_bytes=52 * 1024 * 1024),
-    )(me, side, counts, slots, blocks, *cotangents)
+    )(me, side, counts, slots, blocks)
 
 
 def joined(refs):
     return jnp.concatenate([ref[h] for ref in refs for h in range(2)])
 
 
-def rows_product_body(half, dense_ref, r0_ref, r1_ref, r2_ref, r3_ref, out_ref):
-    right = joined((r0_ref, r1_ref, r2_ref, r3_ref))
+def rows_product_step(half, dense_ref, right_refs, out_ref):
+    right = joined(right_refs)
     for i in range(4):
-        part = dot(rows_of(dense_ref, 4 * half, i), right, 1, 0)
-        out_ref[i * STEP : (i + 1) * STEP, :] = part.astype(out_ref.dtype)
-
-
-def rows_product(dense, parts, half, dtype):
-    return call(
-        functools.partial(rows_product_body, half),
-        [((2048, BS), dtype)],
+        out_ref[i * STEP : (i + 1) * STEP, :] = dot(rows_of(dense_ref, 4 * half, i), right, 1, 0)
+
+
+def rows_product_far_body(
+    dense_ref, r0_ref, r1_ref, r2_ref, r3_ref, g0_ref, g1_ref, g2_ref, g3_ref, out_ref, grad_ref
+):
+    for d, ref in enumerate((g0_ref, g1_ref, g2_ref, g3_ref)):
+        grad_ref[d] = ref[...]
+    rows_product_step(1, dense_ref, (r0_ref, r1_ref, r2_ref, r3_ref), out_ref)
+
+
+def rows_product_far(dense, parts, cotangents):
+    return call(
+        rows_product_far_body,
+        [((2048, BS), F32), ((4,) + cotangents[0].shape, BF16)],
+        (dense, *parts, *cotangents),
+        flops=2 * 2048 * 1024 * 256,
+    )
+
+
+def rows_product_near_body(dense_ref, r0_ref, r1_ref, r2_ref, r3_ref, out_ref):
+    rows_product_step(0, dense_ref, (r0_ref, r1_ref, r2_ref, r3_ref), out_ref)
+
+
+def rows_product_near(dense, parts):
+    return call(
+        rows_product_near_body,
+        [((2048, BS), F32)],
         (dense, *parts),
-        [vmem()] * 5,
         flops=2 * 2048 * 1024 * 256,
     )[0]
 
@@ -140,8 +151,10 @@
     high = q.astype(BF16)
     low = (q - high.astype(F32)).astype(BF16)
     spread = dot(high, w_out, 0, 0) + dot(low, w_out, 0, 0)
-    pre_grad = (spread * (gate * (1.0 + pre * (1.0 - gate)))).astype(BF16)
-    in_grad = dot(agg, pre_grad, 0, 0)
+    pre_grad = spread * (gate * (1.0 + pre * (1.0 - gate)))
+    pre_high = pre_grad.astype(BF16)
+    pre_low = (pre_grad - pre_high.astype(F32)).astype(BF16)
+    in_grad = dot(agg, pre_high, 0, 0) + dot(agg, pre_low, 0, 0)
     out_grad = dot(high, hid, 1, 0) + dot(low, hid, 1, 0)
     pieces = []
     for array in (in_grad, out_grad):
@@ -368,10 +381,10 @@
     parts = gather_col(features)
     grad_t = logit_grad.T
     cotangents = [grad_t] + [permute(grad_t, f) for f in Z_FLIPS]
-    dense, grad_z = densify(me, side, block_counts, block_slots, block_values, cotangents)
-    far = rows_product(dense, parts, 1, F32)
+    dense = densify(me, side, block_counts, block_slots, block_values)
+    far, grad_z = rows_product_far(dense, parts, cotangents)
     got = permute(far, CORE)
-    mine = rows_product(dense, parts, 0, F32)
+    mine = rows_product_near(dense, parts)
     s1, s2, s3, keep = core_sum(mine, got)
     received = [permute(s, f) for s, f in zip((s1, s2, s3), X_FLIPS)]
     grad_x = [grad_z] + [permute(grad_z, f) for f in X_FLIPS]

time: 141 us -> 136 us (0.965)
  starting transfers between devices: 54.8 us -> 51.6 us
  waiting for transfers between devices: 46.4 us -> 43.5 us
    ppermute x24, waiting for transfers between devices: 39.5 us -> 37.1 us  [permute(): return lax.ppermute(x, 'row', [(i, i ^ flip) for i in range(32)])]
    ppermute x24, starting transfers between devices: 32.3 us -> 30.3 us  [permute(): return lax.ppermute(x, 'row', [(i, i ^ flip) for i in range(32)])]
  transfers between devices with their start and end apart: 32 -> 32, of which waited for: 21 -> 19; matrix products, arithmetic and copies ran while one was open for 1% -> 1% of each run, Pallas kernels for 7% -> 8%
where the time goes in v4:
time: 136 us; the launch traced here: 135 us
  starting transfers between devices  51.6 us (38%)
  waiting for transfers between devices  43.5 us (32%)
  blocking collectives  20.2 us (15%)
  Pallas kernels  16.8 us (12%)
  between operations  1.52 us (1%)
    ppermute x24, waiting for transfers between devices, permute(): return lax.ppermute(x, 'row', [(i, i ^ flip) for i in range(32)])  37.1 us
    ppermute x24, starting transfers between devices, permute(): return lax.ppermute(x, 'row', [(i, i ^ flip) for i in range(32)])  30.3 us
    all_to_all x1, blocking collectives, on_device(): own = share_sum(lax.all_to_all(shares, 'col', 0, 0))  20.2 us
    ppermute x2, starting transfers between devices, gather_col(): far = lax.ppermute(x, 'col', [(i, i ^ 4) for i in range(8)])  11.9 us
    pallas_call x13, Pallas kernels, call(): pl.pallas_call(body, out_shape=[o if len(o) == 1 else jax.ShapeDtypeStruc...  10.5 us
    ppermute x6, starting transfers between devices, gather_col(): lax.ppermute(pair, 'col', [(i, i ^ d) for i in range(8)])  9.48 us
    pallas_call x1, Pallas kernels, densify(): pl.pallas_call(densify_body, out_shape=pltpu.VMEM((4096, 1024), BF16), in...  6.33 us
    ppermute x2, waiting for transfers between devices, gather_col(): far = lax.ppermute(x, 'col', [(i, i ^ 4) for i in range(8)])  3.89 us
  transfers between devices with their start and end apart: 32, of which 19 were waited for; matrix products, arithmetic and copies ran while one was open for 1% of the time, Pallas kernels for 8%

profile of v4, /device:TPU:32, one launch (start us, length us, event | category | flops | bytes accessed | tf_op | source)
XLA Modules:
  0.0 134.8 jit_solution(302463535268755369)
XLA Ops:
  0.6 6.4 %collective-permute-start = (bf16[128,128]{1,0:T(8,128)(2,1)}, bf16[128,128]{1,0:T(8,128)(2,1)S(1)}, u32[]{:S(2)}, u32[]{:S(2)}) collective-permute-start(bf16[128,128]{1,0:T(8,128)(2,1)} %param.7), channel_id=1, source_target_pairs={{0,4},{1,5},{2,6},{3,7},{4,0},{5,1},{6,2},{7,3},{8,12},{9,13},{10,... | collective-permute-start | bytes 98312 | tf_op jit(solution)/shard_map/ppermute | solution.py:366
  11.8 2.9 %collective-permute-start.2 = (bf16[2,128,128]{2,1,0:T(8,128)(2,1)S(1)}, bf16[2,128,128]{2,1,0:T(8,128)(2,1)S(1)}, u32[]{:S(2)}, u32[]{:S(2)}) collective-permute-start(bf16[2,128,128]{2,1,0:T(8,128)(2,1)S(1)} %pad_maximum_fusion.r0_ref), channel_id=1, source_target_pairs={{0,2},{1,3},{2,0},{3,1},{4,6},{5,7},{6,4},{7,5},{8,10},{9,11},{10,... | collective-permute-start | bytes 196616 | tf_op jit(solution)/shard_map/ppermute | solution.py:368
  14.9 2.6 %collective-permute-start.5 = (bf16[172,128]{1,0:T(8,128)(2,1)}, bf16[172,128]{1,0:T(8,128)(2,1)S(1)}, u32[]{:S(2)}, u32[]{:S(2)}) collective-permute-start(bf16[172,128]{1,0:T(8,128)(2,1)} %bitcast.13), channel_id=1, source_target_pairs={{0,32},{8,40},{16,48},{24,56},{32,0},{40,8},{48,16},{56,24},{64,96... | collective-permute-start | bytes 132104 | tf_op jit(solution)/shard_map/ppermute | solution.py:362
  18.3 6.3 %shard_map.94.dense_ref = bf16[4096,1024]{1,0:T(8,128)(2,1)S(1)} custom-call(s32[1]{0:T(128)} %bitcast.me_ref, s32[1]{0:T(128)} %bitcast.1.side_ref, s32[1]{0:T(128)S(6)} %copy.12.count_ref, s32[144]{0:T(256)} %slot_ref.1, bf16[144,128,128]{2,1,0:T(8,128)(2,1)} %block_ref.1), custom_call_target="tpu_custom_call" | custom-call | tf_op jit(solution)/shard_map/pallas_call | solution.py:86
  26.2 3.8 %collective-permute-start.12 = (bf16[4,172,128]{2,1,0:T(8,128)(2,1)S(1)}, bf16[4,172,128]{2,1,0:T(8,128)(2,1)S(1)}, u32[]{:S(2)}, u32[]{:S(2)}) collective-permute-start(bf16[4,172,128]{2,1,0:T(8,128)(2,1)S(1)} %get-tuple-element.33.g0_ref), channel_id=1, source_target_pairs={{0,128},{8,136},{16,144},{24,152},{32,160},{40,168},{48,176},{56,1... | collective-permute-start | bytes 528392 | tf_op jit(solution)/shard_map/ppermute | solution.py:362
  32.2 2.5 %collective-permute-start.10 = (bf16[512,128]{1,0:T(8,128)(2,1)S(1)}, bf16[512,128]{1,0:T(8,128)(2,1)S(1)}, u32[]{:S(2)}, u32[]{:S(2)}) collective-permute-start(bf16[512,128]{1,0:T(8,128)(2,1)S(1)} %get-tuple-element.32), channel_id=1, source_target_pairs={{0,192},{8,200},{16,208},{24,216},{32,224},{40,232},{48,240},{56,2... | collective-permute-start | bytes 393224 | tf_op jit(solution)/shard_map/ppermute | solution.py:362
  34.7 2.3 %collective-permute-start.9 = (bf16[512,128]{1,0:T(8,128)(2,1)S(1)}, bf16[512,128]{1,0:T(8,128)(2,1)S(1)}, u32[]{:S(2)}, u32[]{:S(2)}) collective-permute-start(bf16[512,128]{1,0:T(8,128)(2,1)S(1)} %get-tuple-element.31), channel_id=1, source_target_pairs={{0,128},{8,136},{16,144},{24,152},{32,160},{40,168},{48,176},{56,1... | collective-permute-start | bytes 393224 | tf_op jit(solution)/shard_map/ppermute | solution.py:362
  37.0 2.2 %collective-permute-done.12.g2_ref = bf16[4,172,128]{2,1,0:T(8,128)(2,1)S(1)} collective-permute-done((bf16[4,172,128]{2,1,0:T(8,128)(2,1)S(1)}, bf16[4,172,128]{2,1,0:T(8,128)(2,1)S(1)}, u32[]{:S(2)}, u32[]{:S(2)}) %collective-permute-start.12) | collective-permute-done | bytes 176160 | tf_op jit(solution)/shard_map/ppermute | solution.py:362
  39.2 5.9 %collective-permute-done.13.g3_ref = bf16[4,172,128]{2,1,0:T(8,128)(2,1)S(1)} collective-permute-done((bf16[4,172,128]{2,1,0:T(8,128)(2,1)S(1)}, bf16[4,172,128]{2,1,0:T(8,128)(2,1)S(1)}, u32[]{:S(2)}, u32[]{:S(2)}) %collective-permute-start.13) | collective-permute-done | bytes 176160 | tf_op jit(solution)/shard_map/ppermute | solution.py:362
  54.5 5.5 %collective-permute-start.17 = (bf16[128,128]{1,0:T(8,128)(2,1)S(1)}, bf16[128,128]{1,0:T(8,128)(2,1)S(1)}, u32[]{:S(2)}, u32[]{:S(2)}) collective-permute-start(bf16[128,128]{1,0:T(8,128)(2,1)S(1)} %shard_map.99), channel_id=1, source_target_pairs={{0,4},{1,5},{2,6},{3,7},{4,0},{5,1},{6,2},{7,3},{8,12},{9,13},{10,... | collective-permute-start | bytes 98312 | tf_op jit(solution)/shard_map/ppermute | solution.py:366
  60.0 2.4 %collective-permute-done.17 = bf16[128,128]{1,0:T(8,128)(2,1)S(1)} collective-permute-done((bf16[128,128]{1,0:T(8,128)(2,1)S(1)}, bf16[128,128]{1,0:T(8,128)(2,1)S(1)}, u32[]{:S(2)}, u32[]{:S(2)}) %collective-permute-start.17) | collective-permute-done | bytes 32800 | tf_op jit(solution)/shard_map/ppermute | solution.py:366
  63.8 2.3 %collective-permute-start.19 = (bf16[2,128,128]{2,1,0:T(8,128)(2,1)S(1)}, bf16[2,128,128]{2,1,0:T(8,128)(2,1)S(1)}, u32[]{:S(2)}, u32[]{:S(2)}) collective-permute-start(bf16[2,128,128]{2,1,0:T(8,128)(2,1)S(1)} %pad_maximum_fusion.1.a0_ref), channel_id=1, source_target_pairs={{0,2},{1,3},{2,0},{3,1},{4,6},{5,7},{6,4},{7,5},{8,10},{9,11},{10,... | collective-permute-start | bytes 196616 | tf_op jit(solution)/shard_map/ppermute | solution.py:368
  69.6 2.0 %collective-permute-done.20.a3_ref = bf16[2,128,128]{2,1,0:T(8,128)(2,1)S(1)} collective-permute-done((bf16[2,128,128]{2,1,0:T(8,128)(2,1)S(1)}, bf16[2,128,128]{2,1,0:T(8,128)(2,1)S(1)}, u32[]{:S(2)}, u32[]{:S(2)}) %collective-permute-start.20) | collective-permute-done | bytes 65568 | tf_op jit(solution)/shard_map/ppermute | solution.py:368
  71.6 2.9 %shard_map.101 = (bf16[176,1024]{1,0:T(8,128)(2,1)S(1)}, bf16[3456,128]{1,0:T(8,128)(2,1)S(1)}) custom-call(bf16[2,128,128]{2,1,0:T(8,128)(2,1)S(1)} %pad_maximum_fusion.1.a0_ref, bf16[2,128,128]{2,1,0:T(8,128)(2,1)S(1)} %collective-permute-done.18.a1_ref, bf16[2,128,128]{2,1,0:T(8,128)(2,1)S(1)} %collective-permute-done.19.a2_ref, ...), custom_call_target="tpu_custom_call" | custom-call | flops 2147483648 | bytes 1048576 | tf_op jit(solution)/shard_map/pallas_call | solution.py:34
  77.2 3.6 %collective-permute-start.24 = (bf16[864,128]{1,0:T(8,128)(2,1)S(1)}, bf16[864,128]{1,0:T(8,128)(2,1)S(1)}, u32[]{:S(2)}, u32[]{:S(2)}) collective-permute-start(bf16[864,128]{1,0:T(8,128)(2,1)S(1)} %get-tuple-element.43), channel_id=1, source_target_pairs={{0,128},{8,136},{16,144},{24,152},{32,160},{40,168},{48,176},{56,1... | collective-permute-start | bytes 663560 | tf_op jit(solution)/shard_map/ppermute | solution.py:362
  81.9 3.6 %collective-permute-done.23.r1_ref = bf16[864,128]{1,0:T(8,128)(2,1)S(1)} collective-permute-done((bf16[864,128]{1,0:T(8,128)(2,1)S(1)}, bf16[864,128]{1,0:T(8,128)(2,1)S(1)}, u32[]{:S(2)}, u32[]{:S(2)}) %collective-permute-start.23) | collective-permute-done | bytes 221216 | tf_op jit(solution)/shard_map/ppermute | solution.py:362
  85.5 5.6 %collective-permute-done.24.r2_ref = bf16[864,128]{1,0:T(8,128)(2,1)S(1)} collective-permute-done((bf16[864,128]{1,0:T(8,128)(2,1)S(1)}, bf16[864,128]{1,0:T(8,128)(2,1)S(1)}, u32[]{:S(2)}, u32[]{:S(2)}) %collective-permute-start.24) | collective-permute-done | bytes 221216 | tf_op jit(solution)/shard_map/ppermute | solution.py:362
  91.1 2.6 %collective-permute-done.25.r3_ref = bf16[864,128]{1,0:T(8,128)(2,1)S(1)} collective-permute-done((bf16[864,128]{1,0:T(8,128)(2,1)S(1)}, bf16[864,128]{1,0:T(8,128)(2,1)S(1)}, u32[]{:S(2)}, u32[]{:S(2)}) %collective-permute-start.25) | collective-permute-done | bytes 221216 | tf_op jit(solution)/shard_map/ppermute | solution.py:362
  93.8 2.0 %collective-permute-start.26 = (bf16[336,128]{1,0:T(8,128)(2,1)S(1)}, bf16[336,128]{1,0:T(8,128)(2,1)S(1)}, u32[]{:S(2)}, u32[]{:S(2)}) collective-permute-start(bf16[336,128]{1,0:T(8,128)(2,1)S(1)} %get-tuple-element.46), channel_id=1, source_target_pairs={{0,16},{8,24},{16,0},{24,8},{32,48},{40,56},{48,32},{56,40},{64,80... | collective-permute-start | bytes 258056 | tf_op jit(solution)/shard_map/ppermute | solution.py:362
  99.1 3.0 %collective-permute-done.27.r2_ref = bf16[336,128]{1,0:T(8,128)(2,1)S(1)} collective-permute-done((bf16[336,128]{1,0:T(8,128)(2,1)S(1)}, bf16[336,128]{1,0:T(8,128)(2,1)S(1)}, u32[]{:S(2)}, u32[]{:S(2)}) %collective-permute-start.27) | collective-permute-done | bytes 86048 | tf_op jit(solution)/shard_map/ppermute | solution.py:362
  102.1 2.1 %collective-permute-done.28.r3_ref = bf16[336,128]{1,0:T(8,128)(2,1)S(1)} collective-permute-done((bf16[336,128]{1,0:T(8,128)(2,1)S(1)}, bf16[336,128]{1,0:T(8,128)(2,1)S(1)}, u32[]{:S(2)}, u32[]{:S(2)}) %collective-permute-start.28) | collective-permute-done | bytes 86048 | tf_op jit(solution)/shard_map/ppermute | solution.py:362
  104.8 20.2 %all_to_all.5.parts_ref = bf16[8,160,128]{2,1,0:T(8,128)(2,1)S(1)} all-to-all(bf16[8,160,128]{2,1,0:T(8,128)(2,1)S(1)} %get-tuple-element.50), channel_id=1, replica_groups=mesh['row'=32,'col'=8] {'col'}, dimensions={0} | all-to-all | bytes 655360 | tf_op jit(solution)/shard_map/all_to_all | solution.py:404
  125.2 3.2 %collective-permute-start.30 = (f32[160,128]{1,0:T(8,128)S(1)}, f32[160,128]{1,0:T(8,128)S(1)}, u32[]{:S(2)}, u32[]{:S(2)}) collective-permute-start(f32[160,128]{1,0:T(8,128)S(1)} %shard_map.106.own_ref), channel_id=1, source_target_pairs={{0,128},{8,136},{16,144},{24,152},{32,160},{40,168},{48,176},{56,1... | collective-permute-start | bytes 245768 | tf_op jit(solution)/shard_map/ppermute | solution.py:362
  131.7 2.4 %collective-permute-done.31.r3_ref = f32[160,128]{1,0:T(8,128)S(1)} collective-permute-done((f32[160,128]{1,0:T(8,128)S(1)}, f32[160,128]{1,0:T(8,128)S(1)}, u32[]{:S(2)}, u32[]{:S(2)}) %collective-permute-start.31) | collective-permute-done | bytes 81952 | tf_op jit(solution)/shard_map/ppermute | solution.py:362
  (65 shorter events, 35.1 us)
Async XLA Ops:
  0.6 8.8 %collective-permute-start = (bf16[128,128]{1,0:T(8,128)(2,1)}, bf16[128,128]{1,0:T(8,128)(2,1)S(1)}, u32[]{:S(2)}, u32[]{:S(2)}) collective-permute-start(bf16[128,128]{1,0:T(8,128)(2,1)} %param.7), channel_id=1, source_target_pairs={{0,4},{1,5},{2,6},{3,7},{4,0},{5,1},{6,2},{7,3},{8,12},{9,13},{10,... | collective-permute-start | bytes 98312 | tf_op jit(solution)/shard_map/ppermute | solution.py:366
  7.0 10.5 %collective-permute-start.4 = (bf16[172,128]{1,0:T(8,128)(2,1)}, bf16[172,128]{1,0:T(8,128)(2,1)S(1)}, u32[]{:S(2)}, u32[]{:S(2)}) collective-permute-start(bf16[172,128]{1,0:T(8,128)(2,1)} %bitcast.12), channel_id=1, source_target_pairs={{0,16},{8,24},{16,0},{24,8},{32,48},{40,56},{48,32},{56,40},{64,80... | collective-permute-start | bytes 132104 | tf_op jit(solution)/shard_map/ppermute | solution.py:362
  10.2 14.4 %collective-permute-start.1 = (bf16[2,128,128]{2,1,0:T(8,128)(2,1)S(1)}, bf16[2,128,128]{2,1,0:T(8,128)(2,1)S(1)}, u32[]{:S(2)}, u32[]{:S(2)}) collective-permute-start(bf16[2,128,128]{2,1,0:T(8,128)(2,1)S(1)} %pad_maximum_fusion.r0_ref), channel_id=1, source_target_pairs={{0,1},{1,0},{2,3},{3,2},{4,5},{5,4},{6,7},{7,6},{8,9},{9,8},{10,11... | collective-permute-start | bytes 196616 | tf_op jit(solution)/shard_map/ppermute | solution.py:368
  11.8 12.9 %collective-permute-start.2 = (bf16[2,128,128]{2,1,0:T(8,128)(2,1)S(1)}, bf16[2,128,128]{2,1,0:T(8,128)(2,1)S(1)}, u32[]{:S(2)}, u32[]{:S(2)}) collective-permute-start(bf16[2,128,128]{2,1,0:T(8,128)(2,1)S(1)} %pad_maximum_fusion.r0_ref), channel_id=1, source_target_pairs={{0,2},{1,3},{2,0},{3,1},{4,6},{5,7},{6,4},{7,5},{8,10},{9,11},{10,... | collective-permute-start | bytes 196616 | tf_op jit(solution)/shard_map/ppermute | solution.py:368
  14.7 10.0 %collective-permute-start.3 = (bf16[2,128,128]{2,1,0:T(8,128)(2,1)S(1)}, bf16[2,128,128]{2,1,0:T(8,128)(2,1)S(1)}, u32[]{:S(2)}, u32[]{:S(2)}) collective-permute-start(bf16[2,128,128]{2,1,0:T(8,128)(2,1)S(1)} %pad_maximum_fusion.r0_ref), channel_id=1, source_target_pairs={{0,3},{1,2},{2,1},{3,0},{4,7},{5,6},{6,5},{7,4},{8,11},{9,10},{10,... | collective-permute-start | bytes 196616 | tf_op jit(solution)/shard_map/ppermute | solution.py:368
  14.9 9.7 %collective-permute-start.5 = (bf16[172,128]{1,0:T(8,128)(2,1)}, bf16[172,128]{1,0:T(8,128)(2,1)S(1)}, u32[]{:S(2)}, u32[]{:S(2)}) collective-permute-start(bf16[172,128]{1,0:T(8,128)(2,1)} %bitcast.13), channel_id=1, source_target_pairs={{0,32},{8,40},{16,48},{24,56},{32,0},{40,8},{48,16},{56,24},{64,96... | collective-permute-start | bytes 132104 | tf_op jit(solution)/shard_map/ppermute | solution.py:362
  17.5 7.2 %collective-permute-start.6 = (bf16[172,128]{1,0:T(8,128)(2,1)}, bf16[172,128]{1,0:T(8,128)(2,1)S(1)}, u32[]{:S(2)}, u32[]{:S(2)}) collective-permute-start(bf16[172,128]{1,0:T(8,128)(2,1)} %bitcast.14), channel_id=1, source_target_pairs={{0,48},{8,56},{16,32},{24,40},{32,16},{40,24},{48,0},{56,8},{64,11... | collective-permute-start | bytes 132104 | tf_op jit(solution)/shard_map/ppermute | solution.py:362
  26.0 6.1 %collective-permute-start.7 = (f32[2048,128]{1,0:T(8,128)S(1)}, f32[2048,128]{1,0:T(8,128)S(1)}, u32[]{:S(2)}, u32[]{:S(2)}) collective-permute-start(f32[2048,128]{1,0:T(8,128)S(1)} %get-tuple-element.28), channel_id=1, source_target_pairs={{0,8},{8,0},{16,24},{24,16},{32,40},{40,32},{48,56},{56,48},{64,72... | collective-permute-start | bytes 3145736 | tf_op jit(solution)/shard_map/ppermute | solution.py:362
  26.1 8.6 %collective-permute-start.11 = (bf16[4,172,128]{2,1,0:T(8,128)(2,1)S(1)}, bf16[4,172,128]{2,1,0:T(8,128)(2,1)S(1)}, u32[]{:S(2)}, u32[]{:S(2)}) collective-permute-start(bf16[4,172,128]{2,1,0:T(8,128)(2,1)S(1)} %get-tuple-element.33.g0_ref), channel_id=1, source_target_pairs={{0,64},{8,72},{16,80},{24,88},{32,96},{40,104},{48,112},{56,120},{... | collective-permute-start | bytes 528392 | tf_op jit(solution)/shard_map/ppermute | solution.py:362
  26.2 13.1 %collective-permute-start.12 = (bf16[4,172,128]{2,1,0:T(8,128)(2,1)S(1)}, bf16[4,172,128]{2,1,0:T(8,128)(2,1)S(1)}, u32[]{:S(2)}, u32[]{:S(2)}) collective-permute-start(bf16[4,172,128]{2,1,0:T(8,128)(2,1)S(1)} %get-tuple-element.33.g0_ref), channel_id=1, source_target_pairs={{0,128},{8,136},{16,144},{24,152},{32,160},{40,168},{48,176},{56,1... | collective-permute-start | bytes 528392 | tf_op jit(solution)/shard_map/ppermute | solution.py:362
  30.0 15.1 %collective-permute-start.13 = (bf16[4,172,128]{2,1,0:T(8,128)(2,1)S(1)}, bf16[4,172,128]{2,1,0:T(8,128)(2,1)S(1)}, u32[]{:S(2)}, u32[]{:S(2)}) collective-permute-start(bf16[4,172,128]{2,1,0:T(8,128)(2,1)S(1)} %get-tuple-element.33.g0_ref), channel_id=1, source_target_pairs={{0,192},{8,200},{16,208},{24,216},{32,224},{40,232},{48,240},{56,2... | collective-permute-start | bytes 528392 | tf_op jit(solution)/shard_map/ppermute | solution.py:362
  32.2 14.8 %collective-permute-start.10 = (bf16[512,128]{1,0:T(8,128)(2,1)S(1)}, bf16[512,128]{1,0:T(8,128)(2,1)S(1)}, u32[]{:S(2)}, u32[]{:S(2)}) collective-permute-start(bf16[512,128]{1,0:T(8,128)(2,1)S(1)} %get-tuple-element.32), channel_id=1, source_target_pairs={{0,192},{8,200},{16,208},{24,216},{32,224},{40,232},{48,240},{56,2... | collective-permute-start | bytes 393224 | tf_op jit(solution)/shard_map/ppermute | solution.py:362
  34.7 12.3 %collective-permute-start.8 = (bf16[512,128]{1,0:T(8,128)(2,1)S(1)}, bf16[512,128]{1,0:T(8,128)(2,1)S(1)}, u32[]{:S(2)}, u32[]{:S(2)}) collective-permute-start(bf16[512,128]{1,0:T(8,128)(2,1)S(1)} %get-tuple-element.30), channel_id=1, source_target_pairs={{0,64},{8,72},{16,80},{24,88},{32,96},{40,104},{48,112},{56,120},{... | collective-permute-start | bytes 393224 | tf_op jit(solution)/shard_map/ppermute | solution.py:362
  34.7 12.3 %collective-permute-start.9 = (bf16[512,128]{1,0:T(8,128)(2,1)S(1)}, bf16[512,128]{1,0:T(8,128)(2,1)S(1)}, u32[]{:S(2)}, u32[]{:S(2)}) collective-permute-start(bf16[512,128]{1,0:T(8,128)(2,1)S(1)} %get-tuple-element.31), channel_id=1, source_target_pairs={{0,128},{8,136},{16,144},{24,152},{32,160},{40,168},{48,176},{56,1... | collective-permute-start | bytes 393224 | tf_op jit(solution)/shard_map/ppermute | solution.py:362
  47.3 19.9 %collective-permute-start.21 = (bf16[16,172,128]{2,0,1:T(8,128)(2,1)S(1)}, bf16[16,172,128]{2,0,1:T(8,128)(2,1)S(1)}, u32[]{:S(2)}, u32[]{:S(2)}) collective-permute-start(bf16[16,172,128]{2,0,1:T(8,128)(2,1)S(1)} %copy.10), channel_id=1, source_target_pairs={{0,8},{8,0},{16,24},{24,16},{32,40},{40,32},{48,56},{56,48},{64,72... | collective-permute-start | bytes 2113544 | tf_op jit(solution)/shard_map/ppermute | solution.py:362
  54.5 7.9 %collective-permute-start.17 = (bf16[128,128]{1,0:T(8,128)(2,1)S(1)}, bf16[128,128]{1,0:T(8,128)(2,1)S(1)}, u32[]{:S(2)}, u32[]{:S(2)}) collective-permute-start(bf16[128,128]{1,0:T(8,128)(2,1)S(1)} %shard_map.99), channel_id=1, source_target_pairs={{0,4},{1,5},{2,6},{3,7},{4,0},{5,1},{6,2},{7,3},{8,12},{9,13},{10,... | collective-permute-start | bytes 98312 | tf_op jit(solution)/shard_map/ppermute | solution.py:366
  62.4 6.7 %collective-permute-start.18 = (bf16[2,128,128]{2,1,0:T(8,128)(2,1)S(1)}, bf16[2,128,128]{2,1,0:T(8,128)(2,1)S(1)}, u32[]{:S(2)}, u32[]{:S(2)}) collective-permute-start(bf16[2,128,128]{2,1,0:T(8,128)(2,1)S(1)} %pad_maximum_fusion.1.a0_ref), channel_id=1, source_target_pairs={{0,1},{1,0},{2,3},{3,2},{4,5},{5,4},{6,7},{7,6},{8,9},{9,8},{10,11... | collective-permute-start | bytes 196616 | tf_op jit(solution)/shard_map/ppermute | solution.py:368
  63.8 5.8 %collective-permute-start.19 = (bf16[2,128,128]{2,1,0:T(8,128)(2,1)S(1)}, bf16[2,128,128]{2,1,0:T(8,128)(2,1)S(1)}, u32[]{:S(2)}, u32[]{:S(2)}) collective-permute-start(bf16[2,128,128]{2,1,0:T(8,128)(2,1)S(1)} %pad_maximum_fusion.1.a0_ref), channel_id=1, source_target_pairs={{0,2},{1,3},{2,0},{3,1},{4,6},{5,7},{6,4},{7,5},{8,10},{9,11},{10,... | collective-permute-start | bytes 196616 | tf_op jit(solution)/shard_map/ppermute | solution.py:368
  77.1 8.4 %collective-permute-start.23 = (bf16[864,128]{1,0:T(8,128)(2,1)S(1)}, bf16[864,128]{1,0:T(8,128)(2,1)S(1)}, u32[]{:S(2)}, u32[]{:S(2)}) collective-permute-start(bf16[864,128]{1,0:T(8,128)(2,1)S(1)} %get-tuple-element.42), channel_id=1, source_target_pairs={{0,64},{8,72},{16,80},{24,88},{32,96},{40,104},{48,112},{56,120},{... | collective-permute-start | bytes 663560 | tf_op jit(solution)/shard_map/ppermute | solution.py:362
  77.2 13.9 %collective-permute-start.24 = (bf16[864,128]{1,0:T(8,128)(2,1)S(1)}, bf16[864,128]{1,0:T(8,128)(2,1)S(1)}, u32[]{:S(2)}, u32[]{:S(2)}) collective-permute-start(bf16[864,128]{1,0:T(8,128)(2,1)S(1)} %get-tuple-element.43), channel_id=1, source_target_pairs={{0,128},{8,136},{16,144},{24,152},{32,160},{40,168},{48,176},{56,1... | collective-permute-start | bytes 663560 | tf_op jit(solution)/shard_map/ppermute | solution.py:362
  80.8 12.9 %collective-permute-start.25 = (bf16[864,128]{1,0:T(8,128)(2,1)S(1)}, bf16[864,128]{1,0:T(8,128)(2,1)S(1)}, u32[]{:S(2)}, u32[]{:S(2)}) collective-permute-start(bf16[864,128]{1,0:T(8,128)(2,1)S(1)} %get-tuple-element.44), channel_id=1, source_target_pairs={{0,192},{8,200},{16,208},{24,216},{32,224},{40,232},{48,240},{56,2... | collective-permute-start | bytes 663560 | tf_op jit(solution)/shard_map/ppermute | solution.py:362
  95.8 6.3 %collective-permute-start.27 = (bf16[336,128]{1,0:T(8,128)(2,1)S(1)}, bf16[336,128]{1,0:T(8,128)(2,1)S(1)}, u32[]{:S(2)}, u32[]{:S(2)}) collective-permute-start(bf16[336,128]{1,0:T(8,128)(2,1)S(1)} %get-tuple-element.47), channel_id=1, source_target_pairs={{0,32},{8,40},{16,48},{24,56},{32,0},{40,8},{48,16},{56,24},{64,96... | collective-permute-start | bytes 258056 | tf_op jit(solution)/shard_map/ppermute | solution.py:362
  96.8 7.4 %collective-permute-start.28 = (bf16[336,128]{1,0:T(8,128)(2,1)S(1)}, bf16[336,128]{1,0:T(8,128)(2,1)S(1)}, u32[]{:S(2)}, u32[]{:S(2)}) collective-permute-start(bf16[336,128]{1,0:T(8,128)(2,1)S(1)} %get-tuple-element.48), channel_id=1, source_target_pairs={{0,48},{8,56},{16,32},{24,40},{32,16},{40,24},{48,0},{56,8},{64,11... | collective-permute-start | bytes 258056 | tf_op jit(solution)/shard_map/ppermute | solution.py:362
  125.2 6.5 %collective-permute-start.30 = (f32[160,128]{1,0:T(8,128)S(1)}, f32[160,128]{1,0:T(8,128)S(1)}, u32[]{:S(2)}, u32[]{:S(2)}) collective-permute-start(f32[160,128]{1,0:T(8,128)S(1)} %shard_map.106.own_ref), channel_id=1, source_target_pairs={{0,128},{8,136},{16,144},{24,152},{32,160},{40,168},{48,176},{56,1... | collective-permute-start | bytes 245768 | tf_op jit(solution)/shard_map/ppermute | solution.py:362
  (11 other events, 51.3 us)

commit v5 on v4

--- a/solution.py
+++ b/solution.py
@@ -245,27 +245,17 @@
     return (a.astype(F32) + b.astype(F32)) + (c.astype(F32) + d.astype(F32))
 
 
-def x_sum_body(
-    keep_ref, r1_ref, r2_ref, r3_ref, g0_ref, g1_ref, g2_ref, g3_ref,
-    s1_ref, s2_ref, s3_ref, out_ref, grad_ref,
-):
+def x_sum_body(keep_ref, r1_ref, r2_ref, r3_ref, s1_ref, s2_ref, s3_ref, out_ref):
     n = out_ref.shape[0]
     for d, ref in ((1, s1_ref), (2, s2_ref), (3, s3_ref), (0, out_ref)):
         at = slice(d * n, (d + 1) * n)
         total = four(keep_ref[at, :], r1_ref[at, :], r2_ref[at, :], r3_ref[at, :])
         ref[...] = total.astype(ref.dtype)
-    for d, ref in enumerate((g0_ref, g1_ref, g2_ref, g3_ref)):
-        grad_ref[4 * d : 4 * d + 4] = ref[...]
-
-
-def x_sum(keep, received, cotangents):
+
+
+def x_sum(keep, received):
     shape = (keep.shape[0] // 4, BS)
-    gathered = (16,) + cotangents[0].shape[1:]
-    return call(
-        x_sum_body,
-        [(shape, BF16)] * 3 + [(shape, F32), (gathered, BF16)],
-        (keep, *received, *cotangents),
-    )
+    return call(x_sum_body, [(shape, BF16)] * 3 + [(shape, F32)], (keep, *received))
 
 
 def core_sum_grad_body(mine_ref, far_ref, got_ref, s1_ref, s2_ref, s3_ref, keep_ref):
@@ -313,12 +303,21 @@
     )
 
 
-def aggregate_body(keep_ref, r1_ref, r2_ref, r3_ref, out_ref):
+def aggregate_body(
+    keep_ref, r1_ref, r2_ref, r3_ref, g0_ref, g1_ref, g2_ref, g3_ref, out_ref, grad_ref
+):
     out_ref[...] = four(keep_ref[...], r1_ref[...], r2_ref[...], r3_ref[...]).astype(BF16)
-
-
-def aggregate(keep, received):
-    return call(aggregate_body, [((BS, BS), BF16)], (keep, *received))[0]
+    for d, ref in enumerate((g0_ref, g1_ref, g2_ref, g3_ref)):
+        grad_ref[4 * d : 4 * d + 4] = ref[...]
+
+
+def aggregate(keep, received, cotangents):
+    gathered = (16,) + cotangents[0].shape[1:]
+    return call(
+        aggregate_body,
+        [((BS, BS), BF16), (gathered, BF16)],
+        (keep, *received, *cotangents),
+    )
 
 
 def share_sum_body(parts_ref, out_ref):
@@ -388,11 +387,12 @@
     s1, s2, s3, keep = core_sum(mine, got)
     received = [permute(s, f) for s, f in zip((s1, s2, s3), X_FLIPS)]
     grad_x = [grad_z] + [permute(grad_z, f) for f in X_FLIPS]
-    s1, s2, s3, keep, grad_near = x_sum(keep, received, grad_x)
+    s1, s2, s3, keep = x_sum(keep, received)
+    received = [permute(s, f) for s, f in zip((s1, s2, s3), Z_FLIPS)]
+    agg, grad_near = aggregate(keep, received, grad_x)
     grad_far = permute(grad_near, CORE)
-    received = [permute(s, f) for s, f in zip((s1, s2, s3), Z_FLIPS)]
+    agg = gather_col(agg)
     q = class_columns(grad_near, grad_far, dense)
-    agg = gather_col(aggregate(keep, received))
 
     wide, far = class_rows_far(agg, w_in, w_out_t, q, me, dense)
     got = permute(far, CORE)

time: 136 us -> 137 us (level)
  transfers between devices with their start and end apart: 32 -> 32, of which waited for: 19 -> 19; matrix products, arithmetic and copies ran while one was open for 1% -> 1% of each run, Pallas kernels for 8% -> 7%
where the time goes in v5:
time: 137 us; the launch traced here: 136 us
  starting transfers between devices  52.4 us (38%)
  waiting for transfers between devices  44.4 us (32%)
  blocking collectives  20.3 us (15%)
  Pallas kernels  16 us (12%)
  between operations  1.5 us (1%)
    ppermute x24, waiting for transfers between devices, permute(): return lax.ppermute(x, 'row', [(i, i ^ flip) for i in range(32)])  36.8 us
    ppermute x24, starting transfers between devices, permute(): return lax.ppermute(x, 'row', [(i, i ^ flip) for i in range(32)])  30.8 us
    all_to_all x1, blocking collectives, on_device(): own = share_sum(lax.all_to_all(shares, 'col', 0, 0))  20.3 us
    ppermute x2, starting transfers between devices, gather_col(): far = lax.ppermute(x, 'col', [(i, i ^ 4) for i in range(8)])  11.7 us
    pallas_call x13, Pallas kernels, call(): pl.pallas_call(body, out_shape=[o if len(o) == 1 else jax.ShapeDtypeStruc...  10.5 us
    ppermute x6, starting transfers between devices, gather_col(): lax.ppermute(pair, 'col', [(i, i ^ d) for i in range(8)])  9.94 us
    pallas_call x1, Pallas kernels, densify(): pl.pallas_call(densify_body, out_shape=pltpu.VMEM((4096, 1024), BF16), in...  5.54 us
    ppermute x2, waiting for transfers between devices, gather_col(): far = lax.ppermute(x, 'col', [(i, i ^ 4) for i in range(8)])  4.03 us
  transfers between devices with their start and end apart: 32, of which 19 were waited for; matrix products, arithmetic and copies ran while one was open for 1% of the time, Pallas kernels for 7%

profile of v5, /device:TPU:32, one launch (start us, length us, event | category | flops | bytes accessed | tf_op | source)
XLA Modules:
  0.0 135.9 jit_solution(9709048915367378398)
XLA Ops:
  0.6 6.4 %collective-permute-start = (bf16[128,128]{1,0:T(8,128)(2,1)}, bf16[128,128]{1,0:T(8,128)(2,1)S(1)}, u32[]{:S(2)}, u32[]{:S(2)}) collective-permute-start(bf16[128,128]{1,0:T(8,128)(2,1)} %param.7), channel_id=1, source_target_pairs={{0,4},{1,5},{2,6},{3,7},{4,0},{5,1},{6,2},{7,3},{8,12},{9,13},{10,... | collective-permute-start | bytes 98312 | tf_op jit(solution)/shard_map/ppermute | solution.py:365
  11.8 2.9 %collective-permute-start.2 = (bf16[2,128,128]{2,1,0:T(8,128)(2,1)S(1)}, bf16[2,128,128]{2,1,0:T(8,128)(2,1)S(1)}, u32[]{:S(2)}, u32[]{:S(2)}) collective-permute-start(bf16[2,128,128]{2,1,0:T(8,128)(2,1)S(1)} %pad_maximum_fusion.r0_ref), channel_id=1, source_target_pairs={{0,2},{1,3},{2,0},{3,1},{4,6},{5,7},{6,4},{7,5},{8,10},{9,11},{10,... | collective-permute-start | bytes 196616 | tf_op jit(solution)/shard_map/ppermute | solution.py:367
  14.9 2.6 %collective-permute-start.5 = (bf16[172,128]{1,0:T(8,128)(2,1)}, bf16[172,128]{1,0:T(8,128)(2,1)S(1)}, u32[]{:S(2)}, u32[]{:S(2)}) collective-permute-start(bf16[172,128]{1,0:T(8,128)(2,1)} %bitcast.12), channel_id=1, source_target_pairs={{0,32},{8,40},{16,48},{24,56},{32,0},{40,8},{48,16},{56,24},{64,96... | collective-permute-start | bytes 132104 | tf_op jit(solution)/shard_map/ppermute | solution.py:361
  18.3 5.5 %shard_map.94.dense_ref = bf16[4096,1024]{1,0:T(8,128)(2,1)S(1)} custom-call(s32[1]{0:T(128)} %bitcast.me_ref, s32[1]{0:T(128)} %bitcast.1.side_ref, s32[1]{0:T(128)S(6)} %copy.12.count_ref, s32[144]{0:T(256)} %slot_ref.1, bf16[144,128,128]{2,1,0:T(8,128)(2,1)} %block_ref.1), custom_call_target="tpu_custom_call" | custom-call | tf_op jit(solution)/shard_map/pallas_call | solution.py:86
  28.0 3.4 %collective-permute-start.10 = (bf16[512,128]{1,0:T(8,128)(2,1)S(1)}, bf16[512,128]{1,0:T(8,128)(2,1)S(1)}, u32[]{:S(2)}, u32[]{:S(2)}) collective-permute-start(bf16[512,128]{1,0:T(8,128)(2,1)S(1)} %get-tuple-element.33), channel_id=1, source_target_pairs={{0,192},{8,200},{16,208},{24,216},{32,224},{40,232},{48,240},{56,2... | collective-permute-start | bytes 393224 | tf_op jit(solution)/shard_map/ppermute | solution.py:361
  33.0 3.1 %collective-permute-start.16 = (bf16[4,172,128]{2,1,0:T(8,128)(2,1)S(1)}, bf16[4,172,128]{2,1,0:T(8,128)(2,1)S(1)}, u32[]{:S(2)}, u32[]{:S(2)}) collective-permute-start(bf16[4,172,128]{2,1,0:T(8,128)(2,1)S(1)} %get-tuple-element.38.g0_ref), channel_id=1, source_target_pairs={{0,192},{8,200},{16,208},{24,216},{32,224},{40,232},{48,240},{56,2... | collective-permute-start | bytes 528392 | tf_op jit(solution)/shard_map/ppermute | solution.py:361
  37.7 7.9 %collective-permute-done.8.r1_ref = bf16[512,128]{1,0:T(8,128)(2,1)S(1)} collective-permute-done((bf16[512,128]{1,0:T(8,128)(2,1)S(1)}, bf16[512,128]{1,0:T(8,128)(2,1)S(1)}, u32[]{:S(2)}, u32[]{:S(2)}) %collective-permute-start.8) | collective-permute-done | bytes 131104 | tf_op jit(solution)/shard_map/ppermute | solution.py:361
  51.1 2.2 %collective-permute-done.12.r2_ref = bf16[128,128]{1,0:T(8,128)(2,1)S(1)} collective-permute-done((bf16[128,128]{1,0:T(8,128)(2,1)S(1)}, bf16[128,128]{1,0:T(8,128)(2,1)S(1)}, u32[]{:S(2)}, u32[]{:S(2)}) %collective-permute-start.12) | collective-permute-done | bytes 32800 | tf_op jit(solution)/shard_map/ppermute | solution.py:361
  54.4 5.3 %collective-permute-start.17 = (bf16[128,128]{1,0:T(8,128)(2,1)S(1)}, bf16[128,128]{1,0:T(8,128)(2,1)S(1)}, u32[]{:S(2)}, u32[]{:S(2)}) collective-permute-start(bf16[128,128]{1,0:T(8,128)(2,1)S(1)} %get-tuple-element.39), channel_id=1, source_target_pairs={{0,4},{1,5},{2,6},{3,7},{4,0},{5,1},{6,2},{7,3},{8,12},{9,13},{10,... | collective-permute-start | bytes 98312 | tf_op jit(solution)/shard_map/ppermute | solution.py:365
  59.7 2.6 %collective-permute-done.17 = bf16[128,128]{1,0:T(8,128)(2,1)S(1)} collective-permute-done((bf16[128,128]{1,0:T(8,128)(2,1)S(1)}, bf16[128,128]{1,0:T(8,128)(2,1)S(1)}, u32[]{:S(2)}, u32[]{:S(2)}) %collective-permute-start.17) | collective-permute-done | bytes 32800 | tf_op jit(solution)/shard_map/ppermute | solution.py:365
  63.1 4.5 %collective-permute-start.19 = (bf16[2,128,128]{2,1,0:T(8,128)(2,1)S(1)}, bf16[2,128,128]{2,1,0:T(8,128)(2,1)S(1)}, u32[]{:S(2)}, u32[]{:S(2)}) collective-permute-start(bf16[2,128,128]{2,1,0:T(8,128)(2,1)S(1)} %pad_maximum_fusion.1.a0_ref), channel_id=1, source_target_pairs={{0,2},{1,3},{2,0},{3,1},{4,6},{5,7},{6,4},{7,5},{8,10},{9,11},{10,... | collective-permute-start | bytes 196616 | tf_op jit(solution)/shard_map/ppermute | solution.py:367
  67.8 1.7 %shard_map.100.q_ref = f32[172,1024]{1,0:T(8,128)S(1)} custom-call(bf16[16,172,128]{2,1,0:T(8,128)(2,1)S(1)} %get-tuple-element.40.near_ref, bf16[16,172,128]{2,1,0:T(8,128)(2,1)S(1)} %copy.11.far_ref, bf16[4096,1024]{1,0:T(8,128)(2,1)S(1)} %shard_map.94.dense_ref), custom_call_target="tpu_custom_call" | custom-call | flops 2147483648 | bytes 1048576 | tf_op jit(solution)/shard_map/pallas_call | solution.py:34
  70.6 2.5 %collective-permute-done.20.a3_ref = bf16[2,128,128]{2,1,0:T(8,128)(2,1)S(1)} collective-permute-done((bf16[2,128,128]{2,1,0:T(8,128)(2,1)S(1)}, bf16[2,128,128]{2,1,0:T(8,128)(2,1)S(1)}, u32[]{:S(2)}, u32[]{:S(2)}) %collective-permute-start.20) | collective-permute-done | bytes 65568 | tf_op jit(solution)/shard_map/ppermute | solution.py:367
  73.1 2.9 %shard_map.101 = (bf16[176,1024]{1,0:T(8,128)(2,1)S(1)}, bf16[3456,128]{1,0:T(8,128)(2,1)S(1)}) custom-call(bf16[2,128,128]{2,1,0:T(8,128)(2,1)S(1)} %pad_maximum_fusion.1.a0_ref, bf16[2,128,128]{2,1,0:T(8,128)(2,1)S(1)} %collective-permute-done.18.a1_ref, bf16[2,128,128]{2,1,0:T(8,128)(2,1)S(1)} %collective-permute-done.19.a2_ref, ...), custom_call_target="tpu_custom_call" | custom-call | flops 2147483648 | bytes 1048576 | tf_op jit(solution)/shard_map/pallas_call | solution.py:34
  78.7 4.1 %collective-permute-start.24 = (bf16[864,128]{1,0:T(8,128)(2,1)S(1)}, bf16[864,128]{1,0:T(8,128)(2,1)S(1)}, u32[]{:S(2)}, u32[]{:S(2)}) collective-permute-start(bf16[864,128]{1,0:T(8,128)(2,1)S(1)} %get-tuple-element.45), channel_id=1, source_target_pairs={{0,128},{8,136},{16,144},{24,152},{32,160},{40,168},{48,176},{56,1... | collective-permute-start | bytes 663560 | tf_op jit(solution)/shard_map/ppermute | solution.py:361
  83.4 3.6 %collective-permute-done.23.r1_ref = bf16[864,128]{1,0:T(8,128)(2,1)S(1)} collective-permute-done((bf16[864,128]{1,0:T(8,128)(2,1)S(1)}, bf16[864,128]{1,0:T(8,128)(2,1)S(1)}, u32[]{:S(2)}, u32[]{:S(2)}) %collective-permute-start.23) | collective-permute-done | bytes 221216 | tf_op jit(solution)/shard_map/ppermute | solution.py:361
  87.0 6.1 %collective-permute-done.24.r2_ref = bf16[864,128]{1,0:T(8,128)(2,1)S(1)} collective-permute-done((bf16[864,128]{1,0:T(8,128)(2,1)S(1)}, bf16[864,128]{1,0:T(8,128)(2,1)S(1)}, u32[]{:S(2)}, u32[]{:S(2)}) %collective-permute-start.24) | collective-permute-done | bytes 221216 | tf_op jit(solution)/shard_map/ppermute | solution.py:361
  93.1 2.6 %collective-permute-done.25.r3_ref = bf16[864,128]{1,0:T(8,128)(2,1)S(1)} collective-permute-done((bf16[864,128]{1,0:T(8,128)(2,1)S(1)}, bf16[864,128]{1,0:T(8,128)(2,1)S(1)}, u32[]{:S(2)}, u32[]{:S(2)}) %collective-permute-start.25) | collective-permute-done | bytes 221216 | tf_op jit(solution)/shard_map/ppermute | solution.py:361
  95.8 2.5 %collective-permute-start.26 = (bf16[336,128]{1,0:T(8,128)(2,1)S(1)}, bf16[336,128]{1,0:T(8,128)(2,1)S(1)}, u32[]{:S(2)}, u32[]{:S(2)}) collective-permute-start(bf16[336,128]{1,0:T(8,128)(2,1)S(1)} %get-tuple-element.48), channel_id=1, source_target_pairs={{0,16},{8,24},{16,0},{24,8},{32,48},{40,56},{48,32},{56,40},{64,80... | collective-permute-start | bytes 258056 | tf_op jit(solution)/shard_map/ppermute | solution.py:361
  101.4 2.5 %collective-permute-done.27.r2_ref = bf16[336,128]{1,0:T(8,128)(2,1)S(1)} collective-permute-done((bf16[336,128]{1,0:T(8,128)(2,1)S(1)}, bf16[336,128]{1,0:T(8,128)(2,1)S(1)}, u32[]{:S(2)}, u32[]{:S(2)}) %collective-permute-start.27) | collective-permute-done | bytes 86048 | tf_op jit(solution)/shard_map/ppermute | solution.py:361
  103.9 2.6 %collective-permute-done.28.r3_ref = bf16[336,128]{1,0:T(8,128)(2,1)S(1)} collective-permute-done((bf16[336,128]{1,0:T(8,128)(2,1)S(1)}, bf16[336,128]{1,0:T(8,128)(2,1)S(1)}, u32[]{:S(2)}, u32[]{:S(2)}) %collective-permute-start.28) | collective-permute-done | bytes 86048 | tf_op jit(solution)/shard_map/ppermute | solution.py:361
  107.2 20.3 %all_to_all.5.parts_ref = bf16[8,160,128]{2,1,0:T(8,128)(2,1)S(1)} all-to-all(bf16[8,160,128]{2,1,0:T(8,128)(2,1)S(1)} %get-tuple-element.52), channel_id=1, replica_groups=mesh['row'=32,'col'=8] {'col'}, dimensions={0} | all-to-all | bytes 655360 | tf_op jit(solution)/shard_map/all_to_all | solution.py:404
  127.7 1.8 %collective-permute-start.30 = (f32[160,128]{1,0:T(8,128)S(1)}, f32[160,128]{1,0:T(8,128)S(1)}, u32[]{:S(2)}, u32[]{:S(2)}) collective-permute-start(f32[160,128]{1,0:T(8,128)S(1)} %shard_map.106.own_ref), channel_id=1, source_target_pairs={{0,128},{8,136},{16,144},{24,152},{32,160},{40,168},{48,176},{56,1... | collective-permute-start | bytes 245768 | tf_op jit(solution)/shard_map/ppermute | solution.py:361
  129.5 2.9 %collective-permute-start.31 = (f32[160,128]{1,0:T(8,128)S(1)}, f32[160,128]{1,0:T(8,128)S(1)}, u32[]{:S(2)}, u32[]{:S(2)}) collective-permute-start(f32[160,128]{1,0:T(8,128)S(1)} %shard_map.106.own_ref), channel_id=1, source_target_pairs={{0,192},{8,200},{16,208},{24,216},{32,224},{40,232},{48,240},{56,2... | collective-permute-start | bytes 245768 | tf_op jit(solution)/shard_map/ppermute | solution.py:361
  (65 shorter events, 32.0 us)
Async XLA Ops:
  0.6 8.8 %collective-permute-start = (bf16[128,128]{1,0:T(8,128)(2,1)}, bf16[128,128]{1,0:T(8,128)(2,1)S(1)}, u32[]{:S(2)}, u32[]{:S(2)}) collective-permute-start(bf16[128,128]{1,0:T(8,128)(2,1)} %param.7), channel_id=1, source_target_pairs={{0,4},{1,5},{2,6},{3,7},{4,0},{5,1},{6,2},{7,3},{8,12},{9,13},{10,... | collective-permute-start | bytes 98312 | tf_op jit(solution)/shard_map/ppermute | solution.py:365
  7.0 10.5 %collective-permute-start.4 = (bf16[172,128]{1,0:T(8,128)(2,1)}, bf16[172,128]{1,0:T(8,128)(2,1)S(1)}, u32[]{:S(2)}, u32[]{:S(2)}) collective-permute-start(bf16[172,128]{1,0:T(8,128)(2,1)} %bitcast.11), channel_id=1, source_target_pairs={{0,16},{8,24},{16,0},{24,8},{32,48},{40,56},{48,32},{56,40},{64,80... | collective-permute-start | bytes 132104 | tf_op jit(solution)/shard_map/ppermute | solution.py:361
  10.2 13.6 %collective-permute-start.1 = (bf16[2,128,128]{2,1,0:T(8,128)(2,1)S(1)}, bf16[2,128,128]{2,1,0:T(8,128)(2,1)S(1)}, u32[]{:S(2)}, u32[]{:S(2)}) collective-permute-start(bf16[2,128,128]{2,1,0:T(8,128)(2,1)S(1)} %pad_maximum_fusion.r0_ref), channel_id=1, source_target_pairs={{0,1},{1,0},{2,3},{3,2},{4,5},{5,4},{6,7},{7,6},{8,9},{9,8},{10,11... | collective-permute-start | bytes 196616 | tf_op jit(solution)/shard_map/ppermute | solution.py:367
  11.8 12.1 %collective-permute-start.2 = (bf16[2,128,128]{2,1,0:T(8,128)(2,1)S(1)}, bf16[2,128,128]{2,1,0:T(8,128)(2,1)S(1)}, u32[]{:S(2)}, u32[]{:S(2)}) collective-permute-start(bf16[2,128,128]{2,1,0:T(8,128)(2,1)S(1)} %pad_maximum_fusion.r0_ref), channel_id=1, source_target_pairs={{0,2},{1,3},{2,0},{3,1},{4,6},{5,7},{6,4},{7,5},{8,10},{9,11},{10,... | collective-permute-start | bytes 196616 | tf_op jit(solution)/shard_map/ppermute | solution.py:367
  14.7 9.2 %collective-permute-start.3 = (bf16[2,128,128]{2,1,0:T(8,128)(2,1)S(1)}, bf16[2,128,128]{2,1,0:T(8,128)(2,1)S(1)}, u32[]{:S(2)}, u32[]{:S(2)}) collective-permute-start(bf16[2,128,128]{2,1,0:T(8,128)(2,1)S(1)} %pad_maximum_fusion.r0_ref), channel_id=1, source_target_pairs={{0,3},{1,2},{2,1},{3,0},{4,7},{5,6},{6,5},{7,4},{8,11},{9,10},{10,... | collective-permute-start | bytes 196616 | tf_op jit(solution)/shard_map/ppermute | solution.py:367
  14.9 8.9 %collective-permute-start.5 = (bf16[172,128]{1,0:T(8,128)(2,1)}, bf16[172,128]{1,0:T(8,128)(2,1)S(1)}, u32[]{:S(2)}, u32[]{:S(2)}) collective-permute-start(bf16[172,128]{1,0:T(8,128)(2,1)} %bitcast.12), channel_id=1, source_target_pairs={{0,32},{8,40},{16,48},{24,56},{32,0},{40,8},{48,16},{56,24},{64,96... | collective-permute-start | bytes 132104 | tf_op jit(solution)/shard_map/ppermute | solution.py:361
  17.5 6.4 %collective-permute-start.6 = (bf16[172,128]{1,0:T(8,128)(2,1)}, bf16[172,128]{1,0:T(8,128)(2,1)S(1)}, u32[]{:S(2)}, u32[]{:S(2)}) collective-permute-start(bf16[172,128]{1,0:T(8,128)(2,1)} %bitcast.13), channel_id=1, source_target_pairs={{0,48},{8,56},{16,32},{24,40},{32,16},{40,24},{48,0},{56,8},{64,11... | collective-permute-start | bytes 132104 | tf_op jit(solution)/shard_map/ppermute | solution.py:361
  28.0 8.1 %collective-permute-start.10 = (bf16[512,128]{1,0:T(8,128)(2,1)S(1)}, bf16[512,128]{1,0:T(8,128)(2,1)S(1)}, u32[]{:S(2)}, u32[]{:S(2)}) collective-permute-start(bf16[512,128]{1,0:T(8,128)(2,1)S(1)} %get-tuple-element.33), channel_id=1, source_target_pairs={{0,192},{8,200},{16,208},{24,216},{32,224},{40,232},{48,240},{56,2... | collective-permute-start | bytes 393224 | tf_op jit(solution)/shard_map/ppermute | solution.py:361
  31.4 18.4 %collective-permute-start.14 = (bf16[4,172,128]{2,1,0:T(8,128)(2,1)S(1)}, bf16[4,172,128]{2,1,0:T(8,128)(2,1)S(1)}, u32[]{:S(2)}, u32[]{:S(2)}) collective-permute-start(bf16[4,172,128]{2,1,0:T(8,128)(2,1)S(1)} %get-tuple-element.38.g0_ref), channel_id=1, source_target_pairs={{0,64},{8,72},{16,80},{24,88},{32,96},{40,104},{48,112},{56,120},{... | collective-permute-start | bytes 528392 | tf_op jit(solution)/shard_map/ppermute | solution.py:361
  31.4 19.3 %collective-permute-start.15 = (bf16[4,172,128]{2,1,0:T(8,128)(2,1)S(1)}, bf16[4,172,128]{2,1,0:T(8,128)(2,1)S(1)}, u32[]{:S(2)}, u32[]{:S(2)}) collective-permute-start(bf16[4,172,128]{2,1,0:T(8,128)(2,1)S(1)} %get-tuple-element.38.g0_ref), channel_id=1, source_target_pairs={{0,128},{8,136},{16,144},{24,152},{32,160},{40,168},{48,176},{56,1... | collective-permute-start | bytes 528392 | tf_op jit(solution)/shard_map/ppermute | solution.py:361
  33.0 17.7 %collective-permute-start.16 = (bf16[4,172,128]{2,1,0:T(8,128)(2,1)S(1)}, bf16[4,172,128]{2,1,0:T(8,128)(2,1)S(1)}, u32[]{:S(2)}, u32[]{:S(2)}) collective-permute-start(bf16[4,172,128]{2,1,0:T(8,128)(2,1)S(1)} %get-tuple-element.38.g0_ref), channel_id=1, source_target_pairs={{0,192},{8,200},{16,208},{24,216},{32,224},{40,232},{48,240},{56,2... | collective-permute-start | bytes 528392 | tf_op jit(solution)/shard_map/ppermute | solution.py:361
  36.1 9.5 %collective-permute-start.8 = (bf16[512,128]{1,0:T(8,128)(2,1)S(1)}, bf16[512,128]{1,0:T(8,128)(2,1)S(1)}, u32[]{:S(2)}, u32[]{:S(2)}) collective-permute-start(bf16[512,128]{1,0:T(8,128)(2,1)S(1)} %get-tuple-element.31), channel_id=1, source_target_pairs={{0,64},{8,72},{16,80},{24,88},{32,96},{40,104},{48,112},{56,120},{... | collective-permute-start | bytes 393224 | tf_op jit(solution)/shard_map/ppermute | solution.py:361
  36.1 10.9 %collective-permute-start.9 = (bf16[512,128]{1,0:T(8,128)(2,1)S(1)}, bf16[512,128]{1,0:T(8,128)(2,1)S(1)}, u32[]{:S(2)}, u32[]{:S(2)}) collective-permute-start(bf16[512,128]{1,0:T(8,128)(2,1)S(1)} %get-tuple-element.32), channel_id=1, source_target_pairs={{0,128},{8,136},{16,144},{24,152},{32,160},{40,168},{48,176},{56,1... | collective-permute-start | bytes 393224 | tf_op jit(solution)/shard_map/ppermute | solution.py:361
  54.3 13.3 %collective-permute-start.21 = (bf16[16,172,128]{2,0,1:T(8,128)(2,1)S(1)}, bf16[16,172,128]{2,0,1:T(8,128)(2,1)S(1)}, u32[]{:S(2)}, u32[]{:S(2)}) collective-permute-start(bf16[16,172,128]{2,0,1:T(8,128)(2,1)S(1)} %copy.10), channel_id=1, source_target_pairs={{0,8},{8,0},{16,24},{24,16},{32,40},{40,32},{48,56},{56,48},{64,72... | collective-permute-start | bytes 2113544 | tf_op jit(solution)/shard_map/ppermute | solution.py:361
  54.4 7.9 %collective-permute-start.17 = (bf16[128,128]{1,0:T(8,128)(2,1)S(1)}, bf16[128,128]{1,0:T(8,128)(2,1)S(1)}, u32[]{:S(2)}, u32[]{:S(2)}) collective-permute-start(bf16[128,128]{1,0:T(8,128)(2,1)S(1)} %get-tuple-element.39), channel_id=1, source_target_pairs={{0,4},{1,5},{2,6},{3,7},{4,0},{5,1},{6,2},{7,3},{8,12},{9,13},{10,... | collective-permute-start | bytes 98312 | tf_op jit(solution)/shard_map/ppermute | solution.py:365
  62.3 7.1 %collective-permute-start.18 = (bf16[2,128,128]{2,1,0:T(8,128)(2,1)S(1)}, bf16[2,128,128]{2,1,0:T(8,128)(2,1)S(1)}, u32[]{:S(2)}, u32[]{:S(2)}) collective-permute-start(bf16[2,128,128]{2,1,0:T(8,128)(2,1)S(1)} %pad_maximum_fusion.1.a0_ref), channel_id=1, source_target_pairs={{0,1},{1,0},{2,3},{3,2},{4,5},{5,4},{6,7},{7,6},{8,9},{9,8},{10,11... | collective-permute-start | bytes 196616 | tf_op jit(solution)/shard_map/ppermute | solution.py:367
  63.1 7.5 %collective-permute-start.19 = (bf16[2,128,128]{2,1,0:T(8,128)(2,1)S(1)}, bf16[2,128,128]{2,1,0:T(8,128)(2,1)S(1)}, u32[]{:S(2)}, u32[]{:S(2)}) collective-permute-start(bf16[2,128,128]{2,1,0:T(8,128)(2,1)S(1)} %pad_maximum_fusion.1.a0_ref), channel_id=1, source_target_pairs={{0,2},{1,3},{2,0},{3,1},{4,6},{5,7},{6,4},{7,5},{8,10},{9,11},{10,... | collective-permute-start | bytes 196616 | tf_op jit(solution)/shard_map/ppermute | solution.py:367
  78.6 8.4 %collective-permute-start.23 = (bf16[864,128]{1,0:T(8,128)(2,1)S(1)}, bf16[864,128]{1,0:T(8,128)(2,1)S(1)}, u32[]{:S(2)}, u32[]{:S(2)}) collective-permute-start(bf16[864,128]{1,0:T(8,128)(2,1)S(1)} %get-tuple-element.44), channel_id=1, source_target_pairs={{0,64},{8,72},{16,80},{24,88},{32,96},{40,104},{48,112},{56,120},{... | collective-permute-start | bytes 663560 | tf_op jit(solution)/shard_map/ppermute | solution.py:361
  78.7 14.4 %collective-permute-start.24 = (bf16[864,128]{1,0:T(8,128)(2,1)S(1)}, bf16[864,128]{1,0:T(8,128)(2,1)S(1)}, u32[]{:S(2)}, u32[]{:S(2)}) collective-permute-start(bf16[864,128]{1,0:T(8,128)(2,1)S(1)} %get-tuple-element.45), channel_id=1, source_target_pairs={{0,128},{8,136},{16,144},{24,152},{32,160},{40,168},{48,176},{56,1... | collective-permute-start | bytes 663560 | tf_op jit(solution)/shard_map/ppermute | solution.py:361
  82.8 12.9 %collective-permute-start.25 = (bf16[864,128]{1,0:T(8,128)(2,1)S(1)}, bf16[864,128]{1,0:T(8,128)(2,1)S(1)}, u32[]{:S(2)}, u32[]{:S(2)}) collective-permute-start(bf16[864,128]{1,0:T(8,128)(2,1)S(1)} %get-tuple-element.46), channel_id=1, source_target_pairs={{0,192},{8,200},{16,208},{24,216},{32,224},{40,232},{48,240},{56,2... | collective-permute-start | bytes 663560 | tf_op jit(solution)/shard_map/ppermute | solution.py:361
  95.8 5.7 %collective-permute-start.26 = (bf16[336,128]{1,0:T(8,128)(2,1)S(1)}, bf16[336,128]{1,0:T(8,128)(2,1)S(1)}, u32[]{:S(2)}, u32[]{:S(2)}) collective-permute-start(bf16[336,128]{1,0:T(8,128)(2,1)S(1)} %get-tuple-element.48), channel_id=1, source_target_pairs={{0,16},{8,24},{16,0},{24,8},{32,48},{40,56},{48,32},{56,40},{64,80... | collective-permute-start | bytes 258056 | tf_op jit(solution)/shard_map/ppermute | solution.py:361
  98.3 5.7 %collective-permute-start.27 = (bf16[336,128]{1,0:T(8,128)(2,1)S(1)}, bf16[336,128]{1,0:T(8,128)(2,1)S(1)}, u32[]{:S(2)}, u32[]{:S(2)}) collective-permute-start(bf16[336,128]{1,0:T(8,128)(2,1)S(1)} %get-tuple-element.49), channel_id=1, source_target_pairs={{0,32},{8,40},{16,48},{24,56},{32,0},{40,8},{48,16},{56,24},{64,96... | collective-permute-start | bytes 258056 | tf_op jit(solution)/shard_map/ppermute | solution.py:361
  99.0 7.5 %collective-permute-start.28 = (bf16[336,128]{1,0:T(8,128)(2,1)S(1)}, bf16[336,128]{1,0:T(8,128)(2,1)S(1)}, u32[]{:S(2)}, u32[]{:S(2)}) collective-permute-start(bf16[336,128]{1,0:T(8,128)(2,1)S(1)} %get-tuple-element.50), channel_id=1, source_target_pairs={{0,48},{8,56},{16,32},{24,40},{32,16},{40,24},{48,0},{56,8},{64,11... | collective-permute-start | bytes 258056 | tf_op jit(solution)/shard_map/ppermute | solution.py:361
  127.7 6.0 %collective-permute-start.30 = (f32[160,128]{1,0:T(8,128)S(1)}, f32[160,128]{1,0:T(8,128)S(1)}, u32[]{:S(2)}, u32[]{:S(2)}) collective-permute-start(f32[160,128]{1,0:T(8,128)S(1)} %shard_map.106.own_ref), channel_id=1, source_target_pairs={{0,128},{8,136},{16,144},{24,152},{32,160},{40,168},{48,176},{56,1... | collective-permute-start | bytes 245768 | tf_op jit(solution)/shard_map/ppermute | solution.py:361
  (11 other events, 50.4 us)
